TPU v7x, 32 devices: a whole 2x2x4 slice. The times are simulated.
32 devices in a mesh: groups: 2 (over y), sector: 4 (over z), contr: 2 (over x), mpo: 2 (over core).
Axes of the slice: x: 2, y: 2, z: 4, core: 2. Of those that a mesh axis runs over, the one named last changes fastest.
Arguments:
- psi: bfloat16 [8, 4, 256, 256], P(('groups', 'sector'), None, 'contr'), parts along dimension 0, may hold values from -6 to 6
- sector_size: int32 [8, 4], P(('groups', 'sector')), parts along dimension 0, may hold values from 64 to 256, as said below
- left_env: bfloat16 [26, 8, 4, 256, 256], P('mpo', ('groups', 'sector'), None, 'contr'), parts along dimension 1
- right_env: bfloat16 [26, 8, 4, 256, 256], P('mpo', ('groups', 'sector'), None, None, 'contr'), parts along dimension 1
- term_shift: int32 [52], P(('groups', 'mpo')), parts along dimension 0, may hold values from 0 to 4
Outputs:
- first_image: bfloat16 [8, 4, 256, 256], P(('groups', 'sector'), None, 'contr'), parts along dimension 0
- second_image: bfloat16 [8, 4, 256, 256], P(('groups', 'sector'), None, 'contr'), parts along dimension 0
- ritz_value: float32 [2], P('groups'), parts along dimension 0
There are 2 independent parts, one for each index of `groups`. A program takes and returns all parts, laid end to end along the dimension named above; each array names one. Nothing has to cross between parts.
Inputs may be any that keep to these rules, and one draw needn't show every extreme that they name: `sector_size`: some sector has live size 256 and some has 64.
All inputs are finite; a program needn't handle non-finite values.
Results may differ from a plain program's by a relative error of at most 0.0024.
The roundings to bfloat16 on the way count: a program that leaves them out, or rounds other values in their place, can miss the bound.
Values may be sent and summed in bfloat16 or wider, within the bound.
No kernel may reach another device: no remote copies, remote signals or barrier semaphores. Data moves between devices by JAX's collectives and lax.ppermute only.
A program may use at most 64 MiB of HBM per device.

v0:
```python
import jax
import jax.numpy as jnp
from jax import lax
from jax.sharding import PartitionSpec as P


def padded(cells, sides, width):
    for axis, dim in sides:
        count = lax.axis_size(axis)
        ends = count - 1
        head = lax.slice_in_dim(cells, 0, width, axis=dim)
        tail = lax.slice_in_dim(cells, cells.shape[dim] - width, cells.shape[dim], axis=dim)
        cells = jnp.concatenate(
            [
                lax.ppermute(tail, axis, [(i, (i + 1) % count) for i in range(ends)]),
                cells,
                lax.ppermute(head, axis, [((i + 1) % count, i) for i in range(ends)]),
            ],
            axis=dim,
        )
    return cells


def on_device(psi, sector_size, left_env, right_env, term_shift):
    slots = psi.shape[1]
    rows_here = psi.shape[2]
    width = psi.shape[3]
    row_ids = lax.axis_index("contr") * rows_here + lax.iota(jnp.int32, rows_here)
    col_ids = lax.iota(jnp.int32, width)
    live = sector_size[0][:, None, None]
    mask = ((row_ids[None, :, None] < live) & (col_ids[None, None, :] < live)).astype(jnp.float32)[
        None
    ]

    def apply_h(field):
        extended = padded(field, (("sector", 0),), 1)
        own = field[0]
        blank = jnp.zeros_like(own[:1])
        stacked = jnp.stack(
            [
                own,
                extended[0],
                extended[2],
                jnp.concatenate([blank, own[:-1]], 0),
                jnp.concatenate([own[1:], blank], 0),
            ]
        )
        sources = stacked[term_shift]
        inner = jnp.einsum(
            "wvrl,wvml->wvrm",
            sources,
            lax.all_gather(left_env, "contr", axis=3, tiled=True)[:, 0],
            preferred_element_type=jnp.float32,
        ).astype(jnp.bfloat16)
        partial_sum = jnp.einsum(
            "wvpr,wvrm->vpm", right_env[:, 0], inner, preferred_element_type=jnp.float32
        )
        summed = lax.psum_scatter(partial_sum, "contr", scatter_dimension=1, tiled=True)
        summed = lax.psum(summed, "mpo")
        return summed[None] * mask

    first = psi * mask.astype(jnp.bfloat16)
    image_one = apply_h(first)
    trial = first.astype(jnp.float32)
    entries = float(lax.axis_size("sector") * slots * width * width)
    product, squares = lax.psum(
        (jnp.sum(trial * image_one), jnp.sum(trial * trial)), ("sector", "contr")
    )
    ritz_value = product / (squares + 1e-06)
    resid = image_one - ritz_value * trial
    total_sq = lax.psum(jnp.sum(resid * resid), ("sector", "contr"))
    factor = lax.rsqrt(total_sq / entries + 1e-06)
    second = (resid * factor).astype(jnp.bfloat16)
    image_two = apply_h(second)
    return (
        image_one.astype(jnp.bfloat16),
        image_two.astype(jnp.bfloat16),
        jnp.reshape(ritz_value, (1,)),
    )


def solution(mesh):
    return jax.shard_map(
        on_device,
        mesh=mesh,
        in_specs=(
            P(("groups", "sector"), None, "contr", None),
            P(("groups", "sector"), None),
            P("mpo", ("groups", "sector"), None, "contr", None),
            P("mpo", ("groups", "sector"), None, None, "contr"),
            P(("groups", "mpo")),
        ),
        out_specs=(
            P(("groups", "sector"), None, "contr", None),
            P(("groups", "sector"), None, "contr", None),
            P("groups"),
        ),
        check_vma=False,
    )
```

profile of v0, /device:TPU:0, one launch (start us, length us, event | category | flops | bytes accessed | tf_op | source)
XLA Modules:
  0.0 259.4 jit_solution(3173446964363676751)
XLA Ops:
  8.0 2.0 copy.8
  10.1 1.9 constant_dynamic-update-slice_fusion.2
  12.0 1.3 collective-permute-start.1
  13.2 5.6 %collective-permute-start = (bf16[1,4,128,256]{2,3,1,0:T(8,128)(2,1)S(1)}, bf16[1,4,128,256]{2,3,1,0:T(8,128)(2,1)S(1)}, u32[]{:S(2)}, u32[]{:S(2)}) collective-permute-start(bf16[1,4,128,256]{2,3,1,0:T(8,128)(2,1)S(1)} %get-tuple-element.13), channel_id=1, source_target_pairs={{0,4},{4,8},{8,12},{1,5},{5,9},{9,13},{2,6},{6,10},{10,14},{3,7},{... | collective-permute-start | bytes 786440 | tf_op jit(solution)/shard_map/ppermute | solution.py:15
  18.9 5.4 %collective-permute-done = bf16[1,4,128,256]{2,3,1,0:T(8,128)(2,1)S(1)} collective-permute-done((bf16[1,4,128,256]{2,3,1,0:T(8,128)(2,1)S(1)}, bf16[1,4,128,256]{2,3,1,0:T(8,128)(2,1)S(1)}, u32[]{:S(2)}, u32[]{:S(2)}) %collective-permute-start) | collective-permute-done | bytes 262176 | tf_op jit(solution)/shard_map/ppermute | solution.py:15
  24.4 0.8 constant_dynamic-update-slice_fusion.1
  25.1 0.8 constant_dynamic-update-slice_fusion
  25.9 0.7 bitcast_dynamic-update-slice_fusion.3
  27.3 4.3 %gather_fusion = bf16[13,4,128,256]{2,3,1,0:T(8,128)(2,1)} fusion(bf16[5,4,128,256]{2,3,1,0:T(8,128)(2,1)} %bitcast_dynamic-update-slice_fusion.2, s32[1024]{0:T(1024)S(1)} %pad_clamp_fusion), kind=kCustom, calls=%fused_computation | custom fusion | bytes 6815796 | tf_op jit(solution)/shard_map/gather | solution.py:48
  31.6 67.0 %all-gather.2.cloned.1.call-done = bf16[13,1,4,256,256]{4,3,2,1,0:T(8,128)(2,1)} async-done(((bf16[13,1,4,128,256]{4,3,2,1,0:T(8,128)(2,1)}), bf16[13,1,4,256,256]{4,3,2,1,0:T(8,128)(2,1)}) %all-gather.2.cloned.1.call-update) | async-done | bytes 6815760 | tf_op jit(solution)/shard_map/all_gather | solution.py:52
  98.6 7.7 %fusion.28 = f32[4,256,256]{1,2,0:T(8,128)} fusion(bf16[13,4,128,256]{2,3,1,0:T(8,128)(2,1)} %gather_fusion, bf16[13,1,4,256,256]{4,3,2,1,0:T(8,128)(2,1)} %all-gather.2.cloned.1.call-done, bf16[13,1,4,256,128]{4,3,2,1,0:T(8,128)(2,1)S(1)} %copy-done), kind=kOutput, calls=%fused_computation.14 | convolution fusion | flops 1746534400 | bytes 14680064 | tf_op jit(solution)/shard_map/wvpr,wvrm->vpm/dot_general | solution.py:55
  106.4 20.4 %reduce-scatter.3.cloned.1.call-done = f32[4,128,256]{1,2,0:T(8,128)} async-done(((f32[4,256,256]{1,2,0:T(8,128)}), f32[4,128,256]{1,2,0:T(8,128)}) %reduce-scatter.3.cloned.1.call-update) | async-done | bytes 524304 | tf_op jit(solution)/shard_map/reduce_scatter | solution.py:58
  126.9 21.2 %all-reduce.8.cloned.1.call-done = f32[4,128,256]{1,2,0:T(8,128)} async-done(((f32[4,128,256]{1,2,0:T(8,128)}), f32[4,128,256]{1,2,0:T(8,128)}) %all-reduce.8.cloned.1.call-update) | async-done | bytes 524304 | tf_op jit(solution)/shard_map/psum | solution.py:59
  148.1 1.9 fusion.48
  150.0 22.2 %all-reduce.4 = (f32[]{:T(128)}, f32[]{:T(128)}) all-reduce(f32[]{:T(128)} %get-tuple-element.7, f32[]{:T(128)} %get-tuple-element.6), channel_id=1, replica_groups=mesh['groups'=2,'sector'=4,'contr'=2,'mpo'=2] {'sector','contr'}, use_global_device_ids=true, to_apply=%region_3.0 | all-reduce | flops 2 | bytes 16 | tf_op jit(solution)/shard_map/psum | solution.py:66
  173.6 1.9 multiply_reduce_fusion
  175.5 17.7 %psum.38 = f32[]{:T(128)} all-reduce(f32[]{:T(128)} %multiply_reduce_fusion), channel_id=1, replica_groups=mesh['groups'=2,'sector'=4,'contr'=2,'mpo'=2] {'sector','contr'}, use_global_device_ids=true, to_apply=%region_7.0 | all-reduce | flops 1 | bytes 8 | tf_op jit(solution)/shard_map/psum | solution.py:71
  193.9 2.0 constant_dynamic-update-slice_fusion.5
  196.0 1.3 collective-permute-start.2
  197.3 1.3 collective-permute-start.3
  198.6 2.5 collective-permute-done.2
  201.1 0.8 constant_dynamic-update-slice_fusion.4
  201.9 3.7 %collective-permute-done.3 = bf16[1,4,128,256]{2,3,1,0:T(8,128)(2,1)S(1)} collective-permute-done((bf16[1,4,128,256]{2,3,1,0:T(8,128)(2,1)S(1)}, bf16[1,4,128,256]{2,3,1,0:T(8,128)(2,1)S(1)}, u32[]{:S(2)}, u32[]{:S(2)}) %collective-permute-start.3) | collective-permute-done | bytes 262176 | tf_op jit(solution)/shard_map/ppermute | solution.py:17
  205.5 0.8 constant_dynamic-update-slice_fusion.3
  206.3 0.7 bitcast_dynamic-update-slice_fusion.1
  207.8 4.1 %gather_fusion.1 = bf16[13,4,128,256]{2,3,1,0:T(8,128)(2,1)} fusion(bf16[5,4,128,256]{2,3,1,0:T(8,128)(2,1)} %bitcast_dynamic-update-slice_fusion, s32[1024]{0:T(1024)S(1)} %pad_clamp_fusion), kind=kCustom, calls=%fused_computation.1 | custom fusion | bytes 6815796 | tf_op jit(solution)/shard_map/gather | solution.py:48
  211.9 7.7 %fusion.37 = f32[4,256,256]{1,2,0:T(8,128)} fusion(bf16[13,4,128,256]{2,3,1,0:T(8,128)(2,1)} %gather_fusion.1, bf16[13,1,4,256,256]{4,3,2,1,0:T(8,128)(2,1)} %all-gather.2.cloned.1.call-done, bf16[13,1,4,256,128]{4,3,2,1,0:T(8,128)(2,1)S(1)} %copy-done), kind=kOutput, calls=%fused_computation.15 | convolution fusion | flops 1746534400 | bytes 14680064 | tf_op jit(solution)/shard_map/wvpr,wvrm->vpm/dot_general | solution.py:55
  219.7 20.3 %reduce-scatter.5.cloned.1.call-done = f32[4,128,256]{1,2,0:T(8,128)} async-done(((f32[4,256,256]{1,2,0:T(8,128)}), f32[4,128,256]{1,2,0:T(8,128)}) %reduce-scatter.5.cloned.1.call-update) | async-done | bytes 524304 | tf_op jit(solution)/shard_map/reduce_scatter | solution.py:58
  240.0 6.1 %all-reduce.9 = bf16[4,128,256]{1,2,0:T(8,128)(2,1)} all-reduce(f32[4,128,256]{1,2,0:T(8,128)} %reduce-scatter.5.cloned.1.call-done), channel_id=1, replica_groups=mesh['groups'=2,'sector'=4,'contr'=2,'mpo'=2] {'mpo'}, use_global_device_ids=true, to_apply=%region_9.0 | all-reduce | flops 131072 | bytes 786432 | tf_op jit(solution)/shard_map/psum | solution.py:59
  246.1 2.1 fusion.53
  248.2 1.8 copy.12
  250.0 1.8 copy.11
  (26 shorter events, 2.6 us)
Async XLA Ops:
  7.2 91.4 %copy-start = (bf16[13,1,4,256,128]{4,3,2,1,0:T(8,128)(2,1)S(1)}, bf16[13,1,4,256,128]{4,3,2,1,0:T(8,128)(2,1)}, u32[]{:S(2)}) copy-start(bf16[13,1,4,256,128]{4,3,2,1,0:T(8,128)(2,1)} %param.8) | copy-start | bytes 10223620
  7.2 2.8 %copy-start.2 = (s32[1,4]{1,0:T(1,128)S(1)}, s32[1,4]{1,0:T(1,128)}, u32[]{:S(2)}) copy-start(s32[1,4]{1,0:T(1,128)} %param.6) | copy-start | bytes 52
  7.2 11.7 %copy-start.3 = (s32[13]{0:T(128)S(1)}, s32[13]{0:T(128)}, u32[]{:S(2)}) copy-start(s32[13]{0:T(128)} %param.9) | copy-start | bytes 160
  7.2 91.4 %all-gather.2.cloned.1.call-start = ((), (), s32[]{:S(2)}) async-start(), calls=%async_computation.2 | async-start | bytes 10223616 | tf_op jit(solution)/shard_map/all_gather | solution.py:52
  7.9 118.9 %reduce-scatter.3.cloned.1.call-start = ((), (), s32[]{:S(2)}) async-start(), calls=%async_computation.3 | async-start | bytes 1572864 | tf_op jit(solution)/shard_map/reduce_scatter | solution.py:58
  12.0 6.9 %copy-start.1 = (bf16[1,4,128,256]{2,3,1,0:T(8,128)(2,1)}, bf16[1,4,128,256]{2,3,1,0:T(8,128)(2,1)S(1)}, u32[]{:S(2)}) copy-start(bf16[1,4,128,256]{2,3,1,0:T(8,128)(2,1)S(1)} %get-tuple-element.13) | copy-start | bytes 786436
  12.0 13.2 %collective-permute-start.1 = (bf16[1,4,128,256]{2,3,1,0:T(8,128)(2,1)S(1)}, bf16[1,4,128,256]{2,3,1,0:T(8,128)(2,1)S(1)}, u32[]{:S(2)}, u32[]{:S(2)}) collective-permute-start(bf16[1,4,128,256]{2,3,1,0:T(8,128)(2,1)S(1)} %get-tuple-element.13), channel_id=1, source_target_pairs={{4,0},{8,4},{12,8},{5,1},{9,5},{13,9},{6,2},{10,6},{14,10},{7,3},{... | collective-permute-start | bytes 786440 | tf_op jit(solution)/shard_map/ppermute | solution.py:17
  13.2 11.1 %collective-permute-start = (bf16[1,4,128,256]{2,3,1,0:T(8,128)(2,1)S(1)}, bf16[1,4,128,256]{2,3,1,0:T(8,128)(2,1)S(1)}, u32[]{:S(2)}, u32[]{:S(2)}) collective-permute-start(bf16[1,4,128,256]{2,3,1,0:T(8,128)(2,1)S(1)} %get-tuple-element.13), channel_id=1, source_target_pairs={{0,4},{4,8},{8,12},{1,5},{5,9},{9,13},{2,6},{6,10},{10,14},{3,7},{... | collective-permute-start | bytes 786440 | tf_op jit(solution)/shard_map/ppermute | solution.py:15
  106.4 41.7 %all-reduce.8.cloned.1.call-start = ((), (), s32[]{:S(2)}) async-start(), calls=%async_computation.4 | async-start | bytes 1048576 | tf_op jit(solution)/shard_map/psum | solution.py:59
  126.9 113.1 %reduce-scatter.5.cloned.1.call-start = ((), (), s32[]{:S(2)}) async-start(), calls=%async_computation.5 | async-start | bytes 1572864 | tf_op jit(solution)/shard_map/reduce_scatter | solution.py:58
  196.0 5.2 %collective-permute-start.2 = (bf16[1,4,128,256]{2,3,1,0:T(8,128)(2,1)S(1)}, bf16[1,4,128,256]{2,3,1,0:T(8,128)(2,1)S(1)}, u32[]{:S(2)}, u32[]{:S(2)}) collective-permute-start(bf16[1,4,128,256]{2,3,1,0:T(8,128)(2,1)S(1)} %get-tuple-element.11), channel_id=1, source_target_pairs={{0,4},{4,8},{8,12},{1,5},{5,9},{9,13},{2,6},{6,10},{10,14},{3,7},{... | collective-permute-start | bytes 786440 | tf_op jit(solution)/shard_map/ppermute | solution.py:15
  197.3 8.3 %collective-permute-start.3 = (bf16[1,4,128,256]{2,3,1,0:T(8,128)(2,1)S(1)}, bf16[1,4,128,256]{2,3,1,0:T(8,128)(2,1)S(1)}, u32[]{:S(2)}, u32[]{:S(2)}) collective-permute-start(bf16[1,4,128,256]{2,3,1,0:T(8,128)(2,1)S(1)} %get-tuple-element.11), channel_id=1, source_target_pairs={{4,0},{8,4},{12,8},{5,1},{9,5},{13,9},{6,2},{10,6},{14,10},{7,3},{... | collective-permute-start | bytes 786440 | tf_op jit(solution)/shard_map/ppermute | solution.py:17
Sparse Core Ops, SparseCore 0:
  9.6 88.9 all-gather.1
  106.5 20.3 reduce-scatter.2
  129.3 18.7 all-reduce.7
  219.8 20.1 reduce-scatter.4
where the time goes:
time: 260 us; the launch traced here: 259 us
  waiting for transfers between devices  141 us (54%)
  blocking collectives  46.1 us (18%)
  local copies, waits for them, and re-layouts  20 us (8%)
  between operations  17 us (7%)
  matrix products  15.5 us (6%)
  other arithmetic  10.1 us (4%)
  starting transfers between devices  9.59 us (4%)
    all_gather x1, waiting for transfers between devices, apply_h(): lax.all_gather(left_env, 'contr', axis=3, tiled=True)[:, 0]  67 us
    reduce_scatter x2, waiting for transfers between devices, apply_h(): lax.psum_scatter(partial_sum, 'contr', scatter_dimension=1, tiled=True)  40.7 us
    psum x1, blocking collectives, on_device(): lax.psum((jnp.sum(trial * image_one), jnp.sum(trial * trial)), ('sector',...  22.2 us
    psum x1, waiting for transfers between devices, apply_h(): summed = lax.psum(summed, 'mpo')  21.2 us
    psum x1, blocking collectives, on_device(): total_sq = lax.psum(jnp.sum(resid * resid), ('sector', 'contr'))  17.7 us
    dot_general x2, matrix products, apply_h(): jnp.einsum('wvpr,wvrm->vpm', right_env[:, 0], inner, preferred_element_ty...  15.5 us
    unnamed x17, local copies, waits for them, and re-layouts  10 us
    gather x2, local copies, waits for them, and re-layouts, apply_h(): sources = stacked[term_shift]  8.41 us
  transfers between devices with their start and end apart: 8, of which 7 were waited for; matrix products, arithmetic and copies ran while one was open for 5% of the time, Pallas kernels for 0%

commit v1 on v0

--- a/solution.py
+++ b/solution.py
@@ -1,7 +1,14 @@
+import functools
+
 import jax
 import jax.numpy as jnp
 from jax import lax
+from jax.experimental import pallas as pl
+from jax.experimental.pallas import tpu as pltpu
 from jax.sharding import PartitionSpec as P
+
+CHUNKS = (4, 4, 3, 2)
+EPS = 1e-06
 
 
 def padded(cells, sides, width):
@@ -21,7 +28,7 @@
     return cells
 
 
-def on_device(psi, sector_size, left_env, right_env, term_shift):
+def on_device_gather(psi, sector_size, left_env, right_env, term_shift):
     slots = psi.shape[1]
     rows_here = psi.shape[2]
     width = psi.shape[3]
@@ -66,10 +73,10 @@
     product, squares = lax.psum(
         (jnp.sum(trial * image_one), jnp.sum(trial * trial)), ("sector", "contr")
     )
-    ritz_value = product / (squares + 1e-06)
+    ritz_value = product / (squares + EPS)
     resid = image_one - ritz_value * trial
     total_sq = lax.psum(jnp.sum(resid * resid), ("sector", "contr"))
-    factor = lax.rsqrt(total_sq / entries + 1e-06)
+    factor = lax.rsqrt(total_sq / entries + EPS)
     second = (resid * factor).astype(jnp.bfloat16)
     image_two = apply_h(second)
     return (
@@ -79,9 +86,297 @@
     )
 
 
+def live_block(shape, live):
+    rows = lax.broadcasted_iota(jnp.int32, shape, 0)
+    cols = lax.broadcasted_iota(jnp.int32, shape, 1)
+    return (rows < live) & (cols < live)
+
+
+def term(source, left, right):
+    inner = lax.dot_general(
+        source, left, (((1,), (1,)), ((), ())), preferred_element_type=jnp.float32
+    ).astype(jnp.bfloat16)
+    return jnp.dot(right, inner, preferred_element_type=jnp.float32)
+
+
+def first_kernel(start, stop, last, info, *refs):
+    (l_own, r_own, l_core, r_core, l_side, r_side, l_diag, r_diag, source) = refs[:9]
+    refs = refs[9:]
+    if start:
+        before, refs = refs[0], refs[3:]
+    left, right, total = refs[:3]
+    step = pl.program_id(0)
+    half = l_side.shape[1]
+    mine = pl.multiple_of(info[0] * half, half)
+    theirs = pl.multiple_of((1 - info[0]) * half, half)
+
+    @pl.when(step == 0)
+    def _():
+        total[...] = before[...] if start else jnp.zeros_like(total)
+
+    halves = (
+        (l_own[0, 0, 0], r_own[0, 0, 0], l_side[0], r_side[0]),
+        (l_core[0], r_core[0], l_diag[0], r_diag[0]),
+    )
+    terms = pl.num_programs(0)
+    sums = None
+    for core, (left_a, right_a, left_b, right_b) in enumerate(halves):
+        left[0, core, pl.ds(mine, half), :] = left_a
+        left[0, core, pl.ds(theirs, half), :] = left_b
+        right[0, core, :, pl.ds(mine, half)] = right_a
+        right[0, core, :, pl.ds(theirs, half)] = right_b
+        shift = info[3 + core * info[2] + start + step]
+        part = term(source[shift], left[0, core], right[0, core])
+        sums = part if sums is None else sums + part
+    total[...] += sums
+    if last:
+        image, stats = refs[3:5]
+
+        @pl.when(step == terms - 1)
+        def _():
+            field = source[0].astype(jnp.float32)
+            block = jnp.where(live_block(field.shape, info[1]), total[...], 0.0)
+            image[...] = block.astype(image.dtype)
+            total[...] = block
+            product = jnp.sum(field * block, keepdims=True)
+            squares = jnp.sum(field * field, keepdims=True)
+            quotient = product / (squares + EPS)
+            resid = block - quotient * field
+            rest = jnp.sum(resid * resid, keepdims=True)
+            lanes = stats.shape[1]
+            for row, value in enumerate((product, squares, rest, quotient)):
+                stats[row : row + 1, :] = jnp.broadcast_to(value, (1, lanes))
+
+
+def second_kernel(entries, info, left, right, blocks, source, stats, image, ritz, second, total):
+    step = pl.program_id(0)
+
+    @pl.when(step == 0)
+    def _():
+        count, slots = stats.shape[:2]
+        tiles = []
+        for u in range(count):
+            shift = lax.rem(info[0] - u + count, count)
+            for v in range(slots):
+                tiles.append(stats[shift, info[1] ^ v])
+        product = sum(t[0:1] for t in tiles)
+        squares = sum(t[1:2] for t in tiles)
+        quotient = product / (squares + EPS)
+        rest = jnp.zeros_like(quotient)
+        for t in tiles:
+            off = t[3:4] - quotient
+            cross = t[0:1] - t[3:4] * t[1:2]
+            rest += t[2:3] + 2.0 * off * cross + off * off * t[1:2]
+        factor = lax.rsqrt(rest / entries + EPS)
+        ritz[...] = jnp.broadcast_to(quotient, ritz.shape)
+        for place, block in enumerate(blocks):
+            resid = block[...] - quotient[:, :1] * source[place].astype(jnp.float32)
+            second[place] = (resid * factor[:, :1]).astype(jnp.bfloat16)
+        total[...] = jnp.zeros_like(total)
+
+    cores = left.shape[1]
+    sums = None
+    for core in range(cores):
+        shift = info[3 + core * pl.num_programs(0) + step]
+        part = term(second[shift], left[0, core], right[0, core])
+        sums = part if sums is None else sums + part
+    total[...] += sums
+
+    @pl.when(step == pl.num_programs(0) - 1)
+    def _():
+        live = live_block(total.shape, info[2])
+        image[...] = jnp.where(live, total[...], 0.0).astype(image.dtype)
+
+
+def on_device(psi, sector_size, left_env, right_env, term_shift):
+    terms, _, slots, half, width = left_env.shape
+    cell = ("contr", "mpo")
+    across, core = lax.axis_index("contr"), lax.axis_index("mpo")
+    me = across * 2 + core
+    sector = lax.axis_index("sector")
+    sectors = lax.axis_size("sector")
+
+    def swap(array, flip):
+        return lax.ppermute(array, cell, [(i, i ^ flip) for i in range(slots)])
+
+    def pick(array, flip, start, stop):
+        part = lax.slice_in_dim(array, start, stop, axis=0)[:, 0]
+        return lax.dynamic_index_in_dim(part, me ^ flip, 1, keepdims=False)
+
+    psi_theirs = swap(lax.dynamic_slice_in_dim(psi[0], 1 - across, 3, axis=0), 2)
+    psi_mine = lax.dynamic_slice_in_dim(psi[0], across, 3, axis=0)
+    shift_core = swap(term_shift, 1)
+    chunks = []
+    start = 0
+    for size in CHUNKS:
+        stop = start + size
+        chunks.append(
+            (start, stop)
+            + tuple(
+                swap(pick(env, flip, start, stop), flip)
+                for flip in (2, 3)
+                for env in (left_env, right_env)
+            )
+        )
+        start = stop
+    left_core = swap(pick(left_env, 1, 0, terms), 1)
+    right_core = swap(pick(right_env, 1, 0, terms), 1)
+
+    whole = jnp.where(
+        across == 0,
+        jnp.concatenate([psi_mine, psi_theirs], axis=1),
+        jnp.concatenate([psi_theirs, psi_mine], axis=1),
+    )
+    sizes = lax.dynamic_slice_in_dim(sector_size[0], across, 3, axis=0)[:, None, None]
+    ids = lax.iota(jnp.int32, width)
+    live = (ids[None, :, None] < sizes) & (ids[None, None, :] < sizes)
+    whole = jnp.where(live, whole, jnp.zeros_like(whole))
+    blank = jnp.zeros_like(whole[:1])
+    framed = jnp.concatenate([blank, whole, blank], axis=0)
+    own = lax.dynamic_index_in_dim(whole, me - across, 0, keepdims=False)
+    up = [(i, i + 1) for i in range(sectors - 1)]
+    down = [(i + 1, i) for i in range(sectors - 1)]
+    source = jnp.stack(
+        [
+            own,
+            lax.ppermute(own, "sector", up),
+            lax.ppermute(own, "sector", down),
+            lax.dynamic_index_in_dim(framed, me - across, 0, keepdims=False),
+            lax.dynamic_index_in_dim(framed, me - across + 2, 0, keepdims=False),
+        ]
+    )
+    size_here = lax.dynamic_index_in_dim(sector_size[0], me, 0, keepdims=False)
+    shifts = jnp.concatenate([term_shift, shift_core])
+    info = jnp.concatenate(
+        [jnp.stack([across, size_here, jnp.int32(terms), me]).astype(jnp.int32)[:3], shifts, me[None]]
+    )
+    spot = info.shape[0] - 1
+
+    kept = None
+    both = jax.ShapeDtypeStruct((terms, 2, width, width), jnp.bfloat16)
+    plain = jax.ShapeDtypeStruct((width, width), jnp.float32)
+    flat = pl.BlockSpec((width, width), lambda i, s: (0, 0))
+    for start, stop, l_side, r_side, l_diag, r_diag in chunks:
+        last = stop == terms
+        pair = pl.BlockSpec((1, 2, width, width), lambda i, s, at=start: (at + i, 0, 0, 0))
+        l_row = lambda at: pl.BlockSpec((1, half, width), lambda i, s, at=at: (at + i, 0, 0))
+        r_row = lambda at: pl.BlockSpec((1, width, half), lambda i, s, at=at: (at + i, 0, 0))
+        in_specs = [
+            pl.BlockSpec((1, 1, 1, half, width), lambda i, s, at=start: (at + i, 0, s[spot], 0, 0)),
+            pl.BlockSpec((1, 1, 1, width, half), lambda i, s, at=start: (at + i, 0, s[spot], 0, 0)),
+            l_row(start),
+            r_row(start),
+            l_row(0),
+            r_row(0),
+            l_row(0),
+            r_row(0),
+            pl.BlockSpec((5, width, width), lambda i, s: (0, 0, 0)),
+        ]
+        operands = [left_env, right_env, left_core, right_core, l_side, r_side, l_diag, r_diag, source]
+        aliases = {}
+        if start:
+            in_specs += [flat, pl.BlockSpec(memory_space=pl.ANY), pl.BlockSpec(memory_space=pl.ANY)]
+            operands += [kept[2], kept[0], kept[1]]
+            aliases = {11: 0, 12: 1}
+        out_shape = [both, both, plain]
+        out_specs = [pair, pair, flat]
+        if last:
+            out_shape += [
+                jax.ShapeDtypeStruct((width, width), jnp.bfloat16),
+                jax.ShapeDtypeStruct((8, 128), jnp.float32),
+            ]
+            out_specs += [flat, pl.BlockSpec((8, 128), lambda i, s: (0, 0))]
+        flops = 8 * (stop - start) * width**3
+        kept = pl.pallas_call(
+            functools.partial(first_kernel, start, stop, last),
+            grid_spec=pltpu.PrefetchScalarGridSpec(
+                num_scalar_prefetch=1,
+                grid=(stop - start,),
+                in_specs=in_specs,
+                out_specs=out_specs,
+            ),
+            out_shape=out_shape,
+            input_output_aliases=aliases,
+            compiler_params=pltpu.CompilerParams(vmem_limit_bytes=32 * 2**20),
+            cost_estimate=pl.CostEstimate(
+                flops=flops, bytes_accessed=(stop - start) * 2**20, transcendentals=0
+            ),
+            name=f"first_terms_{start}",
+        )(info, *operands)
+    left_all, right_all, image_one, first_here, stats = kept
+
+    slot_up = [(i, i + 1) for i in range(slots - 1)]
+    slot_down = [(i + 1, i) for i in range(slots - 1)]
+    blocks = [
+        image_one,
+        lax.ppermute(image_one, "sector", up),
+        lax.ppermute(image_one, "sector", down),
+        lax.ppermute(image_one, cell, slot_up),
+        lax.ppermute(image_one, cell, slot_down),
+    ]
+    stats = jnp.stack([stats, swap(stats, 1), swap(stats, 2), swap(stats, 3)])
+    stats = jnp.stack(
+        [stats]
+        + [
+            lax.ppermute(stats, "sector", [(i, (i + d) % sectors) for i in range(sectors)])
+            for d in range(1, sectors)
+        ]
+    )
+
+    info_two = jnp.concatenate(
+        [jnp.stack([sector, me, size_here]).astype(jnp.int32), shifts]
+    )
+    pair = pl.BlockSpec((1, 2, width, width), lambda i, s: (i, 0, 0, 0))
+    entries = float(sectors * slots * width * width)
+    second_here, ritz = pl.pallas_call(
+        lambda info, left, right, b0, b1, b2, b3, b4, *refs: second_kernel(
+            entries, info, left, right, (b0, b1, b2, b3, b4), *refs
+        ),
+        grid_spec=pltpu.PrefetchScalarGridSpec(
+            num_scalar_prefetch=1,
+            grid=(terms,),
+            in_specs=[pair, pair]
+            + [flat] * 5
+            + [
+                pl.BlockSpec((5, width, width), lambda i, s: (0, 0, 0)),
+                pl.BlockSpec(stats.shape, lambda i, s: (0, 0, 0, 0)),
+            ],
+            out_specs=[flat, pl.BlockSpec((8, 128), lambda i, s: (0, 0))],
+            scratch_shapes=[
+                pltpu.VMEM((5, width, width), jnp.bfloat16),
+                pltpu.VMEM((width, width), jnp.float32),
+            ],
+        ),
+        out_shape=[
+            jax.ShapeDtypeStruct((width, width), jnp.bfloat16),
+            jax.ShapeDtypeStruct((8, 128), jnp.float32),
+        ],
+        compiler_params=pltpu.CompilerParams(vmem_limit_bytes=32 * 2**20),
+        cost_estimate=pl.CostEstimate(
+            flops=8 * terms * width**3, bytes_accessed=terms * 2**19, transcendentals=0
+        ),
+        name="second_terms",
+    )(info_two, left_all, right_all, *blocks, source, stats)
+
+    def spread(block):
+        halves = block.reshape(2, half, width)
+        mine = lax.dynamic_index_in_dim(halves, across, 0, keepdims=False)
+        theirs = lax.dynamic_index_in_dim(halves, 1 - across, 0, keepdims=False)
+        got = jnp.stack([mine, swap(mine, 1), swap(theirs, 2), swap(theirs, 3)])
+        return got[me ^ lax.iota(jnp.int32, slots)][None]
+
+    return spread(first_here), spread(second_here), ritz[0, :1]
+
+
 def solution(mesh):
+    fits = mesh.shape["contr"] == 2 and mesh.shape["mpo"] == 2
+
+    def body(psi, sector_size, left_env, right_env, term_shift):
+        run = on_device if fits and psi.shape[1] == 4 else on_device_gather
+        return run(psi, sector_size, left_env, right_env, term_shift)
+
     return jax.shard_map(
-        on_device,
+        body,
         mesh=mesh,
         in_specs=(
             P(("groups", "sector"), None, "contr", None),

time: 260 us -> 156 us (0.60)
  waiting for transfers between devices: 141 us -> 42 us
  blocking collectives: 46.1 us -> 0 us
  starting transfers between devices: 9.59 us -> 47 us
  Pallas kernels: 0 us -> 22.4 us
  local copies, waits for them, and re-layouts: 20 us -> 40.2 us
  between operations: 17 us -> 0.99 us
  matrix products: 15.5 us -> 0 us
  other arithmetic: 10.1 us -> 2.79 us
    all_gather x1 -> x0, waiting for transfers between devices: 67 us -> none  [apply_h(): lax.all_gather(left_env, 'contr', axis=3, tiled=True)[:, 0]]
    psum x3 -> x0, blocking collectives: 46.1 us -> none  [the longest x1 22.2 us: on_device(): lax.psum((jnp.sum(trial * image_one), jnp.sum(trial * trial)), ('sector',...]
    reduce_scatter x2 -> x0, waiting for transfers between devices: 40.7 us -> none  [apply_h(): lax.psum_scatter(partial_sum, 'contr', scatter_dimension=1, tiled=True)]
    ppermute x4 -> x38, starting transfers between devices: 9.44 us -> 47 us  [the longest x29 25.9 us: swap(): return lax.ppermute(array, cell, [(i, i ^ flip) for i in range(slots)])]
    ppermute x4 -> x38, waiting for transfers between devices: 11.6 us -> 42 us  [the longest x29 38.4 us: swap(): return lax.ppermute(array, cell, [(i, i ^ flip) for i in range(slots)])]
    pallas_call x0 -> x5, Pallas kernels: none -> 22.4 us  [the longest x4 12.4 us: on_device(): pl.pallas_call(functools.partial(first_kernel, start, stop, last), grid_s...]
    psum x1 -> x0, waiting for transfers between devices: 21.2 us -> none  [apply_h(): summed = lax.psum(summed, 'mpo')]
    dot_general x2 -> x0, matrix products: 15.5 us -> none  [apply_h(): jnp.einsum('wvpr,wvrm->vpm', right_env[:, 0], inner, preferred_element_ty...]
  transfers between devices with their start and end apart: 8 -> 38, of which waited for: 7 -> 13; matrix products, arithmetic and copies ran while one was open for 5% -> 15% of each run, Pallas kernels for 0% -> 13%
where the time goes in v1:
time: 156 us; the launch traced here: 155 us
  starting transfers between devices  47 us (30%)
  waiting for transfers between devices  42 us (27%)
  local copies, waits for them, and re-layouts  40.2 us (26%)
  Pallas kernels  22.4 us (14%)
  other arithmetic  2.79 us (2%)
    ppermute x29, waiting for transfers between devices, swap(): return lax.ppermute(array, cell, [(i, i ^ flip) for i in range(slots)])  38.4 us
    ppermute x29, starting transfers between devices, swap(): return lax.ppermute(array, cell, [(i, i ^ flip) for i in range(slots)])  25.9 us
    unnamed x51, local copies, waits for them, and re-layouts  16.7 us
    pallas_call x4, Pallas kernels, on_device(): pl.pallas_call(functools.partial(first_kernel, start, stop, last), grid_s...  12.4 us
    squeeze x10, local copies, waits for them, and re-layouts, pick(): return lax.dynamic_index_in_dim(part, me ^ flip, 1, keepdims=False)  10.8 us
    pallas_call x1, Pallas kernels, on_device(): pl.pallas_call(lambda info, left, right, b0, b1, b2, b3, b4, *refs: secon...  9.95 us
    ppermute x3, starting transfers between devices, on_device(): lax.ppermute(stats, 'sector', [(i, (i + d) % sectors) for i in range(sect...  6.51 us
    slice x10, local copies, waits for them, and re-layouts, pick(): part = lax.slice_in_dim(array, start, stop, axis=0)[:, 0]  4.46 us
  transfers between devices with their start and end apart: 38, of which 13 were waited for; matrix products, arithmetic and copies ran while one was open for 15% of the time, Pallas kernels for 13%

profile of v1, /device:TPU:0, one launch (start us, length us, event | category | flops | bytes accessed | tf_op | source)
XLA Modules:
  0.0 155.4 jit_solution(12102971536688510053)
XLA Ops:
  2.4 2.9 %collective-permute-start.7 = (bf16[3,128,256]{2,1,0:T(8,128)(2,1)}, bf16[3,128,256]{2,1,0:T(8,128)(2,1)S(1)}, u32[]{:S(2)}, u32[]{:S(2)}) collective-permute-start(bf16[3,128,256]{2,1,0:T(8,128)(2,1)} %get-tuple-element.58), channel_id=1, source_target_pairs={{0,2},{1,3},{2,0},{3,1},{4,6},{5,7},{6,4},{7,5},{8,10},{9,11},{10,... | collective-permute-start | bytes 589832 | tf_op jit(solution)/shard_map/ppermute | solution.py:200
  7.9 2.8 %fusion.3 = (bf16[4,1,4,256,128]{4,3,2,1,0:T(8,128)(2,1)S(1)}, bf16[4,1,4,256,128]{4,3,2,1,0:T(8,128)(2,1)}) fusion(bf16[13,1,4,256,128]{4,3,2,1,0:T(8,128)(2,1)} %refs_1_.7), kind=kLoop, calls=%fused_computation.47 | loop fusion | bytes 4194304 | tf_op jit(solution)/shard_map/slice | solution.py:203
  11.5 1.9 %collective-permute-start.19 = (bf16[4,256,128]{2,1,0:T(8,128)(2,1)}, bf16[4,256,128]{2,1,0:T(8,128)(2,1)}, u32[]{:S(2)}, u32[]{:S(2)}) collective-permute-start(bf16[4,256,128]{2,1,0:T(8,128)(2,1)} %get-tuple-element.40), channel_id=1, source_target_pairs={{0,2},{1,3},{2,0},{3,1},{4,6},{5,7},{6,4},{7,5},{8,10},{9,11},{10,... | collective-permute-start | bytes 786440 | tf_op jit(solution)/shard_map/ppermute | solution.py:200
  14.4 2.1 %dynamic-slice_bitcast_fusion.1 = bf16[13,128,256]{2,1,0:T(8,128)(2,1)} fusion(bf16[13,1,4,128,256]{4,3,2,1,0:T(8,128)(2,1)} %refs_0_.7, s32[]{:T(128)S(6)} %select_n.87), kind=kLoop, calls=%fused_computation.3 | loop fusion | bytes 1703940 | tf_op jit(solution)/shard_map/jit(dynamic_index_in_dim)/squeeze | solution.py:204
  16.5 2.3 %dynamic-slice_bitcast_fusion = bf16[13,256,128]{2,1,0:T(8,128)(2,1)} fusion(bf16[13,1,4,256,128]{4,3,2,1,0:T(8,128)(2,1)} %refs_1_.7, s32[]{:T(128)S(6)} %select_n.87), kind=kLoop, calls=%fused_computation.2 | loop fusion | bytes 1703940 | tf_op jit(solution)/shard_map/jit(dynamic_index_in_dim)/squeeze | solution.py:204
  22.0 1.8 %collective-permute-start.20 = (bf16[4,128,256]{2,1,0:T(8,128)(2,1)}, bf16[4,128,256]{2,1,0:T(8,128)(2,1)S(1)}, u32[]{:S(2)}, u32[]{:S(2)}) collective-permute-start(bf16[4,128,256]{2,1,0:T(8,128)(2,1)} %get-tuple-element.41), channel_id=1, source_target_pairs={{0,3},{1,2},{2,1},{3,0},{4,7},{5,6},{6,5},{7,4},{8,11},{9,10},{10,... | collective-permute-start | bytes 786440 | tf_op jit(solution)/shard_map/ppermute | solution.py:200
  24.2 2.2 %collective-permute-done.10.refs_4_ = bf16[3,128,256]{2,1,0:T(8,128)(2,1)S(1)} collective-permute-done((bf16[3,128,256]{2,1,0:T(8,128)(2,1)}, bf16[3,128,256]{2,1,0:T(8,128)(2,1)S(1)}, u32[]{:S(2)}, u32[]{:S(2)}) %collective-permute-start.10) | collective-permute-done | bytes 196640 | tf_op jit(solution)/shard_map/ppermute | solution.py:200
  27.4 8.9 %collective-permute-done.11.refs_5_ = bf16[3,256,128]{2,1,0:T(8,128)(2,1)S(1)} collective-permute-done((bf16[3,256,128]{2,1,0:T(8,128)(2,1)S(1)}, bf16[3,256,128]{2,1,0:T(8,128)(2,1)S(1)}, u32[]{:S(2)}, u32[]{:S(2)}) %collective-permute-start.11) | collective-permute-done | bytes 196640 | tf_op jit(solution)/shard_map/ppermute | solution.py:200
  36.2 3.2 %collective-permute-done.12.refs_6_ = bf16[3,128,256]{2,1,0:T(8,128)(2,1)S(1)} collective-permute-done((bf16[3,128,256]{2,1,0:T(8,128)(2,1)}, bf16[3,128,256]{2,1,0:T(8,128)(2,1)S(1)}, u32[]{:S(2)}, u32[]{:S(2)}) %collective-permute-start.12) | collective-permute-done | bytes 196640 | tf_op jit(solution)/shard_map/ppermute | solution.py:200
  39.8 4.4 %collective-permute-start.8 = (bf16[256,256]{1,0:T(8,128)(2,1)}, bf16[256,256]{1,0:T(8,128)(2,1)}, u32[]{:S(2)}, u32[]{:S(2)}) collective-permute-start(bf16[256,256]{1,0:T(8,128)(2,1)} %get-tuple-element.55), channel_id=1, source_target_pairs={{0,4},{4,8},{8,12},{1,5},{5,9},{9,13},{2,6},{6,10},{10,14},{3,7},{... | collective-permute-start | bytes 393224 | tf_op jit(solution)/shard_map/ppermute | solution.py:242
  51.3 3.5 %collective-permute-done.21.refs_7_ = bf16[4,256,128]{2,1,0:T(8,128)(2,1)S(1)} collective-permute-done((bf16[4,256,128]{2,1,0:T(8,128)(2,1)}, bf16[4,256,128]{2,1,0:T(8,128)(2,1)S(1)}, u32[]{:S(2)}, u32[]{:S(2)}) %collective-permute-start.21) | collective-permute-done | bytes 262176 | tf_op jit(solution)/shard_map/ppermute | solution.py:200
  56.3 4.6 %collective-permute-done.14.refs_4_ = bf16[4,128,256]{2,1,0:T(8,128)(2,1)S(1)} collective-permute-done((bf16[4,128,256]{2,1,0:T(8,128)(2,1)}, bf16[4,128,256]{2,1,0:T(8,128)(2,1)S(1)}, u32[]{:S(2)}, u32[]{:S(2)}) %collective-permute-start.14) | collective-permute-done | bytes 262176 | tf_op jit(solution)/shard_map/ppermute | solution.py:200
  62.8 3.8 %collective-permute-done.15.refs_5_ = bf16[4,256,128]{2,1,0:T(8,128)(2,1)S(1)} collective-permute-done((bf16[4,256,128]{2,1,0:T(8,128)(2,1)}, bf16[4,256,128]{2,1,0:T(8,128)(2,1)S(1)}, u32[]{:S(2)}, u32[]{:S(2)}) %collective-permute-start.15) | collective-permute-done | bytes 262176 | tf_op jit(solution)/shard_map/ppermute | solution.py:200
  68.1 3.5 %collective-permute-done.16.refs_6_ = bf16[4,128,256]{2,1,0:T(8,128)(2,1)S(1)} collective-permute-done((bf16[4,128,256]{2,1,0:T(8,128)(2,1)}, bf16[4,128,256]{2,1,0:T(8,128)(2,1)S(1)}, u32[]{:S(2)}, u32[]{:S(2)}) %collective-permute-start.16) | collective-permute-done | bytes 262176 | tf_op jit(solution)/shard_map/ppermute | solution.py:200
  73.2 4.1 %collective-permute-done.17.refs_7_ = bf16[4,256,128]{2,1,0:T(8,128)(2,1)S(1)} collective-permute-done((bf16[4,256,128]{2,1,0:T(8,128)(2,1)}, bf16[4,256,128]{2,1,0:T(8,128)(2,1)S(1)}, u32[]{:S(2)}, u32[]{:S(2)}) %collective-permute-start.17) | collective-permute-done | bytes 262176 | tf_op jit(solution)/shard_map/ppermute | solution.py:200
  82.4 2.0 %copy-done.1 = bf16[13,1,4,128,256]{4,3,2,1,0:T(8,128)(2,1)S(1)} copy-done((bf16[13,1,4,128,256]{4,3,2,1,0:T(8,128)(2,1)S(1)}, bf16[13,1,4,128,256]{4,3,2,1,0:T(8,128)(2,1)}, u32[]{:S(2)}) %copy-start.1) | copy-done | bytes 3407896
  84.4 2.0 %copy-done.2 = bf16[13,1,4,256,128]{4,3,2,1,0:T(8,128)(2,1)S(1)} copy-done((bf16[13,1,4,256,128]{4,3,2,1,0:T(8,128)(2,1)S(1)}, bf16[13,1,4,256,128]{4,3,2,1,0:T(8,128)(2,1)}, u32[]{:S(2)}) %copy-start.2) | copy-done | bytes 3407896
  90.7 4.1 %first_terms_0.1 = (bf16[13,2,256,256]{3,2,1,0:T(8,128)(2,1)S(1)}, bf16[13,2,256,256]{3,2,1,0:T(8,128)(2,1)S(1)}, f32[256,256]{1,0:T(8,128)S(1)}) custom-call(s32[30]{0:T(128)S(1)} %concatenate.18.info, bf16[13,1,4,128,256]{4,3,2,1,0:T(8,128)(2,1)S(1)} %copy-done.1, bf16[13,1,4,256,128]{4,3,2,1,0:T(8,128)(2,1)S(1)} %copy-done.2, ...), custom_call_target="tpu_custom_call" | custom-call | flops 536870912 | bytes 4194304 | tf_op jit(solution)/shard_map/first_terms_0/pallas_call | solution.py:290
  94.9 3.0 %first_terms_4.1 = (bf16[13,2,256,256]{3,2,1,0:T(8,128)(2,1)S(1)}, bf16[13,2,256,256]{3,2,1,0:T(8,128)(2,1)S(1)}, f32[256,256]{1,0:T(8,128)S(1)}) custom-call(s32[30]{0:T(128)S(1)} %concatenate.18.info, bf16[13,1,4,128,256]{4,3,2,1,0:T(8,128)(2,1)S(1)} %copy-done.1, ...), custom_call_target="tpu_custom_call", output_to_operand_aliasing={{0}: (11, {}), {1}: (12, {})} | custom-call | flops 536870912 | bytes 4194304 | tf_op jit(solution)/shard_map/first_terms_4/pallas_call | solution.py:290
  97.9 2.4 %first_terms_8.1 = (bf16[13,2,256,256]{3,2,1,0:T(8,128)(2,1)S(1)}, bf16[13,2,256,256]{3,2,1,0:T(8,128)(2,1)S(1)}, f32[256,256]{1,0:T(8,128)S(1)}) custom-call(s32[30]{0:T(128)S(1)} %concatenate.18.info, bf16[13,1,4,128,256]{4,3,2,1,0:T(8,128)(2,1)S(1)} %copy-done.1, ...), custom_call_target="tpu_custom_call", output_to_operand_aliasing={{0}: (11, {}), {1}: (12, {})} | custom-call | flops 402653184 | bytes 3145728 | tf_op jit(solution)/shard_map/first_terms_8/pallas_call | solution.py:290
  100.4 2.9 %first_terms_11.1 = (bf16[13,2,256,256]{3,2,1,0:T(8,128)(2,1)S(1)}, bf16[13,2,256,256]{3,2,1,0:T(8,128)(2,1)S(1)}, f32[256,256]{1,0:T(8,128)}, bf16[256,256]{1,0:T(8,128)(2,1)S(1)}, f32[8,128]{1,0:T(8,128)S(1)}) custom-call(s32[30]{0:T(128)S(1)} %concatenate.18.info, ...), custom_call_target="tpu_custom_call", output_to_operand_aliasing={{0}: (11, {}), {1}: (12, {})} | custom-call | flops 268435456 | bytes 2097152 | tf_op jit(solution)/shard_map/first_terms_11/pallas_call | solution.py:290
  106.9 2.1 %collective-permute-done.30 = f32[8,128]{1,0:T(8,128)S(1)} collective-permute-done((f32[8,128]{1,0:T(8,128)S(1)}, f32[8,128]{1,0:T(8,128)S(1)}, u32[]{:S(2)}, u32[]{:S(2)}) %collective-permute-start.30) | collective-permute-done | bytes 4128 | tf_op jit(solution)/shard_map/ppermute | solution.py:200
  110.6 4.2 %collective-permute-start.25 = (f32[256,256]{1,0:T(8,128)}, f32[256,256]{1,0:T(8,128)}, u32[]{:S(2)}, u32[]{:S(2)}) collective-permute-start(f32[256,256]{1,0:T(8,128)} %get-tuple-element.31.b0), channel_id=1, source_target_pairs={{0,4},{4,8},{8,12},{1,5},{5,9},{9,13},{2,6},{6,10},{10,14},{3,7},{... | collective-permute-start | bytes 786440 | tf_op jit(solution)/shard_map/ppermute | solution.py:312
  116.0 2.2 %collective-permute-start.27 = (f32[256,256]{1,0:T(8,128)}, f32[256,256]{1,0:T(8,128)}, u32[]{:S(2)}, u32[]{:S(2)}) collective-permute-start(f32[256,256]{1,0:T(8,128)} %get-tuple-element.31.b0), channel_id=1, source_target_pairs={{0,1},{1,2},{2,3},{4,5},{5,6},{6,7},{8,9},{9,10},{10,11},{12,13},{... | collective-permute-start | bytes 786440 | tf_op jit(solution)/shard_map/ppermute | solution.py:314
  119.5 1.8 %collective-permute-start.33 = (f32[4,8,128]{2,1,0:T(8,128)}, f32[4,8,128]{2,1,0:T(8,128)}, u32[]{:S(2)}, u32[]{:S(2)}) collective-permute-start(f32[4,8,128]{2,1,0:T(8,128)} %get-tuple-element.64), channel_id=1, source_target_pairs={{0,8},{4,12},{8,0},{12,4},{1,9},{5,13},{9,1},{13,5},{2,10},{6,14},... | collective-permute-start | bytes 49160 | tf_op jit(solution)/shard_map/ppermute | solution.py:321
  122.7 2.0 %collective-permute-done.33 = f32[4,8,128]{2,1,0:T(8,128)} collective-permute-done((f32[4,8,128]{2,1,0:T(8,128)}, f32[4,8,128]{2,1,0:T(8,128)}, u32[]{:S(2)}, u32[]{:S(2)}) %collective-permute-start.33) | collective-permute-done | bytes 16416 | tf_op jit(solution)/shard_map/ppermute | solution.py:321
  124.7 3.7 %collective-permute-start.34 = (f32[4,8,128]{2,1,0:T(8,128)}, f32[4,8,128]{2,1,0:T(8,128)S(1)}, u32[]{:S(2)}, u32[]{:S(2)}) collective-permute-start(f32[4,8,128]{2,1,0:T(8,128)} %get-tuple-element.64), channel_id=1, source_target_pairs={{0,12},{4,0},{8,4},{12,8},{1,13},{5,1},{9,5},{13,9},{2,14},{6,2},{... | collective-permute-start | bytes 49160 | tf_op jit(solution)/shard_map/ppermute | solution.py:321
  130.0 3.7 %collective-permute-start.23 = (bf16[128,256]{1,0:T(8,128)(2,1)S(1)}, bf16[128,256]{1,0:T(8,128)(2,1)S(1)}, u32[]{:S(2)}, u32[]{:S(2)}) collective-permute-start(bf16[128,256]{1,0:T(8,128)(2,1)S(1)} %get-tuple-element.62), channel_id=1, source_target_pairs={{0,2},{1,3},{2,0},{3,1},{4,6},{5,7},{6,4},{7,5},{8,10},{9,11},{10,... | collective-permute-start | bytes 196616 | tf_op jit(solution)/shard_map/ppermute | solution.py:200
  134.6 2.0 %copy-done.4 = bf16[13,2,256,256]{3,2,1,0:T(8,128)(2,1)S(1)} copy-done((bf16[13,2,256,256]{3,2,1,0:T(8,128)(2,1)S(1)}, bf16[13,2,256,256]{3,2,1,0:T(8,128)(2,1)}, u32[]{:S(2)}) %copy-start.4) | copy-done | bytes 3407896
  137.7 9.9 %second_terms.1 = (bf16[256,256]{1,0:T(8,128)(2,1)S(1)}, f32[8,128]{1,0:T(8,128)S(1)}) custom-call(s32[29]{0:T(128)S(1)} %concatenate.22.info, bf16[13,2,256,256]{3,2,1,0:T(8,128)(2,1)S(1)} %get-tuple-element.29.left, bf16[13,2,256,256]{3,2,1,0:T(8,128)(2,1)S(1)} %copy-done.4, f32[256,256]{1,0:T(8,128)} %get-tuple-element.31.b0, ...), custom_call_target="tpu_custom_call" | custom-call | flops 1744830464 | bytes 6815744 | tf_op jit(solution)/shard_map/second_terms/pallas_call | solution.py:331
  147.7 2.1 %collective-permute-start.36 = (bf16[128,256]{1,0:T(8,128)(2,1)S(1)}, bf16[128,256]{1,0:T(8,128)(2,1)S(1)}, u32[]{:S(2)}, u32[]{:S(2)}) collective-permute-start(bf16[128,256]{1,0:T(8,128)(2,1)S(1)} %get-tuple-element.60), channel_id=1, source_target_pairs={{0,2},{1,3},{2,0},{3,1},{4,6},{5,7},{6,4},{7,5},{8,10},{9,11},{10,... | collective-permute-start | bytes 196616 | tf_op jit(solution)/shard_map/ppermute | solution.py:200
  152.2 1.9 %collective-permute-done.37 = bf16[128,256]{1,0:T(8,128)(2,1)S(1)} collective-permute-done((bf16[128,256]{1,0:T(8,128)(2,1)S(1)}, bf16[128,256]{1,0:T(8,128)(2,1)S(1)}, u32[]{:S(2)}, u32[]{:S(2)}) %collective-permute-start.37) | collective-permute-done | bytes 65568 | tf_op jit(solution)/shard_map/ppermute | solution.py:200
  (142 shorter events, 50.3 us)
Async XLA Ops:
  2.4 21.5 %collective-permute-start.7 = (bf16[3,128,256]{2,1,0:T(8,128)(2,1)}, bf16[3,128,256]{2,1,0:T(8,128)(2,1)S(1)}, u32[]{:S(2)}, u32[]{:S(2)}) collective-permute-start(bf16[3,128,256]{2,1,0:T(8,128)(2,1)} %get-tuple-element.58), channel_id=1, source_target_pairs={{0,2},{1,3},{2,0},{3,1},{4,6},{5,7},{6,4},{7,5},{8,10},{9,11},{10,... | collective-permute-start | bytes 589832 | tf_op jit(solution)/shard_map/ppermute | solution.py:200
  7.9 31.8 %collective-permute-start.18 = (bf16[4,128,256]{2,1,0:T(8,128)(2,1)}, bf16[4,128,256]{2,1,0:T(8,128)(2,1)}, u32[]{:S(2)}, u32[]{:S(2)}) collective-permute-start(bf16[4,128,256]{2,1,0:T(8,128)(2,1)} %get-tuple-element.42), channel_id=1, source_target_pairs={{0,2},{1,3},{2,0},{3,1},{4,6},{5,7},{6,4},{7,5},{8,10},{9,11},{10,... | collective-permute-start | bytes 786440 | tf_op jit(solution)/shard_map/ppermute | solution.py:200
  11.5 34.7 %collective-permute-start.19 = (bf16[4,256,128]{2,1,0:T(8,128)(2,1)}, bf16[4,256,128]{2,1,0:T(8,128)(2,1)}, u32[]{:S(2)}, u32[]{:S(2)}) collective-permute-start(bf16[4,256,128]{2,1,0:T(8,128)(2,1)} %get-tuple-element.40), channel_id=1, source_target_pairs={{0,2},{1,3},{2,0},{3,1},{4,6},{5,7},{6,4},{7,5},{8,10},{9,11},{10,... | collective-permute-start | bytes 786440 | tf_op jit(solution)/shard_map/ppermute | solution.py:200
  13.5 8.6 %collective-permute-start = (s32[13]{0:T(128)S(1)}, s32[13]{0:T(128)S(1)}, u32[]{:S(2)}, u32[]{:S(2)}) collective-permute-start(s32[13]{0:T(128)S(1)} %copy-done.22), channel_id=1, source_target_pairs={{0,1},{1,0},{2,3},{3,2},{4,5},{5,4},{6,7},{7,6},{8,9},{9,8},{10,11... | collective-permute-start | bytes 164 | tf_op jit(solution)/shard_map/ppermute | solution.py:200
  14.3 12.1 %collective-permute-start.10 = (bf16[3,128,256]{2,1,0:T(8,128)(2,1)}, bf16[3,128,256]{2,1,0:T(8,128)(2,1)S(1)}, u32[]{:S(2)}, u32[]{:S(2)}) collective-permute-start(bf16[3,128,256]{2,1,0:T(8,128)(2,1)} %get-tuple-element.50), channel_id=1, source_target_pairs={{0,2},{1,3},{2,0},{3,1},{4,6},{5,7},{6,4},{7,5},{8,10},{9,11},{10,... | collective-permute-start | bytes 589832 | tf_op jit(solution)/shard_map/ppermute | solution.py:200
  22.0 25.4 %collective-permute-start.20 = (bf16[4,128,256]{2,1,0:T(8,128)(2,1)}, bf16[4,128,256]{2,1,0:T(8,128)(2,1)S(1)}, u32[]{:S(2)}, u32[]{:S(2)}) collective-permute-start(bf16[4,128,256]{2,1,0:T(8,128)(2,1)} %get-tuple-element.41), channel_id=1, source_target_pairs={{0,3},{1,2},{2,1},{3,0},{4,7},{5,6},{6,5},{7,4},{8,11},{9,10},{10,... | collective-permute-start | bytes 786440 | tf_op jit(solution)/shard_map/ppermute | solution.py:200
  23.9 12.4 %collective-permute-start.11 = (bf16[3,256,128]{2,1,0:T(8,128)(2,1)S(1)}, bf16[3,256,128]{2,1,0:T(8,128)(2,1)S(1)}, u32[]{:S(2)}, u32[]{:S(2)}) collective-permute-start(bf16[3,256,128]{2,1,0:T(8,128)(2,1)S(1)} %get-tuple-element.48), channel_id=1, source_target_pairs={{0,2},{1,3},{2,0},{3,1},{4,6},{5,7},{6,4},{7,5},{8,10},{9,11},{10,... | collective-permute-start | bytes 589832 | tf_op jit(solution)/shard_map/ppermute | solution.py:200
  26.4 13.0 %collective-permute-start.12 = (bf16[3,128,256]{2,1,0:T(8,128)(2,1)}, bf16[3,128,256]{2,1,0:T(8,128)(2,1)S(1)}, u32[]{:S(2)}, u32[]{:S(2)}) collective-permute-start(bf16[3,128,256]{2,1,0:T(8,128)(2,1)} %get-tuple-element.49), channel_id=1, source_target_pairs={{0,3},{1,2},{2,1},{3,0},{4,7},{5,6},{6,5},{7,4},{8,11},{9,10},{10,... | collective-permute-start | bytes 589832 | tf_op jit(solution)/shard_map/ppermute | solution.py:200
  36.2 42.6 %collective-permute-start.1 = (bf16[13,128,256]{2,1,0:T(8,128)(2,1)}, bf16[13,128,256]{2,1,0:T(8,128)(2,1)S(1)}, u32[]{:S(2)}, u32[]{:S(2)}) collective-permute-start(bf16[13,128,256]{2,1,0:T(8,128)(2,1)} %dynamic-slice_bitcast_fusion.1), channel_id=1, source_target_pairs={{0,1},{1,0},{2,3},{3,2},{4,5},{5,4},{6,7},{7,6},{8,9},{9,8},{10,11... | collective-permute-start | bytes 2555912 | tf_op jit(solution)/shard_map/ppermute | solution.py:200
  39.4 40.8 %collective-permute-start.2 = (bf16[13,256,128]{2,1,0:T(8,128)(2,1)}, bf16[13,256,128]{2,1,0:T(8,128)(2,1)S(1)}, u32[]{:S(2)}, u32[]{:S(2)}) collective-permute-start(bf16[13,256,128]{2,1,0:T(8,128)(2,1)} %dynamic-slice_bitcast_fusion), channel_id=1, source_target_pairs={{0,1},{1,0},{2,3},{3,2},{4,5},{5,4},{6,7},{7,6},{8,9},{9,8},{10,11... | collective-permute-start | bytes 2555912 | tf_op jit(solution)/shard_map/ppermute | solution.py:200
  39.8 9.3 %collective-permute-start.8 = (bf16[256,256]{1,0:T(8,128)(2,1)}, bf16[256,256]{1,0:T(8,128)(2,1)}, u32[]{:S(2)}, u32[]{:S(2)}) collective-permute-start(bf16[256,256]{1,0:T(8,128)(2,1)} %get-tuple-element.55), channel_id=1, source_target_pairs={{0,4},{4,8},{8,12},{1,5},{5,9},{9,13},{2,6},{6,10},{10,14},{3,7},{... | collective-permute-start | bytes 393224 | tf_op jit(solution)/shard_map/ppermute | solution.py:242
  46.2 8.6 %collective-permute-start.21 = (bf16[4,256,128]{2,1,0:T(8,128)(2,1)}, bf16[4,256,128]{2,1,0:T(8,128)(2,1)S(1)}, u32[]{:S(2)}, u32[]{:S(2)}) collective-permute-start(bf16[4,256,128]{2,1,0:T(8,128)(2,1)} %get-tuple-element.39), channel_id=1, source_target_pairs={{0,3},{1,2},{2,1},{3,0},{4,7},{5,6},{6,5},{7,4},{8,11},{9,10},{10,... | collective-permute-start | bytes 786440 | tf_op jit(solution)/shard_map/ppermute | solution.py:200
  47.5 13.5 %collective-permute-start.14 = (bf16[4,128,256]{2,1,0:T(8,128)(2,1)}, bf16[4,128,256]{2,1,0:T(8,128)(2,1)S(1)}, u32[]{:S(2)}, u32[]{:S(2)}) collective-permute-start(bf16[4,128,256]{2,1,0:T(8,128)(2,1)} %get-tuple-element.46), channel_id=1, source_target_pairs={{0,2},{1,3},{2,0},{3,1},{4,6},{5,7},{6,4},{7,5},{8,10},{9,11},{10,... | collective-permute-start | bytes 786440 | tf_op jit(solution)/shard_map/ppermute | solution.py:200
  49.1 12.6 %collective-permute-start.9 = (bf16[256,256]{1,0:T(8,128)(2,1)}, bf16[256,256]{1,0:T(8,128)(2,1)S(1)}, u32[]{:S(2)}, u32[]{:S(2)}) collective-permute-start(bf16[256,256]{1,0:T(8,128)(2,1)} %get-tuple-element.55), channel_id=1, source_target_pairs={{4,0},{8,4},{12,8},{5,1},{9,5},{13,9},{6,2},{10,6},{14,10},{7,3},{... | collective-permute-start | bytes 393224 | tf_op jit(solution)/shard_map/ppermute | solution.py:243
  54.8 11.7 %collective-permute-start.15 = (bf16[4,256,128]{2,1,0:T(8,128)(2,1)}, bf16[4,256,128]{2,1,0:T(8,128)(2,1)S(1)}, u32[]{:S(2)}, u32[]{:S(2)}) collective-permute-start(bf16[4,256,128]{2,1,0:T(8,128)(2,1)} %get-tuple-element.44), channel_id=1, source_target_pairs={{0,2},{1,3},{2,0},{3,1},{4,6},{5,7},{6,4},{7,5},{8,10},{9,11},{10,... | collective-permute-start | bytes 786440 | tf_op jit(solution)/shard_map/ppermute | solution.py:200
  61.0 10.7 %collective-permute-start.16 = (bf16[4,128,256]{2,1,0:T(8,128)(2,1)}, bf16[4,128,256]{2,1,0:T(8,128)(2,1)S(1)}, u32[]{:S(2)}, u32[]{:S(2)}) collective-permute-start(bf16[4,128,256]{2,1,0:T(8,128)(2,1)} %get-tuple-element.45), channel_id=1, source_target_pairs={{0,3},{1,2},{2,1},{3,0},{4,7},{5,6},{6,5},{7,4},{8,11},{9,10},{10,... | collective-permute-start | bytes 786440 | tf_op jit(solution)/shard_map/ppermute | solution.py:200
  61.7 15.6 %collective-permute-start.17 = (bf16[4,256,128]{2,1,0:T(8,128)(2,1)}, bf16[4,256,128]{2,1,0:T(8,128)(2,1)S(1)}, u32[]{:S(2)}, u32[]{:S(2)}) collective-permute-start(bf16[4,256,128]{2,1,0:T(8,128)(2,1)} %get-tuple-element.43), channel_id=1, source_target_pairs={{0,3},{1,2},{2,1},{3,0},{4,7},{5,6},{6,5},{7,4},{8,11},{9,10},{10,... | collective-permute-start | bytes 786440 | tf_op jit(solution)/shard_map/ppermute | solution.py:200
  66.6 31.3 %collective-permute-start.13 = (bf16[3,256,128]{2,1,0:T(8,128)(2,1)}, bf16[3,256,128]{2,1,0:T(8,128)(2,1)S(1)}, u32[]{:S(2)}, u32[]{:S(2)}) collective-permute-start(bf16[3,256,128]{2,1,0:T(8,128)(2,1)} %get-tuple-element.47), channel_id=1, source_target_pairs={{0,3},{1,2},{2,1},{3,0},{4,7},{5,6},{6,5},{7,4},{8,11},{9,10},{10,... | collective-permute-start | bytes 589832 | tf_op jit(solution)/shard_map/ppermute | solution.py:200
  71.7 28.7 %collective-permute-start.3 = (bf16[2,128,256]{2,1,0:T(8,128)(2,1)}, bf16[2,128,256]{2,1,0:T(8,128)(2,1)S(1)}, u32[]{:S(2)}, u32[]{:S(2)}) collective-permute-start(bf16[2,128,256]{2,1,0:T(8,128)(2,1)} %get-tuple-element.54), channel_id=1, source_target_pairs={{0,2},{1,3},{2,0},{3,1},{4,6},{5,7},{6,4},{7,5},{8,10},{9,11},{10,... | collective-permute-start | bytes 393224 | tf_op jit(solution)/shard_map/ppermute | solution.py:200
  77.3 23.1 %collective-permute-start.4 = (bf16[2,256,128]{2,1,0:T(8,128)(2,1)}, bf16[2,256,128]{2,1,0:T(8,128)(2,1)S(1)}, u32[]{:S(2)}, u32[]{:S(2)}) collective-permute-start(bf16[2,256,128]{2,1,0:T(8,128)(2,1)} %get-tuple-element.52), channel_id=1, source_target_pairs={{0,2},{1,3},{2,0},{3,1},{4,6},{5,7},{6,4},{7,5},{8,10},{9,11},{10,... | collective-permute-start | bytes 393224 | tf_op jit(solution)/shard_map/ppermute | solution.py:200
  79.7 20.7 %collective-permute-start.5 = (bf16[2,128,256]{2,1,0:T(8,128)(2,1)}, bf16[2,128,256]{2,1,0:T(8,128)(2,1)S(1)}, u32[]{:S(2)}, u32[]{:S(2)}) collective-permute-start(bf16[2,128,256]{2,1,0:T(8,128)(2,1)} %get-tuple-element.53), channel_id=1, source_target_pairs={{0,3},{1,2},{2,1},{3,0},{4,7},{5,6},{6,5},{7,4},{8,11},{9,10},{10,... | collective-permute-start | bytes 393224 | tf_op jit(solution)/shard_map/ppermute | solution.py:200
  81.1 19.3 %collective-permute-start.6 = (bf16[2,256,128]{2,1,0:T(8,128)(2,1)}, bf16[2,256,128]{2,1,0:T(8,128)(2,1)S(1)}, u32[]{:S(2)}, u32[]{:S(2)}) collective-permute-start(bf16[2,256,128]{2,1,0:T(8,128)(2,1)} %get-tuple-element.51), channel_id=1, source_target_pairs={{0,3},{1,2},{2,1},{3,0},{4,7},{5,6},{6,5},{7,4},{8,11},{9,10},{10,... | collective-permute-start | bytes 393224 | tf_op jit(solution)/shard_map/ppermute | solution.py:200
  109.6 9.9 %collective-permute-start.32 = (f32[4,8,128]{2,1,0:T(8,128)}, f32[4,8,128]{2,1,0:T(8,128)}, u32[]{:S(2)}, u32[]{:S(2)}) collective-permute-start(f32[4,8,128]{2,1,0:T(8,128)} %get-tuple-element.64), channel_id=1, source_target_pairs={{0,4},{4,8},{8,12},{12,0},{1,5},{5,9},{9,13},{13,1},{2,6},{6,10},{... | collective-permute-start | bytes 49160 | tf_op jit(solution)/shard_map/ppermute | solution.py:321
  110.6 23.9 %collective-permute-start.25 = (f32[256,256]{1,0:T(8,128)}, f32[256,256]{1,0:T(8,128)}, u32[]{:S(2)}, u32[]{:S(2)}) collective-permute-start(f32[256,256]{1,0:T(8,128)} %get-tuple-element.31.b0), channel_id=1, source_target_pairs={{0,4},{4,8},{8,12},{1,5},{5,9},{9,13},{2,6},{6,10},{10,14},{3,7},{... | collective-permute-start | bytes 786440 | tf_op jit(solution)/shard_map/ppermute | solution.py:312
  114.8 19.8 %collective-permute-start.26 = (f32[256,256]{1,0:T(8,128)}, f32[256,256]{1,0:T(8,128)}, u32[]{:S(2)}, u32[]{:S(2)}) collective-permute-start(f32[256,256]{1,0:T(8,128)} %get-tuple-element.31.b0), channel_id=1, source_target_pairs={{4,0},{8,4},{12,8},{5,1},{9,5},{13,9},{6,2},{10,6},{14,10},{7,3},{... | collective-permute-start | bytes 786440 | tf_op jit(solution)/shard_map/ppermute | solution.py:313
  116.0 18.6 %collective-permute-start.27 = (f32[256,256]{1,0:T(8,128)}, f32[256,256]{1,0:T(8,128)}, u32[]{:S(2)}, u32[]{:S(2)}) collective-permute-start(f32[256,256]{1,0:T(8,128)} %get-tuple-element.31.b0), channel_id=1, source_target_pairs={{0,1},{1,2},{2,3},{4,5},{5,6},{6,7},{8,9},{9,10},{10,11},{12,13},{... | collective-permute-start | bytes 786440 | tf_op jit(solution)/shard_map/ppermute | solution.py:314
  118.2 16.4 %collective-permute-start.28 = (f32[256,256]{1,0:T(8,128)}, f32[256,256]{1,0:T(8,128)}, u32[]{:S(2)}, u32[]{:S(2)}) collective-permute-start(f32[256,256]{1,0:T(8,128)} %get-tuple-element.31.b0), channel_id=1, source_target_pairs={{1,0},{2,1},{3,2},{5,4},{6,5},{7,6},{9,8},{10,9},{11,10},{13,12},{... | collective-permute-start | bytes 786440 | tf_op jit(solution)/shard_map/ppermute | solution.py:315
  119.5 5.1 %collective-permute-start.33 = (f32[4,8,128]{2,1,0:T(8,128)}, f32[4,8,128]{2,1,0:T(8,128)}, u32[]{:S(2)}, u32[]{:S(2)}) collective-permute-start(f32[4,8,128]{2,1,0:T(8,128)} %get-tuple-element.64), channel_id=1, source_target_pairs={{0,8},{4,12},{8,0},{12,4},{1,9},{5,13},{9,1},{13,5},{2,10},{6,14},... | collective-permute-start | bytes 49160 | tf_op jit(solution)/shard_map/ppermute | solution.py:321
  124.7 5.4 %collective-permute-start.34 = (f32[4,8,128]{2,1,0:T(8,128)}, f32[4,8,128]{2,1,0:T(8,128)S(1)}, u32[]{:S(2)}, u32[]{:S(2)}) collective-permute-start(f32[4,8,128]{2,1,0:T(8,128)} %get-tuple-element.64), channel_id=1, source_target_pairs={{0,12},{4,0},{8,4},{12,8},{1,13},{5,1},{9,5},{13,9},{2,14},{6,2},{... | collective-permute-start | bytes 49160 | tf_op jit(solution)/shard_map/ppermute | solution.py:321
  130.0 19.9 %collective-permute-start.23 = (bf16[128,256]{1,0:T(8,128)(2,1)S(1)}, bf16[128,256]{1,0:T(8,128)(2,1)S(1)}, u32[]{:S(2)}, u32[]{:S(2)}) collective-permute-start(bf16[128,256]{1,0:T(8,128)(2,1)S(1)} %get-tuple-element.62), channel_id=1, source_target_pairs={{0,2},{1,3},{2,0},{3,1},{4,6},{5,7},{6,4},{7,5},{8,10},{9,11},{10,... | collective-permute-start | bytes 196616 | tf_op jit(solution)/shard_map/ppermute | solution.py:200
  134.5 15.5 %collective-permute-start.24 = (bf16[128,256]{1,0:T(8,128)(2,1)S(1)}, bf16[128,256]{1,0:T(8,128)(2,1)S(1)}, u32[]{:S(2)}, u32[]{:S(2)}) collective-permute-start(bf16[128,256]{1,0:T(8,128)(2,1)S(1)} %get-tuple-element.62), channel_id=1, source_target_pairs={{0,3},{1,2},{2,1},{3,0},{4,7},{5,6},{6,5},{7,4},{8,11},{9,10},{10,... | collective-permute-start | bytes 196616 | tf_op jit(solution)/shard_map/ppermute | solution.py:200
  134.5 15.2 %collective-permute-start.22 = (bf16[128,256]{1,0:T(8,128)(2,1)S(1)}, bf16[128,256]{1,0:T(8,128)(2,1)S(1)}, u32[]{:S(2)}, u32[]{:S(2)}) collective-permute-start(bf16[128,256]{1,0:T(8,128)(2,1)S(1)} %bitcast.85), channel_id=1, source_target_pairs={{0,1},{1,0},{2,3},{3,2},{4,5},{5,4},{6,7},{7,6},{8,9},{9,8},{10,11... | collective-permute-start | bytes 196616 | tf_op jit(solution)/shard_map/ppermute | solution.py:200
  (34 other events, 316.4 us)

commit v2 on v0

--- a/solution.py
+++ b/solution.py
@@ -1,7 +1,14 @@
+import functools
+
 import jax
 import jax.numpy as jnp
 from jax import lax
+from jax.experimental import pallas as pl
+from jax.experimental.pallas import tpu as pltpu
 from jax.sharding import PartitionSpec as P
+
+CUTS = (0, 4, 8, 11, 13)
+EPS = 1e-06
 
 
 def padded(cells, sides, width):
@@ -21,7 +28,7 @@
     return cells
 
 
-def on_device(psi, sector_size, left_env, right_env, term_shift):
+def on_device_gather(psi, sector_size, left_env, right_env, term_shift):
     slots = psi.shape[1]
     rows_here = psi.shape[2]
     width = psi.shape[3]
@@ -66,10 +73,10 @@
     product, squares = lax.psum(
         (jnp.sum(trial * image_one), jnp.sum(trial * trial)), ("sector", "contr")
     )
-    ritz_value = product / (squares + 1e-06)
+    ritz_value = product / (squares + EPS)
     resid = image_one - ritz_value * trial
     total_sq = lax.psum(jnp.sum(resid * resid), ("sector", "contr"))
-    factor = lax.rsqrt(total_sq / entries + 1e-06)
+    factor = lax.rsqrt(total_sq / entries + EPS)
     second = (resid * factor).astype(jnp.bfloat16)
     image_two = apply_h(second)
     return (
@@ -79,9 +86,403 @@
     )
 
 
+def live_block(shape, start, live):
+    rows = (lax.broadcasted_iota(jnp.int32, shape, 0) + start) % shape[0]
+    cols = lax.broadcasted_iota(jnp.int32, shape, 1)
+    return (rows < live) & (cols < live)
+
+
+def fetch(pairs, sems):
+    copies = [pltpu.make_async_copy(x, y, sems.at[n]) for n, (x, y) in enumerate(pairs)]
+    for copy in copies:
+        copy.start()
+    done = [0]
+
+    def until(count):
+        for copy in copies[done[0] : count]:
+            copy.wait()
+        done[0] = max(done[0], count)
+
+    return until
+
+
+def pack_kernel(parts, info, left_env, right_env, *refs):
+    count = len(parts)
+    refs = refs[-2 * count - 2 :]
+    outs, bufs, (ins_sem, outs_sem) = refs[:count], refs[count : 2 * count], refs[-2:]
+    half = right_env.shape[-1]
+    width = right_env.shape[-2]
+    copies = []
+    for (start, stop, flip), buf in zip(parts, bufs):
+        slot = info[2] ^ flip
+        span = pl.ds(start, stop - start)
+        pieces = [(right_env.at[span, 0, slot], buf.at[:, pl.ds(0, width)])]
+        for lane in range(width // half):
+            pieces.append(
+                (
+                    left_env.at[span, 0, slot, :, pl.ds(lane * half, half)],
+                    buf.at[:, pl.ds(width + lane * half, half)],
+                )
+            )
+        copies.append(pieces)
+    flat = [pair for pieces in copies for pair in pieces]
+    until = fetch(flat, ins_sem)
+    sends = [pltpu.make_async_copy(b, o, outs_sem.at[n]) for n, (b, o) in enumerate(zip(bufs, outs))]
+    each = len(copies[0])
+    for n, send in enumerate(sends):
+        until(each * (n + 1))
+        send.start()
+    for send in sends:
+        send.wait()
+
+
+def pack(parts, info, left_env, right_env, after=()):
+    width, half = right_env.shape[-2:]
+    shapes = [(stop - start, 2 * width, half) for start, stop, _ in parts]
+    out_shape = [jax.ShapeDtypeStruct(shape, jnp.bfloat16) for shape in shapes]
+    size = sum(shape[0] for shape in shapes) * width * half * 8
+    return pl.pallas_call(
+        functools.partial(pack_kernel, parts),
+        in_specs=[pl.BlockSpec(memory_space=pltpu.SMEM)]
+        + [pl.BlockSpec(memory_space=pl.ANY)] * (2 + len(after)),
+        out_specs=[pl.BlockSpec(memory_space=pl.ANY)] * len(parts),
+        out_shape=out_shape,
+        scratch_shapes=[pltpu.VMEM(shape, jnp.bfloat16) for shape in shapes]
+        + [
+            pltpu.SemaphoreType.DMA((len(parts) * (1 + width // half),)),
+            pltpu.SemaphoreType.DMA((len(parts),)),
+        ],
+        compiler_params=pltpu.CompilerParams(vmem_limit_bytes=63 * 2**20),
+        cost_estimate=pl.CostEstimate(flops=0, bytes_accessed=size, transcendentals=0),
+        name=f"pack_{parts[0][0]}_{len(parts)}",
+    )(info, left_env, right_env, *after)
+
+
+def inner_block(source, near, far):
+    half = near.shape[1]
+    left = [
+        jnp.concatenate([m[2 * half + k * half : 3 * half + k * half] for k in range(2)], axis=1)
+        for m in (near, far)
+    ]
+    return lax.dot_general(
+        source,
+        jnp.concatenate(left, axis=0),
+        (((1,), (1,)), ((), ())),
+        preferred_element_type=jnp.float32,
+    ).astype(jnp.bfloat16)
+
+
+def add_terms(items, source, kept, group):
+    width = source.shape[-1]
+    half = width // 2
+    total = None
+    groups = [items[at : at + group] for at in range(0, len(items), group)]
+
+    def inners(index):
+        for k, (shift, near, far, i, j) in enumerate(groups[index]):
+            kept[index % 2, k * width : (k + 1) * width, :] = inner_block(
+                source[shift], near[i], far[j]
+            )
+
+    inners(0)
+    for index, batch in enumerate(groups):
+        if index + 1 < len(groups):
+            inners(index + 1)
+        right = jnp.concatenate(
+            [m[n, :width] for _, near, far, i, j in batch for m, n in ((near, i), (far, j))], axis=1
+        )
+        part = jnp.dot(
+            right,
+            kept[index % 2, : len(batch) * width, :],
+            preferred_element_type=jnp.float32,
+        )
+        total = part if total is None else total + part
+    return total
+
+
+def own_first(block, across):
+    half = block.shape[0] // 2
+    turned = jnp.concatenate([block[half:], block[:half]], axis=0)
+    turned = jnp.concatenate([turned[:, half:], turned[:, :half]], axis=1)
+    return jnp.where(across == 0, block, turned)
+
+
+def first_kernel(start, stop, last, info, *refs):
+    count = 6 if start else 5
+    here, refs = refs[:count], refs[count:]
+    outs, (sems, kept, *bufs) = refs[: 4 if last else 1], refs[4 if last else 1 :]
+    own, core, side, diag, source = bufs[:5]
+    terms = here[0].shape[0]
+    span = pl.ds(start, stop - start)
+    until = fetch(
+        [
+            (here[4], source),
+            (here[0].at[span], own),
+            (here[2], side),
+            (here[1].at[span], core),
+            (here[3], diag),
+        ]
+        + list(zip(here[5:], bufs[5:])),
+        sems,
+    )
+    until(count)
+    items = []
+    for n in range(stop - start):
+        items.append((info[4 + start + n], own, side, n, n))
+        items.append((info[4 + terms + start + n], core, diag, n, n))
+    total = add_terms(items, source, kept, 2)
+    if start:
+        total = total + bufs[5][...]
+    if not last:
+        outs[0][...] = total
+        return
+    image, mine, theirs, stats = outs
+    half = mine.shape[0]
+    field = source[0].astype(jnp.float32)
+    live = live_block(field.shape, info[0] * half, info[1])
+    block = jnp.where(live, own_first(total, info[0]), 0.0)
+    image[...] = block
+    mine[...] = block[:half].astype(jnp.bfloat16)
+    theirs[...] = block[half:].astype(jnp.bfloat16)
+    product = jnp.sum(field * block, keepdims=True)
+    squares = jnp.sum(field * field, keepdims=True)
+    quotient = product / (squares + EPS)
+    resid = block - quotient * field
+    rest = jnp.sum(resid * resid, keepdims=True)
+    for row, value in enumerate((product, squares, rest, quotient)):
+        stats[row] = jnp.broadcast_to(value, stats.shape[1:])
+
+
+def merged(*stats):
+    product = sum(t[0] for t in stats)
+    squares = sum(t[1] for t in stats)
+    quotient = product / (squares + EPS)
+    rest = 0.0
+    for t in stats:
+        off = t[3] - quotient
+        rest += t[2] + 2.0 * off * (t[0] - t[3] * t[1]) + off * off * t[1]
+    return product, squares, rest, quotient
+
+
+def second_kernel(entries, spans, info, *refs):
+    count = 12 + 2 * len(spans)
+    here, refs = refs[:count], refs[count:]
+    (mine, theirs, ritz), (sems, second, kept), bufs = refs[:3], refs[3:6], refs[6:]
+    stats_a, stats_b, source, *blocks = bufs[:8]
+    own, core = bufs[10:12]
+    pairs = list(zip(here[:8], bufs[:8]))
+    before = len(pairs)
+    for n, (start, stop) in enumerate(spans):
+        span = pl.ds(start, stop - start)
+        pairs += [
+            (here[10].at[span], own.at[span]),
+            (here[11].at[span], core.at[span]),
+            (here[12 + 2 * n], bufs[12 + 2 * n]),
+            (here[13 + 2 * n], bufs[13 + 2 * n]),
+        ]
+    pairs += [(here[8], mine.at[0]), (here[9], theirs.at[0])]
+    until = fetch(pairs, sems)
+    terms = own.shape[0]
+    across, parity = info[0], info[2] % 2
+    half = mine.shape[1]
+    until(before)
+    _, _, rest, quotient = merged(stats_a[...], stats_b[...])
+    factor = lax.rsqrt(rest / entries + EPS)
+    ritz[...] = quotient
+    factor, quotient = factor[:1, :1], quotient[:1, :1]
+    for place, block, turned in zip((0, 1, 2, 4 - parity, 3 + parity), blocks, (0, 0, 0, 0, 1)):
+        image = block[...]
+        if turned:
+            image = jnp.concatenate([image[half:], image[:half]], axis=0)
+        resid = image - quotient * source[place].astype(jnp.float32)
+        second[place] = (resid * factor).astype(jnp.bfloat16)
+
+    total = None
+    for n, (start, stop) in enumerate(spans):
+        until(before + 4 * (n + 1))
+        items = []
+        for w in range(start, stop):
+            items.append((info[4 + w], own, bufs[12 + 2 * n], w, w - start))
+            items.append((info[4 + terms + w], core, bufs[13 + 2 * n], w, w - start))
+        part = add_terms(items, second, kept, 2)
+        total = part if total is None else total + part
+    total = own_first(total, across)
+    live = live_block(total.shape, across * half, info[1])
+    block = jnp.where(live, total, 0.0).astype(jnp.bfloat16)
+    mine[1] = block[:half]
+    theirs[1] = block[half:]
+    until(len(pairs))
+
+
+def whole_call(body, operands, out_shape, scratch, info, flops, name):
+    space = pl.BlockSpec(memory_space=pltpu.VMEM)
+    return pl.pallas_call(
+        body,
+        in_specs=[pl.BlockSpec(memory_space=pltpu.SMEM)]
+        + [pl.BlockSpec(memory_space=pl.ANY)] * len(operands),
+        out_specs=[space] * len(out_shape),
+        out_shape=out_shape,
+        scratch_shapes=scratch,
+        compiler_params=pltpu.CompilerParams(vmem_limit_bytes=63 * 2**20),
+        cost_estimate=pl.CostEstimate(flops=flops, bytes_accessed=flops // 256, transcendentals=0),
+        name=name,
+    )(info, *operands)
+
+
+def room(array, count=None):
+    return pltpu.VMEM((count or array.shape[0],) + array.shape[1:], array.dtype)
+
+
+def on_device(psi, sector_size, left_env, right_env, term_shift):
+    terms, _, slots, half, width = left_env.shape
+    cell = ("contr", "mpo")
+    across, core = lax.axis_index("contr"), lax.axis_index("mpo")
+    me = across * 2 + core
+    sectors = lax.axis_size("sector")
+    cuts = [terms * part // CUTS[-1] for part in CUTS]
+    spans = list(zip(cuts[:-1], cuts[1:]))
+
+    def swap(array, flip):
+        return lax.ppermute(array, cell, [(i, i ^ flip) for i in range(slots)])
+
+    quarter = half // 2
+    part = lax.dynamic_slice(
+        psi[0], (1 - across, core * quarter, 0), (slots - 1, quarter, width)
+    )
+    part = swap(part, 2)
+    shift_core = swap(term_shift, 1)
+    size_here = lax.dynamic_index_in_dim(sector_size[0], me, 0, keepdims=False)
+    info = jnp.concatenate(
+        [jnp.stack([across, size_here, me, jnp.int32(0)]), term_shift, shift_core]
+    )
+    start, stop = spans[0]
+    head = pack([(start, stop, 2), (start, stop, 3)], info, left_env, right_env)
+    rest = [(start, stop, flip) for start, stop in spans[1:] for flip in (2, 3)]
+    *tail, to_core, own_env = pack(
+        rest + [(0, terms, 1), (0, terms, 0)], info, left_env, right_env, head
+    )
+    messages = [swap(m, 2 + i % 2) for i, m in enumerate([*head, *tail])]
+    core_env = swap(to_core, 1)
+
+    psi_mine = lax.dynamic_slice_in_dim(psi[0], across, slots - 1, axis=0)
+    part_core = swap(part, 1)
+    whole = jnp.concatenate(
+        [
+            psi_mine,
+            jnp.where(core == 0, part, part_core),
+            jnp.where(core == 0, part_core, part),
+        ],
+        axis=1,
+    )
+    sizes = lax.dynamic_slice_in_dim(sector_size[0], across, slots - 1, axis=0)[:, None, None]
+    ids = lax.iota(jnp.int32, width)
+    row_ids = (ids + across * half) % width
+    live = (row_ids[None, :, None] < sizes) & (ids[None, None, :] < sizes)
+    whole = jnp.where(live, whole, jnp.zeros_like(whole))
+    blank = jnp.zeros_like(whole[:1])
+    framed = jnp.concatenate([blank, whole, blank], axis=0)
+    own = lax.dynamic_index_in_dim(whole, core, 0, keepdims=False)
+    own = jnp.where(across == 0, own, lax.dynamic_index_in_dim(whole, core + 1, 0, keepdims=False))
+    up = [(i, i + 1) for i in range(sectors - 1)]
+    down = [(i + 1, i) for i in range(sectors - 1)]
+    source = jnp.stack(
+        [
+            own,
+            lax.ppermute(own, "sector", up),
+            lax.ppermute(own, "sector", down),
+            lax.dynamic_index_in_dim(framed, me - across, 0, keepdims=False),
+            lax.dynamic_index_in_dim(framed, me - across + 2, 0, keepdims=False),
+        ]
+    )
+
+    plain = jax.ShapeDtypeStruct((width, width), jnp.float32)
+    rows = jax.ShapeDtypeStruct((half, width), jnp.bfloat16)
+    tile = jax.ShapeDtypeStruct((4, 8, 128), jnp.float32)
+    kept = pltpu.VMEM((2, 2 * width, width), jnp.bfloat16)
+    total = []
+    for index, (start, stop) in enumerate(spans):
+        last = stop == terms
+        size = stop - start
+        operands = [own_env, core_env, *messages[2 * index : 2 * index + 2], source, *total]
+        total = whole_call(
+            functools.partial(first_kernel, start, stop, last),
+            operands,
+            [plain, rows, rows, tile] if last else [plain],
+            [pltpu.SemaphoreType.DMA((len(operands),)), kept]
+            + [room(m, size) for m in operands[:4]]
+            + [room(m) for m in operands[4:]],
+            info,
+            8 * size * width**3,
+            f"first_terms_{start}",
+        )
+    image_one, mine_one, theirs_one, stats = total
+
+    middle = [(1, 2), (2, 1)]
+    blocks = [
+        image_one,
+        lax.ppermute(image_one, "sector", up),
+        lax.ppermute(image_one, "sector", down),
+        swap(image_one, 1),
+        lax.ppermute(image_one, cell, middle),
+    ]
+    stats = jnp.stack(merged(stats, swap(stats, 1), swap(stats, 2), swap(stats, 3)))
+    flip = 1
+    while flip < sectors:
+        pair = lax.ppermute(stats, "sector", [(i, i ^ flip) for i in range(sectors)])
+        flip *= 2
+        if flip < sectors:
+            stats = jnp.stack(merged(stats, pair))
+
+    operands = [stats, pair, source, *blocks, mine_one, theirs_one, own_env, core_env, *messages]
+    mine, theirs, ritz = whole_call(
+        functools.partial(second_kernel, float(sectors * slots * width * width), spans),
+        operands,
+        [
+            jax.ShapeDtypeStruct((2, half, width), jnp.bfloat16),
+            jax.ShapeDtypeStruct((2, half, width), jnp.bfloat16),
+            jax.ShapeDtypeStruct((8, 128), jnp.float32),
+        ],
+        [
+            pltpu.SemaphoreType.DMA((10 + 4 * len(spans),)),
+            pltpu.VMEM((5, width, width), jnp.bfloat16),
+            kept,
+        ]
+        + [room(m) for m in operands],
+        info,
+        8 * terms * width**3,
+        "second_terms",
+    )
+
+    got = [mine, swap(mine, 1), swap(theirs, 2)]
+    got.append(swap(got[2], 1))
+    flips = [me ^ v for v in range(slots)]
+    images = [
+        jnp.stack(
+            [
+                jnp.where(
+                    f < 2,
+                    jnp.where(f == 0, got[0][n], got[1][n]),
+                    jnp.where(f == 2, got[2][n], got[3][n]),
+                )
+                for f in flips
+            ]
+        )[None]
+        for n in range(2)
+    ]
+    return images[0], images[1], ritz[0, :1]
+
+
 def solution(mesh):
+    sectors = mesh.shape["sector"]
+    fits = mesh.shape["contr"] == 2 and mesh.shape["mpo"] == 2
+    fits = fits and sectors > 1 and sectors & (sectors - 1) == 0
+
+    def body(psi, sector_size, left_env, right_env, term_shift):
+        run = on_device if fits and psi.shape[1] == 4 else on_device_gather
+        return run(psi, sector_size, left_env, right_env, term_shift)
+
     return jax.shard_map(
-        on_device,
+        body,
         mesh=mesh,
         in_specs=(
             P(("groups", "sector"), None, "contr", None),

time: 260 us -> 138 us (0.53)
  waiting for transfers between devices: 141 us -> 65.2 us
  blocking collectives: 46.1 us -> 0 us
  Pallas kernels: 0 us -> 32.2 us
  starting transfers between devices: 9.59 us -> 27.1 us
  between operations: 17 us -> 0.94 us
  matrix products: 15.5 us -> 0 us
  local copies, waits for them, and re-layouts: 20 us -> 7.12 us
  other arithmetic: 10.1 us -> 4.74 us
    all_gather x1 -> x0, waiting for transfers between devices: 67 us -> none  [apply_h(): lax.all_gather(left_env, 'contr', axis=3, tiled=True)[:, 0]]
    ppermute x4 -> x26, waiting for transfers between devices: 11.6 us -> 65.2 us  [the longest x19 54.9 us: swap(): return lax.ppermute(array, cell, [(i, i ^ flip) for i in range(slots)])]
    psum x3 -> x0, blocking collectives: 46.1 us -> none  [the longest x1 22.2 us: on_device(): lax.psum((jnp.sum(trial * image_one), jnp.sum(trial * trial)), ('sector',...]
    reduce_scatter x2 -> x0, waiting for transfers between devices: 40.7 us -> none  [apply_h(): lax.psum_scatter(partial_sum, 'contr', scatter_dimension=1, tiled=True)]
    pallas_call x0 -> x7, Pallas kernels: none -> 32.2 us  [the longest x5 23.6 us: whole_call(): pl.pallas_call(body, in_specs=[pl.BlockSpec(memory_space=pltpu.SMEM)] + [...]
    psum x1 -> x0, waiting for transfers between devices: 21.2 us -> none  [apply_h(): summed = lax.psum(summed, 'mpo')]
    ppermute x4 -> x26, starting transfers between devices: 9.44 us -> 27.1 us  [the longest x19 10.6 us: swap(): return lax.ppermute(array, cell, [(i, i ^ flip) for i in range(slots)])]
    dot_general x2 -> x0, matrix products: 15.5 us -> none  [apply_h(): jnp.einsum('wvpr,wvrm->vpm', right_env[:, 0], inner, preferred_element_ty...]
  transfers between devices with their start and end apart: 8 -> 26, of which waited for: 7 -> 15; matrix products, arithmetic and copies ran while one was open for 5% -> 4% of each run, Pallas kernels for 0% -> 15%
where the time goes in v2:
time: 138 us; the launch traced here: 137 us
  waiting for transfers between devices  65.2 us (47%)
  Pallas kernels  32.2 us (23%)
  starting transfers between devices  27.1 us (20%)
  local copies, waits for them, and re-layouts  7.12 us (5%)
  other arithmetic  4.74 us (3%)
    ppermute x19, waiting for transfers between devices, swap(): return lax.ppermute(array, cell, [(i, i ^ flip) for i in range(slots)])  54.9 us
    pallas_call x5, Pallas kernels, whole_call(): pl.pallas_call(body, in_specs=[pl.BlockSpec(memory_space=pltpu.SMEM)] + [...  23.6 us
    ppermute x19, starting transfers between devices, swap(): return lax.ppermute(array, cell, [(i, i ^ flip) for i in range(slots)])  10.6 us
    pallas_call x2, Pallas kernels, pack(): pl.pallas_call(functools.partial(pack_kernel, parts), in_specs=[pl.BlockS...  8.62 us
    ppermute x2, starting transfers between devices, on_device(): lax.ppermute(stats, 'sector', [(i, i ^ flip) for i in range(sectors)])  6.75 us
    ppermute x2, waiting for transfers between devices, on_device(): lax.ppermute(stats, 'sector', [(i, i ^ flip) for i in range(sectors)])  5.06 us
    ppermute x1, starting transfers between devices, on_device(): lax.ppermute(own, 'sector', up)  3.49 us
    ppermute x1, waiting for transfers between devices, on_device(): lax.ppermute(own, 'sector', down)  3.48 us
  transfers between devices with their start and end apart: 26, of which 15 were waited for; matrix products, arithmetic and copies ran while one was open for 4% of the time, Pallas kernels for 15%

profile of v2, /device:TPU:0, one launch (start us, length us, event | category | flops | bytes accessed | tf_op | source)
XLA Modules:
  0.0 137.3 jit_solution(17849217916825565170)
XLA Ops:
  1.6 3.0 %collective-permute-start.4 = (bf16[3,64,256]{2,1,0:T(8,128)(2,1)S(1)}, bf16[3,64,256]{2,1,0:T(8,128)(2,1)S(1)}, u32[]{:S(2)}, u32[]{:S(2)}) collective-permute-start(bf16[3,64,256]{2,1,0:T(8,128)(2,1)S(1)} %dynamic-slice_bitcast_fusion.1), channel_id=1, source_target_pairs={{0,2},{1,3},{2,0},{3,1},{4,6},{5,7},{6,4},{7,5},{8,10},{9,11},{10,... | collective-permute-start | bytes 294920 | tf_op jit(solution)/shard_map/ppermute | solution.py:346
  4.6 1.2 constant_dynamic-slice_fusion.1
  5.9 1.9 %concatenate.9.info = s32[30]{0:T(128)} concatenate(s32[1]{0:T(128)} %bitcast, s32[1]{0:T(128)} %bitcast.1, s32[1]{0:T(128)} %bitcast.2, s32[1]{0:T(128)} %constant.56.clone.1, s32[13]{0:T(128)} %param.9, s32[13]{0:T(128)S(1)} %collective-permute-done), dimensions={0} | concatenate | bytes 240 | tf_op jit(solution)/shard_map/concatenate | solution.py:355
  7.8 2.8 %pack_0_2.1 = (bf16[4,512,128]{2,1,0:T(8,128)(2,1)}, bf16[4,512,128]{2,1,0:T(8,128)(2,1)}) custom-call(s32[30]{0:T(128)} %concatenate.9.info, bf16[13,1,4,128,256]{4,3,2,1,0:T(8,128)(2,1)} %left_env.3, bf16[13,1,4,256,128]{4,3,2,1,0:T(8,128)(2,1)} %right_env.3), custom_call_target="tpu_custom_call" | custom-call | bytes 2097152 | tf_op jit(solution)/shard_map/pack_0_2/pallas_call | solution.py:144
  10.6 5.8 %pack_4_8.1 = (bf16[4,512,128]{2,1,0:T(8,128)(2,1)}, bf16[4,512,128]{2,1,0:T(8,128)(2,1)}, bf16[3,512,128]{2,1,0:T(8,128)(2,1)}, bf16[3,512,128]{2,1,0:T(8,128)(...) custom-call(s32[30]{0:T(128)} %concatenate.9.info, ...), custom_call_target="tpu_custom_call" | custom-call | bytes 11534336 | tf_op jit(solution)/shard_map/pack_4_8/pallas_call | solution.py:144
  17.3 1.7 %collective-permute-start.13 = (bf16[4,512,128]{2,1,0:T(8,128)(2,1)}, bf16[4,512,128]{2,1,0:T(8,128)(2,1)S(1)}, u32[]{:S(2)}, u32[]{:S(2)}) collective-permute-start(bf16[4,512,128]{2,1,0:T(8,128)(2,1)} %get-tuple-element.21.refs_1_), channel_id=1, source_target_pairs={{0,3},{1,2},{2,1},{3,0},{4,7},{5,6},{6,5},{7,4},{8,11},{9,10},{10,... | collective-permute-start | bytes 1572872 | tf_op jit(solution)/shard_map/ppermute | solution.py:346
  20.5 3.5 %collective-permute-start.6 = (bf16[256,256]{1,0:T(8,128)(2,1)S(1)}, bf16[256,256]{1,0:T(8,128)(2,1)S(1)}, u32[]{:S(2)}, u32[]{:S(2)}) collective-permute-start(bf16[256,256]{1,0:T(8,128)(2,1)S(1)} %get-tuple-element.51), channel_id=1, source_target_pairs={{0,4},{4,8},{8,12},{1,5},{5,9},{9,13},{2,6},{6,10},{10,14},{3,7},{... | collective-permute-start | bytes 393224 | tf_op jit(solution)/shard_map/ppermute | solution.py:391
  24.0 1.3 collective-permute-start.7
  25.3 1.7 %collective-permute-done.6 = bf16[256,256]{1,0:T(8,128)(2,1)S(1)} collective-permute-done((bf16[256,256]{1,0:T(8,128)(2,1)S(1)}, bf16[256,256]{1,0:T(8,128)(2,1)S(1)}, u32[]{:S(2)}, u32[]{:S(2)}) %collective-permute-start.6) | collective-permute-done | bytes 131104 | tf_op jit(solution)/shard_map/ppermute | solution.py:391
  27.7 3.5 %collective-permute-done.7 = bf16[256,256]{1,0:T(8,128)(2,1)S(1)} collective-permute-done((bf16[256,256]{1,0:T(8,128)(2,1)S(1)}, bf16[256,256]{1,0:T(8,128)(2,1)S(1)}, u32[]{:S(2)}, u32[]{:S(2)}) %collective-permute-start.7) | collective-permute-done | bytes 131104 | tf_op jit(solution)/shard_map/ppermute | solution.py:392
  32.4 10.2 %collective-permute-done.13.refs_3_.refs_13_ = bf16[4,512,128]{2,1,0:T(8,128)(2,1)S(1)} collective-permute-done((bf16[4,512,128]{2,1,0:T(8,128)(2,1)}, bf16[4,512,128]{2,1,0:T(8,128)(2,1)S(1)}, u32[]{:S(2)}, u32[]{:S(2)}) %collective-permute-start.13) | collective-permute-done | bytes 524320 | tf_op jit(solution)/shard_map/ppermute | solution.py:346
  43.0 11.6 %collective-permute-done.10.refs_2_.refs_14_ = bf16[4,512,128]{2,1,0:T(8,128)(2,1)S(1)} collective-permute-done((bf16[4,512,128]{2,1,0:T(8,128)(2,1)}, bf16[4,512,128]{2,1,0:T(8,128)(2,1)S(1)}, u32[]{:S(2)}, u32[]{:S(2)}) %collective-permute-start.10) | collective-permute-done | bytes 524320 | tf_op jit(solution)/shard_map/ppermute | solution.py:346
  56.3 4.2 %first_terms_0.1.refs_5_ = f32[256,256]{1,0:T(8,128)} custom-call(s32[30]{0:T(128)} %concatenate.9.info, bf16[13,512,128]{2,1,0:T(8,128)(2,1)} %get-tuple-element.22.refs_0_.refs_10_, bf16[13,512,128]{2,1,0:T(8,128)(2,1)} %collective-permute-done.1.refs_1_.refs_11_, bf16[4,512,128]{2,1,0:T(8,128)(2,1)} %copy-done.3, bf16[4,512,128]{2,1,0:T(8,128)(2,1)} %copy-done.4, ...), custom_call_target="tpu_custom_call" | custom-call | flops 536870912 | bytes 2097152 | tf_op jit(solution)/shard_map/first_terms_0/pallas_call | solution.py:319
  60.5 4.7 %collective-permute-done.11.refs_3_.refs_15_ = bf16[4,512,128]{2,1,0:T(8,128)(2,1)} collective-permute-done((bf16[4,512,128]{2,1,0:T(8,128)(2,1)}, bf16[4,512,128]{2,1,0:T(8,128)(2,1)}, u32[]{:S(2)}, u32[]{:S(2)}) %collective-permute-start.11) | collective-permute-done | bytes 524320 | tf_op jit(solution)/shard_map/ppermute | solution.py:346
  65.2 4.2 %first_terms_4.1.refs_5_ = f32[256,256]{1,0:T(8,128)} custom-call(s32[30]{0:T(128)} %concatenate.9.info, bf16[13,512,128]{2,1,0:T(8,128)(2,1)} %get-tuple-element.22.refs_0_.refs_10_, bf16[13,512,128]{2,1,0:T(8,128)(2,1)} %collective-permute-done.1.refs_1_.refs_11_, bf16[4,512,128]{2,1,0:T(8,128)(2,1)} %copy-done.2, ...), custom_call_target="tpu_custom_call" | custom-call | flops 536870912 | bytes 2097152 | tf_op jit(solution)/shard_map/first_terms_4/pallas_call | solution.py:319
  69.4 5.0 %collective-permute-done.8.refs_2_.refs_16_ = bf16[3,512,128]{2,1,0:T(8,128)(2,1)} collective-permute-done((bf16[3,512,128]{2,1,0:T(8,128)(2,1)}, bf16[3,512,128]{2,1,0:T(8,128)(2,1)}, u32[]{:S(2)}, u32[]{:S(2)}) %collective-permute-start.8) | collective-permute-done | bytes 393248 | tf_op jit(solution)/shard_map/ppermute | solution.py:346
  74.4 7.6 %collective-permute-done.9.refs_3_.refs_17_ = bf16[3,512,128]{2,1,0:T(8,128)(2,1)} collective-permute-done((bf16[3,512,128]{2,1,0:T(8,128)(2,1)}, bf16[3,512,128]{2,1,0:T(8,128)(2,1)}, u32[]{:S(2)}, u32[]{:S(2)}) %collective-permute-start.9) | collective-permute-done | bytes 393248 | tf_op jit(solution)/shard_map/ppermute | solution.py:346
  82.0 4.0 %first_terms_8.1.refs_5_ = f32[256,256]{1,0:T(8,128)} custom-call(s32[30]{0:T(128)} %concatenate.9.info, bf16[13,512,128]{2,1,0:T(8,128)(2,1)} %get-tuple-element.22.refs_0_.refs_10_, bf16[13,512,128]{2,1,0:T(8,128)(2,1)} %collective-permute-done.1.refs_1_.refs_11_, bf16[3,512,128]{2,1,0:T(8,128)(2,1)} %collective-permute-done.8.refs_2_.refs_16_, ...), custom_call_target="tpu_custom_call" | custom-call | flops 402653184 | bytes 1572864 | tf_op jit(solution)/shard_map/first_terms_8/pallas_call | solution.py:319
  86.1 2.4 %collective-permute-done.2.refs_2_.refs_18_ = bf16[2,512,128]{2,1,0:T(8,128)(2,1)} collective-permute-done((bf16[2,512,128]{2,1,0:T(8,128)(2,1)}, bf16[2,512,128]{2,1,0:T(8,128)(2,1)}, u32[]{:S(2)}, u32[]{:S(2)}) %collective-permute-start.2) | collective-permute-done | bytes 262176 | tf_op jit(solution)/shard_map/ppermute | solution.py:346
  88.5 4.8 %collective-permute-done.3.refs_3_.refs_19_ = bf16[2,512,128]{2,1,0:T(8,128)(2,1)} collective-permute-done((bf16[2,512,128]{2,1,0:T(8,128)(2,1)}, bf16[2,512,128]{2,1,0:T(8,128)(2,1)}, u32[]{:S(2)}, u32[]{:S(2)}) %collective-permute-start.3) | collective-permute-done | bytes 262176 | tf_op jit(solution)/shard_map/ppermute | solution.py:346
  93.3 3.9 %first_terms_11.1 = (f32[256,256]{1,0:T(8,128)}, bf16[128,256]{1,0:T(8,128)(2,1)}, bf16[128,256]{1,0:T(8,128)(2,1)}, f32[4,8,128]{2,1,0:T(8,128)}) custom-call(s32[30]{0:T(128)} %concatenate.9.info, bf16[13,512,128]{2,1,0:T(8,128)(2,1)} %get-tuple-element.22.refs_0_.refs_10_, bf16[13,512,128]{2,1,0:T(8,128)(2,1)} %collective-permute-done.1.refs_1_.refs_11_, ...), custom_call_target="tpu_custom_call" | custom-call | flops 268435456 | bytes 1048576 | tf_op jit(solution)/shard_map/first_terms_11/pallas_call | solution.py:319
  97.8 1.3 collective-permute-start.16
  99.1 2.3 %collective-permute-done.15 = f32[4,8,128]{2,1,0:T(8,128)S(1)} collective-permute-done((f32[4,8,128]{2,1,0:T(8,128)}, f32[4,8,128]{2,1,0:T(8,128)S(1)}, u32[]{:S(2)}, u32[]{:S(2)}) %collective-permute-start.15) | collective-permute-done | bytes 16416 | tf_op jit(solution)/shard_map/ppermute | solution.py:346
  102.2 1.8 %collective-permute-start.17 = (f32[4,8,128]{2,1,0:T(8,128)S(1)}, f32[4,8,128]{2,1,0:T(8,128)S(1)}, u32[]{:S(2)}, u32[]{:S(2)}) collective-permute-start(f32[4,8,128]{2,1,0:T(8,128)S(1)} %pad_maximum_fusion.1), channel_id=1, source_target_pairs={{0,4},{4,0},{8,12},{12,8},{1,5},{5,1},{9,13},{13,9},{2,6},{6,2},{1... | collective-permute-start | bytes 49160 | tf_op jit(solution)/shard_map/ppermute | solution.py:431
  104.0 2.2 %collective-permute-start.19 = (f32[256,256]{1,0:T(8,128)}, f32[256,256]{1,0:T(8,128)S(1)}, u32[]{:S(2)}, u32[]{:S(2)}) collective-permute-start(f32[256,256]{1,0:T(8,128)} %get-tuple-element.31.refs_3_), channel_id=1, source_target_pairs={{0,4},{4,8},{8,12},{1,5},{5,9},{9,13},{2,6},{6,10},{10,14},{3,7},{... | collective-permute-start | bytes 786440 | tf_op jit(solution)/shard_map/ppermute | solution.py:423
  106.2 1.3 collective-permute-start.20
  107.6 1.4 collective-permute-start.22
  109.0 5.0 %collective-permute-start.18 = (f32[4,8,128]{2,1,0:T(8,128)S(1)}, f32[4,8,128]{2,1,0:T(8,128)S(1)}, u32[]{:S(2)}, u32[]{:S(2)}) collective-permute-start(f32[4,8,128]{2,1,0:T(8,128)S(1)} %pad_maximum_fusion.2.refs_0_), channel_id=1, source_target_pairs={{0,8},{4,12},{8,0},{12,4},{1,9},{5,13},{9,1},{13,5},{2,10},{6,14},... | collective-permute-start | bytes 49160 | tf_op jit(solution)/shard_map/ppermute | solution.py:431
  114.0 5.1 %collective-permute-done.18.refs_1_ = f32[4,8,128]{2,1,0:T(8,128)S(1)} collective-permute-done((f32[4,8,128]{2,1,0:T(8,128)S(1)}, f32[4,8,128]{2,1,0:T(8,128)S(1)}, u32[]{:S(2)}, u32[]{:S(2)}) %collective-permute-start.18) | collective-permute-done | bytes 16416 | tf_op jit(solution)/shard_map/ppermute | solution.py:431
  119.9 7.3 %second_terms.1 = (bf16[2,128,256]{2,1,0:T(8,128)(2,1)}, bf16[2,128,256]{2,1,0:T(8,128)(2,1)}, f32[8,128]{1,0:T(8,128)}) custom-call(s32[30]{0:T(128)} %concatenate.9.info, f32[4,8,128]{2,1,0:T(8,128)} %copy-done.7, f32[4,8,128]{2,1,0:T(8,128)} %copy-done.8, bf16[5,256,256]{2,1,0:T(8,128)(2,1)} %copy-done.1, f32[256,256]{1,0:T(8,128)} %get-tuple-element.31.refs_3_, ...), custom_call_target="tpu_custom_call" | custom-call | flops 1744830464 | bytes 6815744 | tf_op jit(solution)/shard_map/second_terms/pallas_call | solution.py:319
  127.1 1.4 %collective-permute-start.24 = (bf16[2,128,256]{2,1,0:T(8,128)(2,1)}, bf16[2,128,256]{2,1,0:T(8,128)(2,1)S(1)}, u32[]{:S(2)}, u32[]{:S(2)}) collective-permute-start(bf16[2,128,256]{2,1,0:T(8,128)(2,1)} %get-tuple-element.35), channel_id=1, source_target_pairs={{0,2},{1,3},{2,0},{3,1},{4,6},{5,7},{6,4},{7,5},{8,10},{9,11},{10,... | collective-permute-start | bytes 393224 | tf_op jit(solution)/shard_map/ppermute | solution.py:346
  128.5 3.9 %collective-permute-done.24 = bf16[2,128,256]{2,1,0:T(8,128)(2,1)S(1)} collective-permute-done((bf16[2,128,256]{2,1,0:T(8,128)(2,1)}, bf16[2,128,256]{2,1,0:T(8,128)(2,1)S(1)}, u32[]{:S(2)}, u32[]{:S(2)}) %collective-permute-start.24) | collective-permute-done | bytes 131104 | tf_op jit(solution)/shard_map/ppermute | solution.py:346
  (74 shorter events, 14.3 us)
Async XLA Ops:
  0.6 1.0 copy-start
  1.6 15.6 %collective-permute-start.4 = (bf16[3,64,256]{2,1,0:T(8,128)(2,1)S(1)}, bf16[3,64,256]{2,1,0:T(8,128)(2,1)S(1)}, u32[]{:S(2)}, u32[]{:S(2)}) collective-permute-start(bf16[3,64,256]{2,1,0:T(8,128)(2,1)S(1)} %dynamic-slice_bitcast_fusion.1), channel_id=1, source_target_pairs={{0,2},{1,3},{2,0},{3,1},{4,6},{5,7},{6,4},{7,5},{8,10},{9,11},{10,... | collective-permute-start | bytes 294920 | tf_op jit(solution)/shard_map/ppermute | solution.py:346
  4.6 1.3 collective-permute-start
  10.6 6.4 %copy-start.9 = (s32[1,4]{1,0:T(1,128)S(1)}, s32[1,4]{1,0:T(1,128)}, u32[]{:S(2)}) copy-start(s32[1,4]{1,0:T(1,128)} %param.6) | copy-start | bytes 52
  16.4 38.4 %collective-permute-start.1 = (bf16[13,512,128]{2,1,0:T(8,128)(2,1)}, bf16[13,512,128]{2,1,0:T(8,128)(2,1)}, u32[]{:S(2)}, u32[]{:S(2)}) collective-permute-start(bf16[13,512,128]{2,1,0:T(8,128)(2,1)} %get-tuple-element.23), channel_id=1, source_target_pairs={{0,1},{1,0},{2,3},{3,2},{4,5},{5,4},{6,7},{7,6},{8,9},{9,8},{10,11... | collective-permute-start | bytes 5111816 | tf_op jit(solution)/shard_map/ppermute | solution.py:346
  17.1 3.1 %collective-permute-start.5 = (bf16[3,64,256]{2,1,0:T(8,128)(2,1)S(1)}, bf16[3,64,256]{2,1,0:T(8,128)(2,1)S(1)}, u32[]{:S(2)}, u32[]{:S(2)}) collective-permute-start(bf16[3,64,256]{2,1,0:T(8,128)(2,1)S(1)} %collective-permute-done.4), channel_id=1, source_target_pairs={{0,1},{1,0},{2,3},{3,2},{4,5},{5,4},{6,7},{7,6},{8,9},{9,8},{10,11... | collective-permute-start | bytes 294920 | tf_op jit(solution)/shard_map/ppermute | solution.py:346
  17.2 15.0 %collective-permute-start.12 = (bf16[4,512,128]{2,1,0:T(8,128)(2,1)}, bf16[4,512,128]{2,1,0:T(8,128)(2,1)S(1)}, u32[]{:S(2)}, u32[]{:S(2)}) collective-permute-start(bf16[4,512,128]{2,1,0:T(8,128)(2,1)} %get-tuple-element.20.refs_0_), channel_id=1, source_target_pairs={{0,2},{1,3},{2,0},{3,1},{4,6},{5,7},{6,4},{7,5},{8,10},{9,11},{10,... | collective-permute-start | bytes 1572872 | tf_op jit(solution)/shard_map/ppermute | solution.py:346
  17.3 25.3 %collective-permute-start.13 = (bf16[4,512,128]{2,1,0:T(8,128)(2,1)}, bf16[4,512,128]{2,1,0:T(8,128)(2,1)S(1)}, u32[]{:S(2)}, u32[]{:S(2)}) collective-permute-start(bf16[4,512,128]{2,1,0:T(8,128)(2,1)} %get-tuple-element.21.refs_1_), channel_id=1, source_target_pairs={{0,3},{1,2},{2,1},{3,0},{4,7},{5,6},{6,5},{7,4},{8,11},{9,10},{10,... | collective-permute-start | bytes 1572872 | tf_op jit(solution)/shard_map/ppermute | solution.py:346
  20.5 6.5 %collective-permute-start.6 = (bf16[256,256]{1,0:T(8,128)(2,1)S(1)}, bf16[256,256]{1,0:T(8,128)(2,1)S(1)}, u32[]{:S(2)}, u32[]{:S(2)}) collective-permute-start(bf16[256,256]{1,0:T(8,128)(2,1)S(1)} %get-tuple-element.51), channel_id=1, source_target_pairs={{0,4},{4,8},{8,12},{1,5},{5,9},{9,13},{2,6},{6,10},{10,14},{3,7},{... | collective-permute-start | bytes 393224 | tf_op jit(solution)/shard_map/ppermute | solution.py:391
  24.0 7.2 %collective-permute-start.7 = (bf16[256,256]{1,0:T(8,128)(2,1)S(1)}, bf16[256,256]{1,0:T(8,128)(2,1)S(1)}, u32[]{:S(2)}, u32[]{:S(2)}) collective-permute-start(bf16[256,256]{1,0:T(8,128)(2,1)S(1)} %get-tuple-element.51), channel_id=1, source_target_pairs={{4,0},{8,4},{12,8},{5,1},{9,5},{13,9},{6,2},{10,6},{14,10},{7,3},{... | collective-permute-start | bytes 393224 | tf_op jit(solution)/shard_map/ppermute | solution.py:392
  27.0 27.6 %collective-permute-start.10 = (bf16[4,512,128]{2,1,0:T(8,128)(2,1)}, bf16[4,512,128]{2,1,0:T(8,128)(2,1)S(1)}, u32[]{:S(2)}, u32[]{:S(2)}) collective-permute-start(bf16[4,512,128]{2,1,0:T(8,128)(2,1)} %get-tuple-element.28), channel_id=1, source_target_pairs={{0,2},{1,3},{2,0},{3,1},{4,6},{5,7},{6,4},{7,5},{8,10},{9,11},{10,... | collective-permute-start | bytes 1572872 | tf_op jit(solution)/shard_map/ppermute | solution.py:346
  31.2 34.0 %collective-permute-start.11 = (bf16[4,512,128]{2,1,0:T(8,128)(2,1)}, bf16[4,512,128]{2,1,0:T(8,128)(2,1)}, u32[]{:S(2)}, u32[]{:S(2)}) collective-permute-start(bf16[4,512,128]{2,1,0:T(8,128)(2,1)} %get-tuple-element.29), channel_id=1, source_target_pairs={{0,3},{1,2},{2,1},{3,0},{4,7},{5,6},{6,5},{7,4},{8,11},{9,10},{10,... | collective-permute-start | bytes 1572872 | tf_op jit(solution)/shard_map/ppermute | solution.py:346
  32.2 23.2 %copy-start.3 = (bf16[4,512,128]{2,1,0:T(8,128)(2,1)}, bf16[4,512,128]{2,1,0:T(8,128)(2,1)S(1)}, u32[]{:S(2)}) copy-start(bf16[4,512,128]{2,1,0:T(8,128)(2,1)S(1)} %collective-permute-done.12.refs_2_.refs_12_) | copy-start | bytes 1572868
  32.2 42.2 %collective-permute-start.8 = (bf16[3,512,128]{2,1,0:T(8,128)(2,1)}, bf16[3,512,128]{2,1,0:T(8,128)(2,1)}, u32[]{:S(2)}, u32[]{:S(2)}) collective-permute-start(bf16[3,512,128]{2,1,0:T(8,128)(2,1)} %get-tuple-element.26), channel_id=1, source_target_pairs={{0,2},{1,3},{2,0},{3,1},{4,6},{5,7},{6,4},{7,5},{8,10},{9,11},{10,... | collective-permute-start | bytes 1179656 | tf_op jit(solution)/shard_map/ppermute | solution.py:346
  42.6 12.8 %copy-start.4 = (bf16[4,512,128]{2,1,0:T(8,128)(2,1)}, bf16[4,512,128]{2,1,0:T(8,128)(2,1)S(1)}, u32[]{:S(2)}) copy-start(bf16[4,512,128]{2,1,0:T(8,128)(2,1)S(1)} %collective-permute-done.13.refs_3_.refs_13_) | copy-start | bytes 1572868
  42.6 39.4 %collective-permute-start.9 = (bf16[3,512,128]{2,1,0:T(8,128)(2,1)}, bf16[3,512,128]{2,1,0:T(8,128)(2,1)}, u32[]{:S(2)}, u32[]{:S(2)}) collective-permute-start(bf16[3,512,128]{2,1,0:T(8,128)(2,1)} %get-tuple-element.27), channel_id=1, source_target_pairs={{0,3},{1,2},{2,1},{3,0},{4,7},{5,6},{6,5},{7,4},{8,11},{9,10},{10,... | collective-permute-start | bytes 1179656 | tf_op jit(solution)/shard_map/ppermute | solution.py:346
  54.7 33.8 %collective-permute-start.2 = (bf16[2,512,128]{2,1,0:T(8,128)(2,1)}, bf16[2,512,128]{2,1,0:T(8,128)(2,1)}, u32[]{:S(2)}, u32[]{:S(2)}) collective-permute-start(bf16[2,512,128]{2,1,0:T(8,128)(2,1)} %get-tuple-element.24), channel_id=1, source_target_pairs={{0,2},{1,3},{2,0},{3,1},{4,6},{5,7},{6,4},{7,5},{8,10},{9,11},{10,... | collective-permute-start | bytes 786440 | tf_op jit(solution)/shard_map/ppermute | solution.py:346
  54.8 38.4 %collective-permute-start.3 = (bf16[2,512,128]{2,1,0:T(8,128)(2,1)}, bf16[2,512,128]{2,1,0:T(8,128)(2,1)}, u32[]{:S(2)}, u32[]{:S(2)}) collective-permute-start(bf16[2,512,128]{2,1,0:T(8,128)(2,1)} %get-tuple-element.25), channel_id=1, source_target_pairs={{0,3},{1,2},{2,1},{3,0},{4,7},{5,6},{6,5},{7,4},{8,11},{9,10},{10,... | collective-permute-start | bytes 786440 | tf_op jit(solution)/shard_map/ppermute | solution.py:346
  55.4 0.9 copy-start.1
  97.2 1.9 %collective-permute-start.14 = (f32[4,8,128]{2,1,0:T(8,128)}, f32[4,8,128]{2,1,0:T(8,128)S(1)}, u32[]{:S(2)}, u32[]{:S(2)}) collective-permute-start(f32[4,8,128]{2,1,0:T(8,128)} %get-tuple-element.30), channel_id=1, source_target_pairs={{0,1},{1,0},{2,3},{3,2},{4,5},{5,4},{6,7},{7,6},{8,9},{9,8},{10,11... | collective-permute-start | bytes 49160 | tf_op jit(solution)/shard_map/ppermute | solution.py:346
  97.5 3.9 %collective-permute-start.15 = (f32[4,8,128]{2,1,0:T(8,128)}, f32[4,8,128]{2,1,0:T(8,128)S(1)}, u32[]{:S(2)}, u32[]{:S(2)}) collective-permute-start(f32[4,8,128]{2,1,0:T(8,128)} %get-tuple-element.30), channel_id=1, source_target_pairs={{0,2},{1,3},{2,0},{3,1},{4,6},{5,7},{6,4},{7,5},{8,10},{9,11},{10,... | collective-permute-start | bytes 49160 | tf_op jit(solution)/shard_map/ppermute | solution.py:346
  97.8 3.6 %collective-permute-start.16 = (f32[4,8,128]{2,1,0:T(8,128)}, f32[4,8,128]{2,1,0:T(8,128)S(1)}, u32[]{:S(2)}, u32[]{:S(2)}) collective-permute-start(f32[4,8,128]{2,1,0:T(8,128)} %get-tuple-element.30), channel_id=1, source_target_pairs={{0,3},{1,2},{2,1},{3,0},{4,7},{5,6},{6,5},{7,4},{8,11},{9,10},{10,... | collective-permute-start | bytes 49160 | tf_op jit(solution)/shard_map/ppermute | solution.py:346
  102.2 6.8 %collective-permute-start.17 = (f32[4,8,128]{2,1,0:T(8,128)S(1)}, f32[4,8,128]{2,1,0:T(8,128)S(1)}, u32[]{:S(2)}, u32[]{:S(2)}) collective-permute-start(f32[4,8,128]{2,1,0:T(8,128)S(1)} %pad_maximum_fusion.1), channel_id=1, source_target_pairs={{0,4},{4,0},{8,12},{12,8},{1,5},{5,1},{9,13},{13,9},{2,6},{6,2},{1... | collective-permute-start | bytes 49160 | tf_op jit(solution)/shard_map/ppermute | solution.py:431
  104.0 15.1 %collective-permute-start.19 = (f32[256,256]{1,0:T(8,128)}, f32[256,256]{1,0:T(8,128)S(1)}, u32[]{:S(2)}, u32[]{:S(2)}) collective-permute-start(f32[256,256]{1,0:T(8,128)} %get-tuple-element.31.refs_3_), channel_id=1, source_target_pairs={{0,4},{4,8},{8,12},{1,5},{5,9},{9,13},{2,6},{6,10},{10,14},{3,7},{... | collective-permute-start | bytes 786440 | tf_op jit(solution)/shard_map/ppermute | solution.py:423
  106.2 12.8 %collective-permute-start.20 = (f32[256,256]{1,0:T(8,128)}, f32[256,256]{1,0:T(8,128)S(1)}, u32[]{:S(2)}, u32[]{:S(2)}) collective-permute-start(f32[256,256]{1,0:T(8,128)} %get-tuple-element.31.refs_3_), channel_id=1, source_target_pairs={{4,0},{8,4},{12,8},{5,1},{9,5},{13,9},{6,2},{10,6},{14,10},{7,3},{... | collective-permute-start | bytes 786440 | tf_op jit(solution)/shard_map/ppermute | solution.py:424
  107.5 11.6 %collective-permute-start.21 = (f32[256,256]{1,0:T(8,128)}, f32[256,256]{1,0:T(8,128)}, u32[]{:S(2)}, u32[]{:S(2)}) collective-permute-start(f32[256,256]{1,0:T(8,128)} %get-tuple-element.31.refs_3_), channel_id=1, source_target_pairs={{0,1},{1,0},{2,3},{3,2},{4,5},{5,4},{6,7},{7,6},{8,9},{9,8},{10,11... | collective-permute-start | bytes 786440 | tf_op jit(solution)/shard_map/ppermute | solution.py:346
  107.6 11.5 %collective-permute-start.22 = (f32[256,256]{1,0:T(8,128)}, f32[256,256]{1,0:T(8,128)}, u32[]{:S(2)}, u32[]{:S(2)}) collective-permute-start(f32[256,256]{1,0:T(8,128)} %get-tuple-element.31.refs_3_), channel_id=1, source_target_pairs={{1,2},{2,1},{5,6},{6,5},{9,10},{10,9},{13,14},{14,13},{17,18},{18,... | collective-permute-start | bytes 786440 | tf_op jit(solution)/shard_map/ppermute | solution.py:426
  109.0 10.1 %copy-start.7 = (f32[4,8,128]{2,1,0:T(8,128)}, f32[4,8,128]{2,1,0:T(8,128)S(1)}, u32[]{:S(2)}) copy-start(f32[4,8,128]{2,1,0:T(8,128)S(1)} %pad_maximum_fusion.2.refs_0_) | copy-start | bytes 49156
  109.0 10.0 %collective-permute-start.18 = (f32[4,8,128]{2,1,0:T(8,128)S(1)}, f32[4,8,128]{2,1,0:T(8,128)S(1)}, u32[]{:S(2)}, u32[]{:S(2)}) collective-permute-start(f32[4,8,128]{2,1,0:T(8,128)S(1)} %pad_maximum_fusion.2.refs_0_), channel_id=1, source_target_pairs={{0,8},{4,12},{8,0},{12,4},{1,9},{5,13},{9,1},{13,5},{2,10},{6,14},... | collective-permute-start | bytes 49160 | tf_op jit(solution)/shard_map/ppermute | solution.py:431
  127.1 5.2 %collective-permute-start.24 = (bf16[2,128,256]{2,1,0:T(8,128)(2,1)}, bf16[2,128,256]{2,1,0:T(8,128)(2,1)S(1)}, u32[]{:S(2)}, u32[]{:S(2)}) collective-permute-start(bf16[2,128,256]{2,1,0:T(8,128)(2,1)} %get-tuple-element.35), channel_id=1, source_target_pairs={{0,2},{1,3},{2,0},{3,1},{4,6},{5,7},{6,4},{7,5},{8,10},{9,11},{10,... | collective-permute-start | bytes 393224 | tf_op jit(solution)/shard_map/ppermute | solution.py:346
  128.5 5.1 %collective-permute-start.23 = (bf16[2,128,256]{2,1,0:T(8,128)(2,1)}, bf16[2,128,256]{2,1,0:T(8,128)(2,1)S(1)}, u32[]{:S(2)}, u32[]{:S(2)}) collective-permute-start(bf16[2,128,256]{2,1,0:T(8,128)(2,1)} %get-tuple-element.34), channel_id=1, source_target_pairs={{0,1},{1,0},{2,3},{3,2},{4,5},{5,4},{6,7},{7,6},{8,9},{9,8},{10,11... | collective-permute-start | bytes 393224 | tf_op jit(solution)/shard_map/ppermute | solution.py:346
  132.4 1.3 collective-permute-start.25
  (4 other events, 2.9 us)

commit v3 on v2

--- a/solution.py
+++ b/solution.py
@@ -7,7 +7,7 @@
 from jax.experimental.pallas import tpu as pltpu
 from jax.sharding import PartitionSpec as P
 
-CUTS = (0, 4, 8, 11, 13)
+CUTS = (0, 6, 9, 12, 13)
 EPS = 1e-06
 
 
@@ -106,15 +106,16 @@
     return until
 
 
-def pack_kernel(parts, info, left_env, right_env, *refs):
+def pack_kernel(parts, left_env, right_env, *refs):
     count = len(parts)
     refs = refs[-2 * count - 2 :]
     outs, bufs, (ins_sem, outs_sem) = refs[:count], refs[count : 2 * count], refs[-2:]
     half = right_env.shape[-1]
     width = right_env.shape[-2]
+    me = lax.axis_index("contr") * 2 + lax.axis_index("mpo")
     copies = []
     for (start, stop, flip), buf in zip(parts, bufs):
-        slot = info[2] ^ flip
+        slot = me ^ flip
         span = pl.ds(start, stop - start)
         pieces = [(right_env.at[span, 0, slot], buf.at[:, pl.ds(0, width)])]
         for lane in range(width // half):
@@ -136,15 +137,14 @@
         send.wait()
 
 
-def pack(parts, info, left_env, right_env, after=()):
+def pack(parts, left_env, right_env, after=()):
     width, half = right_env.shape[-2:]
     shapes = [(stop - start, 2 * width, half) for start, stop, _ in parts]
     out_shape = [jax.ShapeDtypeStruct(shape, jnp.bfloat16) for shape in shapes]
     size = sum(shape[0] for shape in shapes) * width * half * 8
     return pl.pallas_call(
         functools.partial(pack_kernel, parts),
-        in_specs=[pl.BlockSpec(memory_space=pltpu.SMEM)]
-        + [pl.BlockSpec(memory_space=pl.ANY)] * (2 + len(after)),
+        in_specs=[pl.BlockSpec(memory_space=pl.ANY)] * (2 + len(after)),
         out_specs=[pl.BlockSpec(memory_space=pl.ANY)] * len(parts),
         out_shape=out_shape,
         scratch_shapes=[pltpu.VMEM(shape, jnp.bfloat16) for shape in shapes]
@@ -155,7 +155,7 @@
         compiler_params=pltpu.CompilerParams(vmem_limit_bytes=63 * 2**20),
         cost_estimate=pl.CostEstimate(flops=0, bytes_accessed=size, transcendentals=0),
         name=f"pack_{parts[0][0]}_{len(parts)}",
-    )(info, left_env, right_env, *after)
+    )(left_env, right_env, *after)
 
 
 def inner_block(source, near, far):
@@ -207,10 +207,15 @@
     return jnp.where(across == 0, block, turned)
 
 
+def folded(block):
+    rows = jnp.sum(block.reshape(block.shape[0] // 8, 8, block.shape[1]), axis=0)
+    return sum(rows[:, at : at + 128] for at in range(0, block.shape[1], 128))
+
+
 def first_kernel(start, stop, last, info, *refs):
     count = 6 if start else 5
     here, refs = refs[:count], refs[count:]
-    outs, (sems, kept, *bufs) = refs[: 4 if last else 1], refs[4 if last else 1 :]
+    outs, (sems, kept, *bufs) = refs[: 3 if last else 1], refs[3 if last else 1 :]
     own, core, side, diag, source = bufs[:5]
     terms = here[0].shape[0]
     span = pl.ds(start, stop - start)
@@ -230,27 +235,58 @@
     for n in range(stop - start):
         items.append((info[4 + start + n], own, side, n, n))
         items.append((info[4 + terms + start + n], core, diag, n, n))
-    total = add_terms(items, source, kept, 2)
+    total = add_terms(items, source, kept, 4)
     if start:
         total = total + bufs[5][...]
     if not last:
         outs[0][...] = total
         return
-    image, mine, theirs, stats = outs
+    image, mine, theirs = outs
     half = mine.shape[0]
     field = source[0].astype(jnp.float32)
     live = live_block(field.shape, info[0] * half, info[1])
     block = jnp.where(live, own_first(total, info[0]), 0.0)
-    image[...] = block
+    image[: field.shape[0], :] = block
     mine[...] = block[:half].astype(jnp.bfloat16)
     theirs[...] = block[half:].astype(jnp.bfloat16)
-    product = jnp.sum(field * block, keepdims=True)
-    squares = jnp.sum(field * field, keepdims=True)
+    product, squares = folded(field * block), folded(field * field)
     quotient = product / (squares + EPS)
-    resid = block - quotient * field
-    rest = jnp.sum(resid * resid, keepdims=True)
-    for row, value in enumerate((product, squares, rest, quotient)):
-        stats[row] = jnp.broadcast_to(value, stats.shape[1:])
+    turns = (field.shape[0] // 8, field.shape[1] // 128)
+    resid = block - jnp.tile(quotient, turns) * field
+    for row, value in enumerate((product, squares, folded(resid * resid), quotient)):
+        at = field.shape[0] + 8 * (row // 2)
+        image[at : at + 8, 128 * (row % 2) : 128 * (row % 2 + 1)] = value
+
+
+def spread_kernel(mine, near, across, far, first, second):
+    me = lax.axis_index("contr") * 2 + lax.axis_index("mpo")
+    for flip, piece in enumerate((mine, near, across, far)):
+        first[0, me ^ flip] = piece[0]
+        second[0, me ^ flip] = piece[1]
+
+
+def merged(a, b):
+    product = a[0] + b[0]
+    squares = a[1] + b[1]
+    quotient = product / (squares + EPS)
+    return product, squares, about(a, quotient) + about(b, quotient), quotient
+
+
+def merge_tiles(a, b):
+    return jnp.stack(merged(a, b))
+
+
+def about(part, quotient):
+    product, squares, rest, own = part
+    off = own - quotient
+    return rest + (2.0 * off * (product - own * squares) + off * off * squares)
+
+
+def spread_kernel(mine, near, across, far, first, second):
+    me = lax.axis_index("contr") * 2 + lax.axis_index("mpo")
+    for flip, piece in enumerate((mine, near, across, far)):
+        first[0, me ^ flip] = piece[0]
+        second[0, me ^ flip] = piece[1]
 
 
 def merged(*stats):
@@ -283,29 +319,32 @@
     pairs += [(here[8], mine.at[0]), (here[9], theirs.at[0])]
     until = fetch(pairs, sems)
     terms = own.shape[0]
-    across, parity = info[0], info[2] % 2
+    across, parity, lower = info[0], info[2] % 2, info[3]
     half = mine.shape[1]
     until(before)
-    _, _, rest, quotient = merged(stats_a[...], stats_b[...])
-    factor = lax.rsqrt(rest / entries + EPS)
+    parts = merged(
+        [stats_a[row] for row in range(4)],
+        [stats_b[row] for row in range(4)],
+    )
+    product, squares = (jnp.sum(part, keepdims=True) for part in parts[:2])
+    quotient = product / (squares + EPS)
+    factor = lax.rsqrt(jnp.sum(about(parts, quotient), keepdims=True) / entries + EPS)
     ritz[...] = quotient
-    factor, quotient = factor[:1, :1], quotient[:1, :1]
-    for place, block, turned in zip((0, 1, 2, 4 - parity, 3 + parity), blocks, (0, 0, 0, 0, 1)):
-        image = block[...]
+    places = (0, 2 - lower, 1 + lower, 4 - parity, 3 + parity)
+    for place, block, turned in zip(places, blocks, (0, 0, 0, 0, 1)):
+        image = block[: 2 * half, :]
         if turned:
             image = jnp.concatenate([image[half:], image[:half]], axis=0)
         resid = image - quotient * source[place].astype(jnp.float32)
         second[place] = (resid * factor).astype(jnp.bfloat16)
 
-    total = None
+    items = []
     for n, (start, stop) in enumerate(spans):
-        until(before + 4 * (n + 1))
-        items = []
         for w in range(start, stop):
             items.append((info[4 + w], own, bufs[12 + 2 * n], w, w - start))
             items.append((info[4 + terms + w], core, bufs[13 + 2 * n], w, w - start))
-        part = add_terms(items, second, kept, 2)
-        total = part if total is None else total + part
+    until(len(pairs) - 2)
+    total = add_terms(items, second, kept, 4)
     total = own_first(total, across)
     live = live_block(total.shape, across * half, info[1])
     block = jnp.where(live, total, 0.0).astype(jnp.bfloat16)
@@ -323,7 +362,7 @@
         out_specs=[space] * len(out_shape),
         out_shape=out_shape,
         scratch_shapes=scratch,
-        compiler_params=pltpu.CompilerParams(vmem_limit_bytes=63 * 2**20),
+        compiler_params=pltpu.CompilerParams(vmem_limit_bytes=24 * 2**20),
         cost_estimate=pl.CostEstimate(flops=flops, bytes_accessed=flops // 256, transcendentals=0),
         name=name,
     )(info, *operands)
@@ -338,6 +377,7 @@
     cell = ("contr", "mpo")
     across, core = lax.axis_index("contr"), lax.axis_index("mpo")
     me = across * 2 + core
+    lower = lax.axis_index("sector") % 2
     sectors = lax.axis_size("sector")
     cuts = [terms * part // CUTS[-1] for part in CUTS]
     spans = list(zip(cuts[:-1], cuts[1:]))
@@ -351,18 +391,18 @@
     )
     part = swap(part, 2)
     shift_core = swap(term_shift, 1)
+    start, stop = spans[0]
+    head = pack([(start, stop, 2), (start, stop, 3)], left_env, right_env)
+    rest = [(start, stop, flip) for start, stop in spans[1:] for flip in (2, 3)]
+    *tail, to_core, own_env = pack(
+        rest + [(0, terms, 1), (0, terms, 0)], left_env, right_env, [*head, part]
+    )
+    messages = [swap(m, 2 + i % 2) for i, m in enumerate([*head, *tail])]
+    core_env = swap(to_core, 1)
     size_here = lax.dynamic_index_in_dim(sector_size[0], me, 0, keepdims=False)
     info = jnp.concatenate(
-        [jnp.stack([across, size_here, me, jnp.int32(0)]), term_shift, shift_core]
-    )
-    start, stop = spans[0]
-    head = pack([(start, stop, 2), (start, stop, 3)], info, left_env, right_env)
-    rest = [(start, stop, flip) for start, stop in spans[1:] for flip in (2, 3)]
-    *tail, to_core, own_env = pack(
-        rest + [(0, terms, 1), (0, terms, 0)], info, left_env, right_env, head
-    )
-    messages = [swap(m, 2 + i % 2) for i, m in enumerate([*head, *tail])]
-    core_env = swap(to_core, 1)
+        [jnp.stack([across, size_here, me, lower ^ core]), term_shift, shift_core]
+    )
 
     psi_mine = lax.dynamic_slice_in_dim(psi[0], across, slots - 1, axis=0)
     part_core = swap(part, 1)
@@ -383,22 +423,23 @@
     framed = jnp.concatenate([blank, whole, blank], axis=0)
     own = lax.dynamic_index_in_dim(whole, core, 0, keepdims=False)
     own = jnp.where(across == 0, own, lax.dynamic_index_in_dim(whole, core + 1, 0, keepdims=False))
-    up = [(i, i + 1) for i in range(sectors - 1)]
-    down = [(i + 1, i) for i in range(sectors - 1)]
+    even = [(i, i ^ 1) for i in range(sectors)]
+    odd = [(i, (i - 1 ^ 1) + 1) for i in range(1, sectors - 1)]
+    in_even, in_odd = lax.ppermute(own, "sector", even), lax.ppermute(own, "sector", odd)
     source = jnp.stack(
         [
             own,
-            lax.ppermute(own, "sector", up),
-            lax.ppermute(own, "sector", down),
+            jnp.where(lower == 1, in_even, in_odd),
+            jnp.where(lower == 1, in_odd, in_even),
             lax.dynamic_index_in_dim(framed, me - across, 0, keepdims=False),
             lax.dynamic_index_in_dim(framed, me - across + 2, 0, keepdims=False),
         ]
     )
 
     plain = jax.ShapeDtypeStruct((width, width), jnp.float32)
+    sent = jax.ShapeDtypeStruct((width + 16, width), jnp.float32)
     rows = jax.ShapeDtypeStruct((half, width), jnp.bfloat16)
-    tile = jax.ShapeDtypeStruct((4, 8, 128), jnp.float32)
-    kept = pltpu.VMEM((2, 2 * width, width), jnp.bfloat16)
+    kept = pltpu.VMEM((2, 4 * width, width), jnp.bfloat16)
     total = []
     for index, (start, stop) in enumerate(spans):
         last = stop == terms
@@ -407,7 +448,7 @@
         total = whole_call(
             functools.partial(first_kernel, start, stop, last),
             operands,
-            [plain, rows, rows, tile] if last else [plain],
+            [sent, rows, rows] if last else [plain],
             [pltpu.SemaphoreType.DMA((len(operands),)), kept]
             + [room(m, size) for m in operands[:4]]
             + [room(m) for m in operands[4:]],
@@ -415,23 +456,32 @@
             8 * size * width**3,
             f"first_terms_{start}",
         )
-    image_one, mine_one, theirs_one, stats = total
-
-    middle = [(1, 2), (2, 1)]
-    blocks = [
-        image_one,
-        lax.ppermute(image_one, "sector", up),
-        lax.ppermute(image_one, "sector", down),
-        swap(image_one, 1),
-        lax.ppermute(image_one, cell, middle),
+    image_one, mine_one, theirs_one = total
+
+    def sums_of(tail):
+        tail = tail.reshape(2, 8, 2, 128)
+        return tail.transpose(0, 2, 1, 3).reshape(4, 8, 128)
+
+    near = swap(image_one, 1)
+    beyond = lax.ppermute(image_one, cell, [(1, 2), (2, 1)])
+    planes = ("sector", "mpo")
+    turns = [
+        [(2 * i + (c ^ turn), 2 * j + (c ^ turn)) for c, pairs in enumerate((even, odd)) for i, j in pairs]
+        for turn in range(2)
     ]
-    stats = jnp.stack(merged(stats, swap(stats, 1), swap(stats, 2), swap(stats, 3)))
-    flip = 1
+    in_late = lax.ppermute(image_one, planes, turns[1])
+    in_early = lax.ppermute(image_one, planes, turns[0])
+    near, in_late, in_early, beyond = lax.optimization_barrier((near, in_late, in_early, beyond))
+    even_sums = jnp.where(core == 0, in_early[width:], in_late[width:])
+    stats = merge_tiles(sums_of(image_one[width:]), sums_of(even_sums))
+    stats = merge_tiles(merge_tiles(stats, swap(stats, 1)), merge_tiles(swap(stats, 2), swap(stats, 3)))
+    blocks = [image_one, in_early, in_late, near, beyond]
+    flip = 2
     while flip < sectors:
         pair = lax.ppermute(stats, "sector", [(i, i ^ flip) for i in range(sectors)])
         flip *= 2
         if flip < sectors:
-            stats = jnp.stack(merged(stats, pair))
+            stats = merge_tiles(stats, pair)
 
     operands = [stats, pair, source, *blocks, mine_one, theirs_one, own_env, core_env, *messages]
     mine, theirs, ritz = whole_call(
@@ -440,7 +490,7 @@
         [
             jax.ShapeDtypeStruct((2, half, width), jnp.bfloat16),
             jax.ShapeDtypeStruct((2, half, width), jnp.bfloat16),
-            jax.ShapeDtypeStruct((8, 128), jnp.float32),
+            jax.ShapeDtypeStruct((1, 1), jnp.float32),
         ],
         [
             pltpu.SemaphoreType.DMA((10 + 4 * len(spans),)),
@@ -455,27 +505,23 @@
 
     got = [mine, swap(mine, 1), swap(theirs, 2)]
     got.append(swap(got[2], 1))
-    flips = [me ^ v for v in range(slots)]
-    images = [
-        jnp.stack(
-            [
-                jnp.where(
-                    f < 2,
-                    jnp.where(f == 0, got[0][n], got[1][n]),
-                    jnp.where(f == 2, got[2][n], got[3][n]),
-                )
-                for f in flips
-            ]
-        )[None]
-        for n in range(2)
-    ]
-    return images[0], images[1], ritz[0, :1]
+    image = jax.ShapeDtypeStruct((1, slots, half, width), jnp.bfloat16)
+    space = pl.BlockSpec(memory_space=pltpu.VMEM)
+    first_image, second_image = pl.pallas_call(
+        spread_kernel,
+        in_specs=[space] * 4,
+        out_specs=[space] * 2,
+        out_shape=[image, image],
+        compiler_params=pltpu.CompilerParams(vmem_limit_bytes=16 * 2**20),
+        name="spread",
+    )(*got)
+    return first_image, second_image, ritz.reshape(1)
 
 
 def solution(mesh):
     sectors = mesh.shape["sector"]
     fits = mesh.shape["contr"] == 2 and mesh.shape["mpo"] == 2
-    fits = fits and sectors > 1 and sectors & (sectors - 1) == 0
+    fits = fits and sectors > 2 and sectors & (sectors - 1) == 0
 
     def body(psi, sector_size, left_env, right_env, term_shift):
         run = on_device if fits and psi.shape[1] == 4 else on_device_gather

time: 138 us -> 124 us (0.90)
  waiting for transfers between devices: 65.2 us -> 52.2 us
  starting transfers between devices: 27.1 us -> 37.3 us
  Pallas kernels: 32.2 us -> 27.3 us
  local copies, waits for them, and re-layouts: 7.12 us -> 3.17 us
  other arithmetic: 4.74 us -> 3.1 us
    ppermute x19, starting transfers between devices: 10.6 us -> 24.6 us  [swap(): return lax.ppermute(array, cell, [(i, i ^ flip) for i in range(slots)])]
    ppermute x19, waiting for transfers between devices: 54.9 us -> 48.9 us  [swap(): return lax.ppermute(array, cell, [(i, i ^ flip) for i in range(slots)])]
    pallas_call x5, Pallas kernels: 23.6 us -> 19.3 us  [whole_call(): pl.pallas_call(body, in_specs=[pl.BlockSpec(memory_space=pltpu.SMEM)] + [...]
    ppermute x2 -> x1, starting transfers between devices: 6.75 us -> 2.96 us  [on_device(): lax.ppermute(stats, 'sector', [(i, i ^ flip) for i in range(sectors)])]
    ppermute x5, waiting for transfers between devices: 5.21 us -> 1.42 us  [the longest x1 1.41 us: on_device(): lax.ppermute(own, 'sector', even)]
    ppermute x2 -> x1, waiting for transfers between devices: 5.06 us -> 1.82 us  [on_device(): lax.ppermute(stats, 'sector', [(i, i ^ flip) for i in range(sectors)])]
    select_n x3 -> x1, other arithmetic: 2.67 us -> 0.01 us  [on_device(): even_sums = jnp.where(core == 0, in_early[width:], in_late[width:])]
    pallas_call x2, Pallas kernels: 8.62 us -> 7.1 us  [pack(): pl.pallas_call(functools.partial(pack_kernel, parts), in_specs=[pl.BlockS...]
  transfers between devices with their start and end apart: 26 -> 25, of which waited for: 15 -> 13; matrix products, arithmetic and copies ran while one was open for 4% -> 4% of each run, Pallas kernels for 15% -> 14%
where the time goes in v3:
time: 124 us
  waiting for transfers between devices  52.2 us (42%)
  starting transfers between devices  37.3 us (30%)
  Pallas kernels  27.3 us (22%)
  local copies, waits for them, and re-layouts  3.17 us (3%)
  other arithmetic  3.1 us (2%)
    ppermute x19, waiting for transfers between devices, swap(): return lax.ppermute(array, cell, [(i, i ^ flip) for i in range(slots)])  48.9 us
    ppermute x19, starting transfers between devices, swap(): return lax.ppermute(array, cell, [(i, i ^ flip) for i in range(slots)])  24.6 us
    pallas_call x5, Pallas kernels, whole_call(): pl.pallas_call(body, in_specs=[pl.BlockSpec(memory_space=pltpu.SMEM)] + [...  19.3 us
    pallas_call x2, Pallas kernels, pack(): pl.pallas_call(functools.partial(pack_kernel, parts), in_specs=[pl.BlockS...  7.1 us
    ppermute x1, starting transfers between devices, on_device(): lax.ppermute(own, 'sector', even)  4.39 us
    ppermute x1, starting transfers between devices, on_device(): in_early = lax.ppermute(image_one, planes, turns[0])  3.3 us
    ppermute x1, starting transfers between devices, on_device(): lax.ppermute(stats, 'sector', [(i, i ^ flip) for i in range(sectors)])  2.96 us
  transfers between devices with their start and end apart: 25, of which 13 were waited for; matrix products, arithmetic and copies ran while one was open for 4% of the time, Pallas kernels for 14%

profile of v3, /device:TPU:0, one launch (start us, length us, event | category | flops | bytes accessed | tf_op | source)
XLA Modules:
  0.0 123.9 jit_solution(8675440097569895406)
XLA Ops:
  0.7 0.9 copy-done
  1.6 3.0 %collective-permute-start.1 = (bf16[3,64,256]{2,1,0:T(8,128)(2,1)S(1)}, bf16[3,64,256]{2,1,0:T(8,128)(2,1)S(1)}, u32[]{:S(2)}, u32[]{:S(2)}) collective-permute-start(bf16[3,64,256]{2,1,0:T(8,128)(2,1)S(1)} %dynamic-slice_bitcast_fusion.1), channel_id=1, source_target_pairs={{0,2},{1,3},{2,0},{3,1},{4,6},{5,7},{6,4},{7,5},{8,10},{9,11},{10,... | collective-permute-start | bytes 294920 | tf_op jit(solution)/shard_map/ppermute | solution.py:386
  4.6 2.4 %pack_0_2.1 = (bf16[6,512,128]{2,1,0:T(8,128)(2,1)}, bf16[6,512,128]{2,1,0:T(8,128)(2,1)}) custom-call(bf16[13,1,4,128,256]{4,3,2,1,0:T(8,128)(2,1)} %left_env.3, bf16[13,1,4,256,128]{4,3,2,1,0:T(8,128)(2,1)} %right_env.3), custom_call_target="tpu_custom_call" | custom-call | bytes 3145728 | tf_op jit(solution)/shard_map/pack_0_2/pallas_call | solution.py:145
  8.0 4.7 %pack_6_8.1 = (bf16[3,512,128]{2,1,0:T(8,128)(2,1)}, bf16[3,512,128]{2,1,0:T(8,128)(2,1)}, bf16[3,512,128]{2,1,0:T(8,128)(2,1)}, bf16[3,512,128]{2,1,0:T(8,128)(...) custom-call(bf16[13,1,4,128,256]{4,3,2,1,0:T(8,128)(2,1)} %left_env., ...), custom_call_target="tpu_custom_call" | custom-call | bytes 10485760 | tf_op jit(solution)/shard_map/pack_6_8/pallas_call | solution.py:145
  13.5 3.0 %collective-permute-done.5 = bf16[3,64,256]{2,1,0:T(8,128)(2,1)S(1)} collective-permute-done((bf16[3,64,256]{2,1,0:T(8,128)(2,1)}, bf16[3,64,256]{2,1,0:T(8,128)(2,1)S(1)}, u32[]{:S(2)}, u32[]{:S(2)}) %collective-permute-start.5) | collective-permute-done | bytes 98336 | tf_op jit(solution)/shard_map/ppermute | solution.py:386
  19.0 1.9 %collective-permute-start.10 = (bf16[3,512,128]{2,1,0:T(8,128)(2,1)}, bf16[3,512,128]{2,1,0:T(8,128)(2,1)S(1)}, u32[]{:S(2)}, u32[]{:S(2)}) collective-permute-start(bf16[3,512,128]{2,1,0:T(8,128)(2,1)} %get-tuple-element.33), channel_id=1, source_target_pairs={{0,2},{1,3},{2,0},{3,1},{4,6},{5,7},{6,4},{7,5},{8,10},{9,11},{10,... | collective-permute-start | bytes 1179656 | tf_op jit(solution)/shard_map/ppermute | solution.py:386
  20.9 1.0 collective-permute-done
  22.0 4.4 %collective-permute-start.6 = (bf16[256,256]{1,0:T(8,128)(2,1)}, bf16[256,256]{1,0:T(8,128)(2,1)S(1)}, u32[]{:S(2)}, u32[]{:S(2)}) collective-permute-start(bf16[256,256]{1,0:T(8,128)(2,1)} %get-tuple-element.53), channel_id=1, source_target_pairs={{0,4},{4,0},{8,12},{12,8},{1,5},{5,1},{9,13},{13,9},{2,6},{6,2},{1... | collective-permute-start | bytes 393224 | tf_op jit(solution)/shard_map/ppermute | solution.py:428
  28.0 1.1 pad_maximum_fusion
  29.0 1.4 %collective-permute-done.6 = bf16[256,256]{1,0:T(8,128)(2,1)S(1)} collective-permute-done((bf16[256,256]{1,0:T(8,128)(2,1)}, bf16[256,256]{1,0:T(8,128)(2,1)S(1)}, u32[]{:S(2)}, u32[]{:S(2)}) %collective-permute-start.6) | collective-permute-done | bytes 131104 | tf_op jit(solution)/shard_map/ppermute | solution.py:428
  31.0 5.1 %collective-permute-done.10.refs_2_.refs_14_ = bf16[3,512,128]{2,1,0:T(8,128)(2,1)S(1)} collective-permute-done((bf16[3,512,128]{2,1,0:T(8,128)(2,1)}, bf16[3,512,128]{2,1,0:T(8,128)(2,1)S(1)}, u32[]{:S(2)}, u32[]{:S(2)}) %collective-permute-start.10) | collective-permute-done | bytes 393248 | tf_op jit(solution)/shard_map/ppermute | solution.py:386
  36.1 1.7 %collective-permute-start.11 = (bf16[3,512,128]{2,1,0:T(8,128)(2,1)}, bf16[3,512,128]{2,1,0:T(8,128)(2,1)S(1)}, u32[]{:S(2)}, u32[]{:S(2)}) collective-permute-start(bf16[3,512,128]{2,1,0:T(8,128)(2,1)} %get-tuple-element.34), channel_id=1, source_target_pairs={{0,3},{1,2},{2,1},{3,0},{4,7},{5,6},{6,5},{7,4},{8,11},{9,10},{10,... | collective-permute-start | bytes 1179656 | tf_op jit(solution)/shard_map/ppermute | solution.py:386
  38.0 12.6 %collective-permute-done.13.refs_3_.refs_13_ = bf16[6,512,128]{2,1,0:T(8,128)(2,1)S(1)} collective-permute-done((bf16[6,512,128]{2,1,0:T(8,128)(2,1)}, bf16[6,512,128]{2,1,0:T(8,128)(2,1)S(1)}, u32[]{:S(2)}, u32[]{:S(2)}) %collective-permute-start.13) | collective-permute-done | bytes 786464 | tf_op jit(solution)/shard_map/ppermute | solution.py:386
  50.6 2.0 %collective-permute-start.3 = (bf16[1,512,128]{2,1,0:T(8,128)(2,1)}, bf16[1,512,128]{2,1,0:T(8,128)(2,1)S(1)}, u32[]{:S(2)}, u32[]{:S(2)}) collective-permute-start(bf16[1,512,128]{2,1,0:T(8,128)(2,1)} %get-tuple-element.29), channel_id=1, source_target_pairs={{0,2},{1,3},{2,0},{3,1},{4,6},{5,7},{6,4},{7,5},{8,10},{9,11},{10,... | collective-permute-start | bytes 393224 | tf_op jit(solution)/shard_map/ppermute | solution.py:386
  52.6 1.5 %collective-permute-start.4 = (bf16[1,512,128]{2,1,0:T(8,128)(2,1)}, bf16[1,512,128]{2,1,0:T(8,128)(2,1)S(1)}, u32[]{:S(2)}, u32[]{:S(2)}) collective-permute-start(bf16[1,512,128]{2,1,0:T(8,128)(2,1)} %get-tuple-element.30), channel_id=1, source_target_pairs={{0,3},{1,2},{2,1},{3,0},{4,7},{5,6},{6,5},{7,4},{8,11},{9,10},{10,... | collective-permute-start | bytes 393224 | tf_op jit(solution)/shard_map/ppermute | solution.py:386
  54.2 3.7 %first_terms_0.1.refs_5_ = f32[256,256]{1,0:T(8,128)S(1)} custom-call(s32[30]{0:T(128)S(1)} %concatenate.9.info, bf16[13,512,128]{2,1,0:T(8,128)(2,1)S(1)} %copy-done.1, bf16[13,512,128]{2,1,0:T(8,128)(2,1)} %collective-permute-done.2.refs_1_.refs_11_, bf16[6,512,128]{2,1,0:T(8,128)(2,1)} %collective-permute-done.12.refs_2_.refs_12_, ...), custom_call_target="tpu_custom_call" | custom-call | flops 805306368 | bytes 3145728 | tf_op jit(solution)/shard_map/first_terms_0/pallas_call | solution.py:358
  57.8 18.0 %collective-permute-done.11.refs_3_.refs_15_ = bf16[3,512,128]{2,1,0:T(8,128)(2,1)S(1)} collective-permute-done((bf16[3,512,128]{2,1,0:T(8,128)(2,1)}, bf16[3,512,128]{2,1,0:T(8,128)(2,1)S(1)}, u32[]{:S(2)}, u32[]{:S(2)}) %collective-permute-start.11) | collective-permute-done | bytes 393248 | tf_op jit(solution)/shard_map/ppermute | solution.py:386
  75.9 3.2 %first_terms_6.1.refs_5_ = f32[256,256]{1,0:T(8,128)S(1)} custom-call(s32[30]{0:T(128)S(1)} %concatenate.9.info, bf16[13,512,128]{2,1,0:T(8,128)(2,1)S(1)} %copy-done.1, bf16[13,512,128]{2,1,0:T(8,128)(2,1)} %collective-permute-done.2.refs_1_.refs_11_, bf16[3,512,128]{2,1,0:T(8,128)(2,1)S(1)} %collective-permute-done.10.refs_2_.refs_14_, ...), custom_call_target="tpu_custom_call" | custom-call | flops 402653184 | bytes 1572864 | tf_op jit(solution)/shard_map/first_terms_6/pallas_call | solution.py:358
  79.1 3.2 %first_terms_9.1.refs_5_ = f32[256,256]{1,0:T(8,128)S(1)} custom-call(s32[30]{0:T(128)S(1)} %concatenate.9.info, bf16[13,512,128]{2,1,0:T(8,128)(2,1)S(1)} %copy-done.1, bf16[13,512,128]{2,1,0:T(8,128)(2,1)} %collective-permute-done.2.refs_1_.refs_11_, bf16[3,512,128]{2,1,0:T(8,128)(2,1)S(1)} %collective-permute-done.8.refs_2_.refs_16_, ...), custom_call_target="tpu_custom_call" | custom-call | flops 402653184 | bytes 1572864 | tf_op jit(solution)/shard_map/first_terms_9/pallas_call | solution.py:358
  82.4 2.6 %first_terms_12.1 = (f32[272,256]{1,0:T(8,128)S(1)}, bf16[128,256]{1,0:T(8,128)(2,1)S(1)}, bf16[128,256]{1,0:T(8,128)(2,1)S(1)}) custom-call(s32[30]{0:T(128)S(1)} %concatenate.9.info, bf16[13,512,128]{2,1,0:T(8,128)(2,1)S(1)} %copy-done.1, bf16[13,512,128]{2,1,0:T(8,128)(2,1)} %collective-permute-done.2.refs_1_.refs_11_, ...), custom_call_target="tpu_custom_call" | custom-call | flops 134217728 | bytes 524288 | tf_op jit(solution)/shard_map/first_terms_12/pallas_call | solution.py:358
  85.7 3.3 %collective-permute-start.16 = (f32[272,256]{1,0:T(8,128)S(1)}, f32[272,256]{1,0:T(8,128)S(1)}, u32[]{:S(2)}, u32[]{:S(2)}) collective-permute-start(f32[272,256]{1,0:T(8,128)S(1)} %get-tuple-element.35.refs_3_), channel_id=1, source_target_pairs={{0,4},{4,0},{8,12},{12,8},{5,9},{9,5},{2,6},{6,2},{10,14},{14,10},... | collective-permute-start | bytes 835592 | tf_op jit(solution)/shard_map/ppermute | solution.py:473
  89.7 6.2 %collective-permute-start.14 = (f32[272,256]{1,0:T(8,128)S(1)}, f32[272,256]{1,0:T(8,128)S(1)}, u32[]{:S(2)}, u32[]{:S(2)}) collective-permute-start(f32[272,256]{1,0:T(8,128)S(1)} %get-tuple-element.35.refs_3_), channel_id=1, source_target_pairs={{0,1},{1,0},{2,3},{3,2},{4,5},{5,4},{6,7},{7,6},{8,9},{9,8},{10,11... | collective-permute-start | bytes 835592 | tf_op jit(solution)/shard_map/ppermute | solution.py:386
  95.9 1.2 collective-permute-done.14.refs_6_
  97.2 3.7 %collective-permute-start.20 = (f32[4,8,128]{2,1,0:T(8,128)S(1)}, f32[4,8,128]{2,1,0:T(8,128)S(1)}, u32[]{:S(2)}, u32[]{:S(2)}) collective-permute-start(f32[4,8,128]{2,1,0:T(8,128)S(1)} %pad_maximum_fusion.1), channel_id=1, source_target_pairs={{0,3},{1,2},{2,1},{3,0},{4,7},{5,6},{6,5},{7,4},{8,11},{9,10},{10,... | collective-permute-start | bytes 49160 | tf_op jit(solution)/shard_map/ppermute | solution.py:386
  100.9 1.1 collective-permute-start.19
  102.3 2.3 %collective-permute-done.19 = f32[4,8,128]{2,1,0:T(8,128)S(1)} collective-permute-done((f32[4,8,128]{2,1,0:T(8,128)S(1)}, f32[4,8,128]{2,1,0:T(8,128)S(1)}, u32[]{:S(2)}, u32[]{:S(2)}) %collective-permute-start.19) | collective-permute-done | bytes 16416 | tf_op jit(solution)/shard_map/ppermute | solution.py:386
  104.8 3.0 %collective-permute-start.21 = (f32[4,8,128]{2,1,0:T(8,128)S(1)}, f32[4,8,128]{2,1,0:T(8,128)S(1)}, u32[]{:S(2)}, u32[]{:S(2)}) collective-permute-start(f32[4,8,128]{2,1,0:T(8,128)S(1)} %pad_maximum_fusion.2.refs_0_), channel_id=1, source_target_pairs={{0,8},{4,12},{8,0},{12,4},{1,9},{5,13},{9,1},{13,5},{2,10},{6,14},... | collective-permute-start | bytes 49160 | tf_op jit(solution)/shard_map/ppermute | solution.py:481
  107.7 1.8 %collective-permute-done.21.refs_1_ = f32[4,8,128]{2,1,0:T(8,128)S(1)} collective-permute-done((f32[4,8,128]{2,1,0:T(8,128)S(1)}, f32[4,8,128]{2,1,0:T(8,128)S(1)}, u32[]{:S(2)}, u32[]{:S(2)}) %collective-permute-start.21) | collective-permute-done | bytes 16416 | tf_op jit(solution)/shard_map/ppermute | solution.py:481
  109.5 6.6 %second_terms.1 = (bf16[2,128,256]{2,1,0:T(8,128)(2,1)S(1)}, bf16[2,128,256]{2,1,0:T(8,128)(2,1)S(1)}, f32[1,1]{1,0:T(1,128)}) custom-call(s32[30]{0:T(128)S(1)} %concatenate.9.info, f32[4,8,128]{2,1,0:T(8,128)S(1)} %pad_maximum_fusion.2.refs_0_, f32[4,8,128]{2,1,0:T(8,128)S(1)} %collective-permute-done.21.refs_1_, ...), custom_call_target="tpu_custom_call" | custom-call | flops 1744830464 | bytes 6815744 | tf_op jit(solution)/shard_map/second_terms/pallas_call | solution.py:358
  116.2 1.9 %collective-permute-start.23 = (bf16[2,128,256]{2,1,0:T(8,128)(2,1)S(1)}, bf16[2,128,256]{2,1,0:T(8,128)(2,1)S(1)}, u32[]{:S(2)}, u32[]{:S(2)}) collective-permute-start(bf16[2,128,256]{2,1,0:T(8,128)(2,1)S(1)} %get-tuple-element.43), channel_id=1, source_target_pairs={{0,2},{1,3},{2,0},{3,1},{4,6},{5,7},{6,4},{7,5},{8,10},{9,11},{10,... | collective-permute-start | bytes 393224 | tf_op jit(solution)/shard_map/ppermute | solution.py:386
  118.0 3.7 %collective-permute-done.23.across = bf16[2,128,256]{2,1,0:T(8,128)(2,1)S(1)} collective-permute-done((bf16[2,128,256]{2,1,0:T(8,128)(2,1)S(1)}, bf16[2,128,256]{2,1,0:T(8,128)(2,1)S(1)}, u32[]{:S(2)}, u32[]{:S(2)}) %collective-permute-start.23) | collective-permute-done | bytes 131104 | tf_op jit(solution)/shard_map/ppermute | solution.py:386
  121.7 1.3 %collective-permute-done.24.far = bf16[2,128,256]{2,1,0:T(8,128)(2,1)S(1)} collective-permute-done((bf16[2,128,256]{2,1,0:T(8,128)(2,1)S(1)}, bf16[2,128,256]{2,1,0:T(8,128)(2,1)S(1)}, u32[]{:S(2)}, u32[]{:S(2)}) %collective-permute-start.24) | collective-permute-done | bytes 131104 | tf_op jit(solution)/shard_map/ppermute | solution.py:386
  (64 shorter events, 9.2 us)
Async XLA Ops:
  0.6 1.0 copy-start
  1.6 5.5 %copy-start.6 = (s32[1,4]{1,0:T(1,128)S(1)}, s32[1,4]{1,0:T(1,128)}, u32[]{:S(2)}) copy-start(s32[1,4]{1,0:T(1,128)} %param.6) | copy-start | bytes 52
  1.6 5.8 %collective-permute-start.1 = (bf16[3,64,256]{2,1,0:T(8,128)(2,1)S(1)}, bf16[3,64,256]{2,1,0:T(8,128)(2,1)S(1)}, u32[]{:S(2)}, u32[]{:S(2)}) collective-permute-start(bf16[3,64,256]{2,1,0:T(8,128)(2,1)S(1)} %dynamic-slice_bitcast_fusion.1), channel_id=1, source_target_pairs={{0,2},{1,3},{2,0},{3,1},{4,6},{5,7},{6,4},{7,5},{8,10},{9,11},{10,... | collective-permute-start | bytes 294920 | tf_op jit(solution)/shard_map/ppermute | solution.py:386
  7.0 29.2 %collective-permute-start.12 = (bf16[6,512,128]{2,1,0:T(8,128)(2,1)}, bf16[6,512,128]{2,1,0:T(8,128)(2,1)}, u32[]{:S(2)}, u32[]{:S(2)}) collective-permute-start(bf16[6,512,128]{2,1,0:T(8,128)(2,1)} %get-tuple-element.25.refs_0_), channel_id=1, source_target_pairs={{0,2},{1,3},{2,0},{3,1},{4,6},{5,7},{6,4},{7,5},{8,10},{9,11},{10,... | collective-permute-start | bytes 2359304 | tf_op jit(solution)/shard_map/ppermute | solution.py:386
  7.4 0.6 copy-start.3
  12.8 8.1 %copy-start.4 = (s32[13]{0:T(128)S(1)}, s32[13]{0:T(128)}, u32[]{:S(2)}) copy-start(s32[13]{0:T(128)} %param.9) | copy-start | bytes 160
  12.8 39.8 %collective-permute-start.2 = (bf16[13,512,128]{2,1,0:T(8,128)(2,1)}, bf16[13,512,128]{2,1,0:T(8,128)(2,1)}, u32[]{:S(2)}, u32[]{:S(2)}) collective-permute-start(bf16[13,512,128]{2,1,0:T(8,128)(2,1)} %get-tuple-element.28), channel_id=1, source_target_pairs={{0,1},{1,0},{2,3},{3,2},{4,5},{5,4},{6,7},{7,6},{8,9},{9,8},{10,11... | collective-permute-start | bytes 5111816 | tf_op jit(solution)/shard_map/ppermute | solution.py:386
  13.0 3.5 %collective-permute-start.5 = (bf16[3,64,256]{2,1,0:T(8,128)(2,1)}, bf16[3,64,256]{2,1,0:T(8,128)(2,1)S(1)}, u32[]{:S(2)}, u32[]{:S(2)}) collective-permute-start(bf16[3,64,256]{2,1,0:T(8,128)(2,1)} %copy-done.3), channel_id=1, source_target_pairs={{0,1},{1,0},{2,3},{3,2},{4,5},{5,4},{6,7},{7,6},{8,9},{9,8},{10,11... | collective-permute-start | bytes 294920 | tf_op jit(solution)/shard_map/ppermute | solution.py:386
  17.6 1.4 %copy-start.2 = (bf16[3,256,256]{2,1,0:T(8,128)(2,1)}, bf16[3,256,256]{2,1,0:T(8,128)(2,1)S(1)}, u32[]{:S(2)}) copy-start(bf16[3,256,256]{2,1,0:T(8,128)(2,1)S(1)} %and_select_fusion) | copy-start | bytes 1179652
  17.6 36.6 %copy-start.1 = (bf16[13,512,128]{2,1,0:T(8,128)(2,1)S(1)}, bf16[13,512,128]{2,1,0:T(8,128)(2,1)}, u32[]{:S(2)}) copy-start(bf16[13,512,128]{2,1,0:T(8,128)(2,1)} %get-tuple-element.27.refs_0_.refs_10_) | copy-start | bytes 5111812
  18.3 9.5 %collective-permute-start.7 = (bf16[256,256]{1,0:T(8,128)(2,1)}, bf16[256,256]{1,0:T(8,128)(2,1)S(1)}, u32[]{:S(2)}, u32[]{:S(2)}) collective-permute-start(bf16[256,256]{1,0:T(8,128)(2,1)} %get-tuple-element.53), channel_id=1, source_target_pairs={{4,8},{8,4},{5,9},{9,5},{6,10},{10,6},{7,11},{11,7},{20,24},{24,20... | collective-permute-start | bytes 393224 | tf_op jit(solution)/shard_map/ppermute | solution.py:428
  19.0 17.2 %collective-permute-start.10 = (bf16[3,512,128]{2,1,0:T(8,128)(2,1)}, bf16[3,512,128]{2,1,0:T(8,128)(2,1)S(1)}, u32[]{:S(2)}, u32[]{:S(2)}) collective-permute-start(bf16[3,512,128]{2,1,0:T(8,128)(2,1)} %get-tuple-element.33), channel_id=1, source_target_pairs={{0,2},{1,3},{2,0},{3,1},{4,6},{5,7},{6,4},{7,5},{8,10},{9,11},{10,... | collective-permute-start | bytes 1179656 | tf_op jit(solution)/shard_map/ppermute | solution.py:386
  20.9 1.1 collective-permute-start
  22.0 8.5 %collective-permute-start.6 = (bf16[256,256]{1,0:T(8,128)(2,1)}, bf16[256,256]{1,0:T(8,128)(2,1)S(1)}, u32[]{:S(2)}, u32[]{:S(2)}) collective-permute-start(bf16[256,256]{1,0:T(8,128)(2,1)} %get-tuple-element.53), channel_id=1, source_target_pairs={{0,4},{4,0},{8,12},{12,8},{1,5},{5,1},{9,13},{13,9},{2,6},{6,2},{1... | collective-permute-start | bytes 393224 | tf_op jit(solution)/shard_map/ppermute | solution.py:428
  27.8 8.3 %copy-start.5 = (bf16[3,512,128]{2,1,0:T(8,128)(2,1)S(1)}, bf16[3,512,128]{2,1,0:T(8,128)(2,1)}, u32[]{:S(2)}) copy-start(bf16[3,512,128]{2,1,0:T(8,128)(2,1)} %get-tuple-element.32) | copy-start | bytes 1179652
  27.8 22.8 %collective-permute-start.13 = (bf16[6,512,128]{2,1,0:T(8,128)(2,1)}, bf16[6,512,128]{2,1,0:T(8,128)(2,1)S(1)}, u32[]{:S(2)}, u32[]{:S(2)}) collective-permute-start(bf16[6,512,128]{2,1,0:T(8,128)(2,1)} %get-tuple-element.26.refs_1_), channel_id=1, source_target_pairs={{0,3},{1,2},{2,1},{3,0},{4,7},{5,6},{6,5},{7,4},{8,11},{9,10},{10,... | collective-permute-start | bytes 2359304 | tf_op jit(solution)/shard_map/ppermute | solution.py:386
  30.5 48.6 %collective-permute-start.8 = (bf16[3,512,128]{2,1,0:T(8,128)(2,1)}, bf16[3,512,128]{2,1,0:T(8,128)(2,1)S(1)}, u32[]{:S(2)}, u32[]{:S(2)}) collective-permute-start(bf16[3,512,128]{2,1,0:T(8,128)(2,1)} %get-tuple-element.31), channel_id=1, source_target_pairs={{0,2},{1,3},{2,0},{3,1},{4,6},{5,7},{6,4},{7,5},{8,10},{9,11},{10,... | collective-permute-start | bytes 1179656 | tf_op jit(solution)/shard_map/ppermute | solution.py:386
  36.1 43.0 %collective-permute-start.9 = (bf16[3,512,128]{2,1,0:T(8,128)(2,1)S(1)}, bf16[3,512,128]{2,1,0:T(8,128)(2,1)S(1)}, u32[]{:S(2)}, u32[]{:S(2)}) collective-permute-start(bf16[3,512,128]{2,1,0:T(8,128)(2,1)S(1)} %copy-done.5), channel_id=1, source_target_pairs={{0,3},{1,2},{2,1},{3,0},{4,7},{5,6},{6,5},{7,4},{8,11},{9,10},{10,... | collective-permute-start | bytes 1179656 | tf_op jit(solution)/shard_map/ppermute | solution.py:386
  36.1 39.7 %collective-permute-start.11 = (bf16[3,512,128]{2,1,0:T(8,128)(2,1)}, bf16[3,512,128]{2,1,0:T(8,128)(2,1)S(1)}, u32[]{:S(2)}, u32[]{:S(2)}) collective-permute-start(bf16[3,512,128]{2,1,0:T(8,128)(2,1)} %get-tuple-element.34), channel_id=1, source_target_pairs={{0,3},{1,2},{2,1},{3,0},{4,7},{5,6},{6,5},{7,4},{8,11},{9,10},{10,... | collective-permute-start | bytes 1179656 | tf_op jit(solution)/shard_map/ppermute | solution.py:386
  50.6 31.7 %collective-permute-start.3 = (bf16[1,512,128]{2,1,0:T(8,128)(2,1)}, bf16[1,512,128]{2,1,0:T(8,128)(2,1)S(1)}, u32[]{:S(2)}, u32[]{:S(2)}) collective-permute-start(bf16[1,512,128]{2,1,0:T(8,128)(2,1)} %get-tuple-element.29), channel_id=1, source_target_pairs={{0,2},{1,3},{2,0},{3,1},{4,6},{5,7},{6,4},{7,5},{8,10},{9,11},{10,... | collective-permute-start | bytes 393224 | tf_op jit(solution)/shard_map/ppermute | solution.py:386
  52.6 29.7 %collective-permute-start.4 = (bf16[1,512,128]{2,1,0:T(8,128)(2,1)}, bf16[1,512,128]{2,1,0:T(8,128)(2,1)S(1)}, u32[]{:S(2)}, u32[]{:S(2)}) collective-permute-start(bf16[1,512,128]{2,1,0:T(8,128)(2,1)} %get-tuple-element.30), channel_id=1, source_target_pairs={{0,3},{1,2},{2,1},{3,0},{4,7},{5,6},{6,5},{7,4},{8,11},{9,10},{10,... | collective-permute-start | bytes 393224 | tf_op jit(solution)/shard_map/ppermute | solution.py:386
  85.0 10.9 %collective-permute-start.17 = (f32[272,256]{1,0:T(8,128)S(1)}, f32[272,256]{1,0:T(8,128)S(1)}, u32[]{:S(2)}, u32[]{:S(2)}) collective-permute-start(f32[272,256]{1,0:T(8,128)S(1)} %get-tuple-element.35.refs_3_), channel_id=1, source_target_pairs={{1,2},{2,1},{5,6},{6,5},{9,10},{10,9},{13,14},{14,13},{17,18},{18,... | collective-permute-start | bytes 835592 | tf_op jit(solution)/shard_map/ppermute | solution.py:466
  85.7 10.2 %collective-permute-start.16 = (f32[272,256]{1,0:T(8,128)S(1)}, f32[272,256]{1,0:T(8,128)S(1)}, u32[]{:S(2)}, u32[]{:S(2)}) collective-permute-start(f32[272,256]{1,0:T(8,128)S(1)} %get-tuple-element.35.refs_3_), channel_id=1, source_target_pairs={{0,4},{4,0},{8,12},{12,8},{5,9},{9,5},{2,6},{6,2},{10,14},{14,10},... | collective-permute-start | bytes 835592 | tf_op jit(solution)/shard_map/ppermute | solution.py:473
  89.0 6.9 %collective-permute-start.15 = (f32[272,256]{1,0:T(8,128)S(1)}, f32[272,256]{1,0:T(8,128)S(1)}, u32[]{:S(2)}, u32[]{:S(2)}) collective-permute-start(f32[272,256]{1,0:T(8,128)S(1)} %get-tuple-element.35.refs_3_), channel_id=1, source_target_pairs={{1,5},{5,1},{9,13},{13,9},{4,8},{8,4},{3,7},{7,3},{11,15},{15,11},... | collective-permute-start | bytes 835592 | tf_op jit(solution)/shard_map/ppermute | solution.py:472
  89.7 7.4 %collective-permute-start.14 = (f32[272,256]{1,0:T(8,128)S(1)}, f32[272,256]{1,0:T(8,128)S(1)}, u32[]{:S(2)}, u32[]{:S(2)}) collective-permute-start(f32[272,256]{1,0:T(8,128)S(1)} %get-tuple-element.35.refs_3_), channel_id=1, source_target_pairs={{0,1},{1,0},{2,3},{3,2},{4,5},{5,4},{6,7},{7,6},{8,9},{9,8},{10,11... | collective-permute-start | bytes 835592 | tf_op jit(solution)/shard_map/ppermute | solution.py:386
  97.2 5.2 %collective-permute-start.20 = (f32[4,8,128]{2,1,0:T(8,128)S(1)}, f32[4,8,128]{2,1,0:T(8,128)S(1)}, u32[]{:S(2)}, u32[]{:S(2)}) collective-permute-start(f32[4,8,128]{2,1,0:T(8,128)S(1)} %pad_maximum_fusion.1), channel_id=1, source_target_pairs={{0,3},{1,2},{2,1},{3,0},{4,7},{5,6},{6,5},{7,4},{8,11},{9,10},{10,... | collective-permute-start | bytes 49160 | tf_op jit(solution)/shard_map/ppermute | solution.py:386
  100.9 3.8 %collective-permute-start.19 = (f32[4,8,128]{2,1,0:T(8,128)S(1)}, f32[4,8,128]{2,1,0:T(8,128)S(1)}, u32[]{:S(2)}, u32[]{:S(2)}) collective-permute-start(f32[4,8,128]{2,1,0:T(8,128)S(1)} %pad_maximum_fusion.1), channel_id=1, source_target_pairs={{0,2},{1,3},{2,0},{3,1},{4,6},{5,7},{6,4},{7,5},{8,10},{9,11},{10,... | collective-permute-start | bytes 49160 | tf_op jit(solution)/shard_map/ppermute | solution.py:386
  102.0 2.7 %collective-permute-start.18 = (f32[4,8,128]{2,1,0:T(8,128)S(1)}, f32[4,8,128]{2,1,0:T(8,128)S(1)}, u32[]{:S(2)}, u32[]{:S(2)}) collective-permute-start(f32[4,8,128]{2,1,0:T(8,128)S(1)} %pad_maximum_fusion.1), channel_id=1, source_target_pairs={{0,1},{1,0},{2,3},{3,2},{4,5},{5,4},{6,7},{7,6},{8,9},{9,8},{10,11... | collective-permute-start | bytes 49160 | tf_op jit(solution)/shard_map/ppermute | solution.py:386
  104.8 4.8 %collective-permute-start.21 = (f32[4,8,128]{2,1,0:T(8,128)S(1)}, f32[4,8,128]{2,1,0:T(8,128)S(1)}, u32[]{:S(2)}, u32[]{:S(2)}) collective-permute-start(f32[4,8,128]{2,1,0:T(8,128)S(1)} %pad_maximum_fusion.2.refs_0_), channel_id=1, source_target_pairs={{0,8},{4,12},{8,0},{12,4},{1,9},{5,13},{9,1},{13,5},{2,10},{6,14},... | collective-permute-start | bytes 49160 | tf_op jit(solution)/shard_map/ppermute | solution.py:481
  116.2 5.6 %collective-permute-start.23 = (bf16[2,128,256]{2,1,0:T(8,128)(2,1)S(1)}, bf16[2,128,256]{2,1,0:T(8,128)(2,1)S(1)}, u32[]{:S(2)}, u32[]{:S(2)}) collective-permute-start(bf16[2,128,256]{2,1,0:T(8,128)(2,1)S(1)} %get-tuple-element.43), channel_id=1, source_target_pairs={{0,2},{1,3},{2,0},{3,1},{4,6},{5,7},{6,4},{7,5},{8,10},{9,11},{10,... | collective-permute-start | bytes 393224 | tf_op jit(solution)/shard_map/ppermute | solution.py:386
  118.0 3.7 %collective-permute-start.22 = (bf16[2,128,256]{2,1,0:T(8,128)(2,1)S(1)}, bf16[2,128,256]{2,1,0:T(8,128)(2,1)S(1)}, u32[]{:S(2)}, u32[]{:S(2)}) collective-permute-start(bf16[2,128,256]{2,1,0:T(8,128)(2,1)S(1)} %get-tuple-element.42.mine), channel_id=1, source_target_pairs={{0,1},{1,0},{2,3},{3,2},{4,5},{5,4},{6,7},{7,6},{8,9},{9,8},{10,11... | collective-permute-start | bytes 393224 | tf_op jit(solution)/shard_map/ppermute | solution.py:386
  121.7 1.3 %collective-permute-start.24 = (bf16[2,128,256]{2,1,0:T(8,128)(2,1)S(1)}, bf16[2,128,256]{2,1,0:T(8,128)(2,1)S(1)}, u32[]{:S(2)}, u32[]{:S(2)}) collective-permute-start(bf16[2,128,256]{2,1,0:T(8,128)(2,1)S(1)} %collective-permute-done.23.across), channel_id=1, source_target_pairs={{0,1},{1,0},{2,3},{3,2},{4,5},{5,4},{6,7},{7,6},{8,9},{9,8},{10,11... | collective-permute-start | bytes 393224 | tf_op jit(solution)/shard_map/ppermute | solution.py:386

commit v4 on v3

--- a/solution.py
+++ b/solution.py
@@ -7,7 +7,7 @@
 from jax.experimental.pallas import tpu as pltpu
 from jax.sharding import PartitionSpec as P
 
-CUTS = (0, 6, 9, 12, 13)
+CUTS = (0, 6, 11, 13)
 EPS = 1e-06
 
 
@@ -471,7 +471,7 @@
     ]
     in_late = lax.ppermute(image_one, planes, turns[1])
     in_early = lax.ppermute(image_one, planes, turns[0])
-    near, in_late, in_early, beyond = lax.optimization_barrier((near, in_late, in_early, beyond))
+    near, beyond, in_late, in_early = lax.optimization_barrier((near, beyond, in_late, in_early))
     even_sums = jnp.where(core == 0, in_early[width:], in_late[width:])
     stats = merge_tiles(sums_of(image_one[width:]), sums_of(even_sums))
     stats = merge_tiles(merge_tiles(stats, swap(stats, 1)), merge_tiles(swap(stats, 2), swap(stats, 3)))

time: 124 us -> 122 us (0.984)
  waiting for transfers between devices: 52.2 us -> 57.6 us
  starting transfers between devices: 37.3 us -> 32.8 us
  Pallas kernels: 27.3 us -> 24.7 us
    pallas_call x5 -> x4, Pallas kernels: 19.3 us -> 16.3 us  [whole_call(): pl.pallas_call(body, in_specs=[pl.BlockSpec(memory_space=pltpu.SMEM)] + [...]
    ppermute x1, starting transfers between devices: 2.96 us -> 0.07 us  [on_device(): lax.ppermute(stats, 'sector', [(i, i ^ flip) for i in range(sectors)])]
    ppermute x1, waiting for transfers between devices: 1.82 us -> 4.62 us  [on_device(): lax.ppermute(stats, 'sector', [(i, i ^ flip) for i in range(sectors)])]
    ppermute x19 -> x17, waiting for transfers between devices: 48.9 us -> 50.9 us  [swap(): return lax.ppermute(array, cell, [(i, i ^ flip) for i in range(slots)])]
    ppermute x19 -> x17, starting transfers between devices: 24.6 us -> 22.9 us  [swap(): return lax.ppermute(array, cell, [(i, i ^ flip) for i in range(slots)])]
  transfers between devices with their start and end apart: 25 -> 23, of which waited for: 13 -> 13; matrix products, arithmetic and copies ran while one was open for 4% -> 3% of each run, Pallas kernels for 14% -> 12%
where the time goes in v4:
time: 122 us; the launch traced here: 121 us
  waiting for transfers between devices  57.6 us (47%)
  starting transfers between devices  32.8 us (27%)
  Pallas kernels  24.7 us (20%)
  local copies, waits for them, and re-layouts  3.05 us (2%)
  other arithmetic  2.1 us (2%)
    ppermute x17, waiting for transfers between devices, swap(): return lax.ppermute(array, cell, [(i, i ^ flip) for i in range(slots)])  50.9 us
    ppermute x17, starting transfers between devices, swap(): return lax.ppermute(array, cell, [(i, i ^ flip) for i in range(slots)])  22.9 us
    pallas_call x4, Pallas kernels, whole_call(): pl.pallas_call(body, in_specs=[pl.BlockSpec(memory_space=pltpu.SMEM)] + [...  16.3 us
    pallas_call x2, Pallas kernels, pack(): pl.pallas_call(functools.partial(pack_kernel, parts), in_specs=[pl.BlockS...  7.63 us
    ppermute x1, waiting for transfers between devices, on_device(): lax.ppermute(stats, 'sector', [(i, i ^ flip) for i in range(sectors)])  4.62 us
    ppermute x1, starting transfers between devices, on_device(): lax.ppermute(own, 'sector', even)  4.39 us
    ppermute x1, starting transfers between devices, on_device(): in_early = lax.ppermute(image_one, planes, turns[0])  3.48 us
  transfers between devices with their start and end apart: 23, of which 13 were waited for; matrix products, arithmetic and copies ran while one was open for 3% of the time, Pallas kernels for 12%

profile of v4, /device:TPU:0, one launch (start us, length us, event | category | flops | bytes accessed | tf_op | source)
XLA Modules:
  0.0 121.2 jit_solution(9432365526640340886)
XLA Ops:
  0.7 0.9 copy-done
  1.6 3.0 %collective-permute-start.1 = (bf16[3,64,256]{2,1,0:T(8,128)(2,1)S(1)}, bf16[3,64,256]{2,1,0:T(8,128)(2,1)S(1)}, u32[]{:S(2)}, u32[]{:S(2)}) collective-permute-start(bf16[3,64,256]{2,1,0:T(8,128)(2,1)S(1)} %dynamic-slice_bitcast_fusion.1), channel_id=1, source_target_pairs={{0,2},{1,3},{2,0},{3,1},{4,6},{5,7},{6,4},{7,5},{8,10},{9,11},{10,... | collective-permute-start | bytes 294920 | tf_op jit(solution)/shard_map/ppermute | solution.py:386
  4.6 2.5 %pack_0_2.1 = (bf16[6,512,128]{2,1,0:T(8,128)(2,1)}, bf16[6,512,128]{2,1,0:T(8,128)(2,1)}) custom-call(bf16[13,1,4,128,256]{4,3,2,1,0:T(8,128)(2,1)} %left_env.3, bf16[13,1,4,256,128]{4,3,2,1,0:T(8,128)(2,1)} %right_env.3), custom_call_target="tpu_custom_call" | custom-call | bytes 3145728 | tf_op jit(solution)/shard_map/pack_0_2/pallas_call | solution.py:145
  7.2 0.9 collective-permute-start.11
  8.8 5.2 %pack_6_6.1 = (bf16[5,512,128]{2,1,0:T(8,128)(2,1)}, bf16[5,512,128]{2,1,0:T(8,128)(2,1)}, bf16[2,512,128]{2,1,0:T(8,128)(2,1)}, bf16[2,512,128]{2,1,0:T(8,128)(...) custom-call(bf16[13,1,4,128,256]{4,3,2,1,0:T(8,128)(2,1)} %left_env.3, ...), custom_call_target="tpu_custom_call" | custom-call | bytes 10485760 | tf_op jit(solution)/shard_map/pack_6_6/pallas_call | solution.py:145
  14.0 1.3 %collective-permute-start.2 = (bf16[13,512,128]{2,1,0:T(8,128)(2,1)}, bf16[13,512,128]{2,1,0:T(8,128)(2,1)}, u32[]{:S(2)}, u32[]{:S(2)}) collective-permute-start(bf16[13,512,128]{2,1,0:T(8,128)(2,1)} %get-tuple-element.26), channel_id=1, source_target_pairs={{0,1},{1,0},{2,3},{3,2},{4,5},{5,4},{6,7},{7,6},{8,9},{9,8},{10,11... | collective-permute-start | bytes 5111816 | tf_op jit(solution)/shard_map/ppermute | solution.py:386
  15.4 3.3 %collective-permute-done.5 = bf16[3,64,256]{2,1,0:T(8,128)(2,1)S(1)} collective-permute-done((bf16[3,64,256]{2,1,0:T(8,128)(2,1)}, bf16[3,64,256]{2,1,0:T(8,128)(2,1)S(1)}, u32[]{:S(2)}, u32[]{:S(2)}) %collective-permute-start.5) | collective-permute-done | bytes 98336 | tf_op jit(solution)/shard_map/ppermute | solution.py:386
  18.7 0.9 broadcast_select_fusion.1
  21.4 1.0 collective-permute-done
  22.4 4.4 %collective-permute-start.6 = (bf16[256,256]{1,0:T(8,128)(2,1)}, bf16[256,256]{1,0:T(8,128)(2,1)S(1)}, u32[]{:S(2)}, u32[]{:S(2)}) collective-permute-start(bf16[256,256]{1,0:T(8,128)(2,1)} %get-tuple-element.49), channel_id=1, source_target_pairs={{0,4},{4,0},{8,12},{12,8},{1,5},{5,1},{9,13},{13,9},{2,6},{6,2},{1... | collective-permute-start | bytes 393224 | tf_op jit(solution)/shard_map/ppermute | solution.py:428
  28.8 2.0 %collective-permute-done.6 = bf16[256,256]{1,0:T(8,128)(2,1)S(1)} collective-permute-done((bf16[256,256]{1,0:T(8,128)(2,1)}, bf16[256,256]{1,0:T(8,128)(2,1)S(1)}, u32[]{:S(2)}, u32[]{:S(2)}) %collective-permute-start.6) | collective-permute-done | bytes 131104 | tf_op jit(solution)/shard_map/ppermute | solution.py:428
  31.0 1.5 %collective-permute-start.3 = (bf16[2,512,128]{2,1,0:T(8,128)(2,1)}, bf16[2,512,128]{2,1,0:T(8,128)(2,1)S(1)}, u32[]{:S(2)}, u32[]{:S(2)}) collective-permute-start(bf16[2,512,128]{2,1,0:T(8,128)(2,1)} %get-tuple-element.27), channel_id=1, source_target_pairs={{0,2},{1,3},{2,0},{3,1},{4,6},{5,7},{6,4},{7,5},{8,10},{9,11},{10,... | collective-permute-start | bytes 786440 | tf_op jit(solution)/shard_map/ppermute | solution.py:386
  32.5 9.8 %collective-permute-done.11.refs_3_.refs_13_ = bf16[6,512,128]{2,1,0:T(8,128)(2,1)} collective-permute-done((bf16[6,512,128]{2,1,0:T(8,128)(2,1)}, bf16[6,512,128]{2,1,0:T(8,128)(2,1)}, u32[]{:S(2)}, u32[]{:S(2)}) %collective-permute-start.11) | collective-permute-done | bytes 786464 | tf_op jit(solution)/shard_map/ppermute | solution.py:386
  42.3 1.9 %collective-permute-start.4 = (bf16[2,512,128]{2,1,0:T(8,128)(2,1)}, bf16[2,512,128]{2,1,0:T(8,128)(2,1)S(1)}, u32[]{:S(2)}, u32[]{:S(2)}) collective-permute-start(bf16[2,512,128]{2,1,0:T(8,128)(2,1)} %get-tuple-element.28), channel_id=1, source_target_pairs={{0,3},{1,2},{2,1},{3,0},{4,7},{5,6},{6,5},{7,4},{8,11},{9,10},{10,... | collective-permute-start | bytes 786440 | tf_op jit(solution)/shard_map/ppermute | solution.py:386
  44.2 3.9 %first_terms_0.1.refs_5_ = f32[256,256]{1,0:T(8,128)S(1)} custom-call(s32[30]{0:T(128)S(1)} %concatenate.9.info, bf16[13,512,128]{2,1,0:T(8,128)(2,1)S(1)} %copy-done.1, bf16[13,512,128]{2,1,0:T(8,128)(2,1)} %collective-permute-done.2.refs_1_.refs_11_, bf16[6,512,128]{2,1,0:T(8,128)(2,1)} %collective-permute-done.10.refs_2_.refs_12_, ...), custom_call_target="tpu_custom_call" | custom-call | flops 805306368 | bytes 3145728 | tf_op jit(solution)/shard_map/first_terms_0/pallas_call | solution.py:358
  48.2 10.5 %collective-permute-done.8.refs_2_.refs_14_ = bf16[5,512,128]{2,1,0:T(8,128)(2,1)S(1)} collective-permute-done((bf16[5,512,128]{2,1,0:T(8,128)(2,1)}, bf16[5,512,128]{2,1,0:T(8,128)(2,1)S(1)}, u32[]{:S(2)}, u32[]{:S(2)}) %collective-permute-start.8) | collective-permute-done | bytes 655392 | tf_op jit(solution)/shard_map/ppermute | solution.py:386
  58.7 11.7 %collective-permute-done.9.refs_3_.refs_15_ = bf16[5,512,128]{2,1,0:T(8,128)(2,1)S(1)} collective-permute-done((bf16[5,512,128]{2,1,0:T(8,128)(2,1)}, bf16[5,512,128]{2,1,0:T(8,128)(2,1)S(1)}, u32[]{:S(2)}, u32[]{:S(2)}) %collective-permute-start.9) | collective-permute-done | bytes 655392 | tf_op jit(solution)/shard_map/ppermute | solution.py:386
  70.4 3.6 %first_terms_6.1.refs_5_ = f32[256,256]{1,0:T(8,128)S(1)} custom-call(s32[30]{0:T(128)S(1)} %concatenate.9.info, bf16[13,512,128]{2,1,0:T(8,128)(2,1)S(1)} %copy-done.1, bf16[13,512,128]{2,1,0:T(8,128)(2,1)} %collective-permute-done.2.refs_1_.refs_11_, bf16[5,512,128]{2,1,0:T(8,128)(2,1)S(1)} %collective-permute-done.8.refs_2_.refs_14_, ...), custom_call_target="tpu_custom_call" | custom-call | flops 671088640 | bytes 2621440 | tf_op jit(solution)/shard_map/first_terms_6/pallas_call | solution.py:358
  74.0 4.4 %collective-permute-done.3.refs_2_.refs_16_ = bf16[2,512,128]{2,1,0:T(8,128)(2,1)S(1)} collective-permute-done((bf16[2,512,128]{2,1,0:T(8,128)(2,1)}, bf16[2,512,128]{2,1,0:T(8,128)(2,1)S(1)}, u32[]{:S(2)}, u32[]{:S(2)}) %collective-permute-start.3) | collective-permute-done | bytes 262176 | tf_op jit(solution)/shard_map/ppermute | solution.py:386
  78.4 2.7 %collective-permute-done.4.refs_3_.refs_17_ = bf16[2,512,128]{2,1,0:T(8,128)(2,1)S(1)} collective-permute-done((bf16[2,512,128]{2,1,0:T(8,128)(2,1)}, bf16[2,512,128]{2,1,0:T(8,128)(2,1)S(1)}, u32[]{:S(2)}, u32[]{:S(2)}) %collective-permute-start.4) | collective-permute-done | bytes 262176 | tf_op jit(solution)/shard_map/ppermute | solution.py:386
  81.0 2.5 %first_terms_11.1 = (f32[272,256]{1,0:T(8,128)S(1)}, bf16[128,256]{1,0:T(8,128)(2,1)S(1)}, bf16[128,256]{1,0:T(8,128)(2,1)S(1)}) custom-call(s32[30]{0:T(128)S(1)} %concatenate.9.info, bf16[13,512,128]{2,1,0:T(8,128)(2,1)S(1)} %copy-done.1, bf16[13,512,128]{2,1,0:T(8,128)(2,1)} %collective-permute-done.2.refs_1_.refs_11_, ...), custom_call_target="tpu_custom_call" | custom-call | flops 268435456 | bytes 1048576 | tf_op jit(solution)/shard_map/first_terms_11/pallas_call | solution.py:358
  83.6 3.5 %collective-permute-start.15 = (f32[272,256]{1,0:T(8,128)S(1)}, f32[272,256]{1,0:T(8,128)S(1)}, u32[]{:S(2)}, u32[]{:S(2)}) collective-permute-start(f32[272,256]{1,0:T(8,128)S(1)} %get-tuple-element.31.refs_3_), channel_id=1, source_target_pairs={{0,4},{4,0},{8,12},{12,8},{5,9},{9,5},{2,6},{6,2},{10,14},{14,10},... | collective-permute-start | bytes 835592 | tf_op jit(solution)/shard_map/ppermute | solution.py:473
  88.4 4.8 %collective-permute-start.12 = (f32[272,256]{1,0:T(8,128)S(1)}, f32[272,256]{1,0:T(8,128)S(1)}, u32[]{:S(2)}, u32[]{:S(2)}) collective-permute-start(f32[272,256]{1,0:T(8,128)S(1)} %get-tuple-element.31.refs_3_), channel_id=1, source_target_pairs={{0,1},{1,0},{2,3},{3,2},{4,5},{5,4},{6,7},{7,6},{8,9},{9,8},{10,11... | collective-permute-start | bytes 835592 | tf_op jit(solution)/shard_map/ppermute | solution.py:386
  93.3 1.2 collective-permute-done.12.refs_6_
  94.5 1.8 %collective-permute-start.18 = (f32[4,8,128]{2,1,0:T(8,128)S(1)}, f32[4,8,128]{2,1,0:T(8,128)S(1)}, u32[]{:S(2)}, u32[]{:S(2)}) collective-permute-start(f32[4,8,128]{2,1,0:T(8,128)S(1)} %pad_maximum_fusion.1), channel_id=1, source_target_pairs={{0,3},{1,2},{2,1},{3,0},{4,7},{5,6},{6,5},{7,4},{8,11},{9,10},{10,... | collective-permute-start | bytes 49160 | tf_op jit(solution)/shard_map/ppermute | solution.py:386
  96.3 4.8 %collective-permute-start.17 = (f32[4,8,128]{2,1,0:T(8,128)S(1)}, f32[4,8,128]{2,1,0:T(8,128)S(1)}, u32[]{:S(2)}, u32[]{:S(2)}) collective-permute-start(f32[4,8,128]{2,1,0:T(8,128)S(1)} %pad_maximum_fusion.1), channel_id=1, source_target_pairs={{0,2},{1,3},{2,0},{3,1},{4,6},{5,7},{6,4},{7,5},{8,10},{9,11},{10,... | collective-permute-start | bytes 49160 | tf_op jit(solution)/shard_map/ppermute | solution.py:386
  101.1 1.9 %collective-permute-done.17 = f32[4,8,128]{2,1,0:T(8,128)S(1)} collective-permute-done((f32[4,8,128]{2,1,0:T(8,128)S(1)}, f32[4,8,128]{2,1,0:T(8,128)S(1)}, u32[]{:S(2)}, u32[]{:S(2)}) %collective-permute-start.17) | collective-permute-done | bytes 16416 | tf_op jit(solution)/shard_map/ppermute | solution.py:386
  103.1 4.6 %collective-permute-done.19.refs_1_ = f32[4,8,128]{2,1,0:T(8,128)S(1)} collective-permute-done((f32[4,8,128]{2,1,0:T(8,128)S(1)}, f32[4,8,128]{2,1,0:T(8,128)S(1)}, u32[]{:S(2)}, u32[]{:S(2)}) %collective-permute-start.19) | collective-permute-done | bytes 16416 | tf_op jit(solution)/shard_map/ppermute | solution.py:481
  107.7 6.2 %second_terms.1 = (bf16[2,128,256]{2,1,0:T(8,128)(2,1)S(1)}, bf16[2,128,256]{2,1,0:T(8,128)(2,1)S(1)}, f32[1,1]{1,0:T(1,128)}) custom-call(s32[30]{0:T(128)S(1)} %concatenate.9.info, f32[4,8,128]{2,1,0:T(8,128)S(1)} %pad_maximum_fusion.2.refs_0_, f32[4,8,128]{2,1,0:T(8,128)S(1)} %collective-permute-done.19.refs_1_, ...), custom_call_target="tpu_custom_call" | custom-call | flops 1744830464 | bytes 6815744 | tf_op jit(solution)/shard_map/second_terms/pallas_call | solution.py:358
  114.0 1.9 %collective-permute-start.21 = (bf16[2,128,256]{2,1,0:T(8,128)(2,1)S(1)}, bf16[2,128,256]{2,1,0:T(8,128)(2,1)S(1)}, u32[]{:S(2)}, u32[]{:S(2)}) collective-permute-start(bf16[2,128,256]{2,1,0:T(8,128)(2,1)S(1)} %get-tuple-element.39), channel_id=1, source_target_pairs={{0,2},{1,3},{2,0},{3,1},{4,6},{5,7},{6,4},{7,5},{8,10},{9,11},{10,... | collective-permute-start | bytes 393224 | tf_op jit(solution)/shard_map/ppermute | solution.py:386
  115.9 3.1 %collective-permute-done.21.across = bf16[2,128,256]{2,1,0:T(8,128)(2,1)S(1)} collective-permute-done((bf16[2,128,256]{2,1,0:T(8,128)(2,1)S(1)}, bf16[2,128,256]{2,1,0:T(8,128)(2,1)S(1)}, u32[]{:S(2)}, u32[]{:S(2)}) %collective-permute-start.21) | collective-permute-done | bytes 131104 | tf_op jit(solution)/shard_map/ppermute | solution.py:386
  119.0 1.3 %collective-permute-done.22.far = bf16[2,128,256]{2,1,0:T(8,128)(2,1)S(1)} collective-permute-done((bf16[2,128,256]{2,1,0:T(8,128)(2,1)S(1)}, bf16[2,128,256]{2,1,0:T(8,128)(2,1)S(1)}, u32[]{:S(2)}, u32[]{:S(2)}) %collective-permute-start.22) | collective-permute-done | bytes 131104 | tf_op jit(solution)/shard_map/ppermute | solution.py:386
  (55 shorter events, 7.2 us)
Async XLA Ops:
  0.6 1.0 copy-start
  1.6 6.5 %copy-start.4 = (s32[1,4]{1,0:T(1,128)S(1)}, s32[1,4]{1,0:T(1,128)}, u32[]{:S(2)}) copy-start(s32[1,4]{1,0:T(1,128)} %param.6) | copy-start | bytes 52
  1.6 6.5 %collective-permute-start.1 = (bf16[3,64,256]{2,1,0:T(8,128)(2,1)S(1)}, bf16[3,64,256]{2,1,0:T(8,128)(2,1)S(1)}, u32[]{:S(2)}, u32[]{:S(2)}) collective-permute-start(bf16[3,64,256]{2,1,0:T(8,128)(2,1)S(1)} %dynamic-slice_bitcast_fusion.1), channel_id=1, source_target_pairs={{0,2},{1,3},{2,0},{3,1},{4,6},{5,7},{6,4},{7,5},{8,10},{9,11},{10,... | collective-permute-start | bytes 294920 | tf_op jit(solution)/shard_map/ppermute | solution.py:386
  7.1 23.9 %collective-permute-start.10 = (bf16[6,512,128]{2,1,0:T(8,128)(2,1)}, bf16[6,512,128]{2,1,0:T(8,128)(2,1)}, u32[]{:S(2)}, u32[]{:S(2)}) collective-permute-start(bf16[6,512,128]{2,1,0:T(8,128)(2,1)} %get-tuple-element.23.refs_0_), channel_id=1, source_target_pairs={{0,2},{1,3},{2,0},{3,1},{4,6},{5,7},{6,4},{7,5},{8,10},{9,11},{10,... | collective-permute-start | bytes 2359304 | tf_op jit(solution)/shard_map/ppermute | solution.py:386
  7.2 35.1 %collective-permute-start.11 = (bf16[6,512,128]{2,1,0:T(8,128)(2,1)}, bf16[6,512,128]{2,1,0:T(8,128)(2,1)}, u32[]{:S(2)}, u32[]{:S(2)}) collective-permute-start(bf16[6,512,128]{2,1,0:T(8,128)(2,1)} %get-tuple-element.24.refs_1_), channel_id=1, source_target_pairs={{0,3},{1,2},{2,1},{3,0},{4,7},{5,6},{6,5},{7,4},{8,11},{9,10},{10,... | collective-permute-start | bytes 2359304 | tf_op jit(solution)/shard_map/ppermute | solution.py:386
  8.1 0.6 copy-start.2
  13.9 7.3 %copy-start.3 = (s32[13]{0:T(128)S(1)}, s32[13]{0:T(128)}, u32[]{:S(2)}) copy-start(s32[13]{0:T(128)} %param.9) | copy-start | bytes 160
  14.0 30.3 %collective-permute-start.2 = (bf16[13,512,128]{2,1,0:T(8,128)(2,1)}, bf16[13,512,128]{2,1,0:T(8,128)(2,1)}, u32[]{:S(2)}, u32[]{:S(2)}) collective-permute-start(bf16[13,512,128]{2,1,0:T(8,128)(2,1)} %get-tuple-element.26), channel_id=1, source_target_pairs={{0,1},{1,0},{2,3},{3,2},{4,5},{5,4},{6,7},{7,6},{8,9},{9,8},{10,11... | collective-permute-start | bytes 5111816 | tf_op jit(solution)/shard_map/ppermute | solution.py:386
  15.3 3.4 %collective-permute-start.5 = (bf16[3,64,256]{2,1,0:T(8,128)(2,1)}, bf16[3,64,256]{2,1,0:T(8,128)(2,1)S(1)}, u32[]{:S(2)}, u32[]{:S(2)}) collective-permute-start(bf16[3,64,256]{2,1,0:T(8,128)(2,1)} %copy-done.2), channel_id=1, source_target_pairs={{0,1},{1,0},{2,3},{3,2},{4,5},{5,4},{6,7},{7,6},{8,9},{9,8},{10,11... | collective-permute-start | bytes 294920 | tf_op jit(solution)/shard_map/ppermute | solution.py:386
  19.8 24.4 %copy-start.1 = (bf16[13,512,128]{2,1,0:T(8,128)(2,1)S(1)}, bf16[13,512,128]{2,1,0:T(8,128)(2,1)}, u32[]{:S(2)}) copy-start(bf16[13,512,128]{2,1,0:T(8,128)(2,1)} %get-tuple-element.25.refs_0_.refs_10_) | copy-start | bytes 5111812
  20.5 7.7 %collective-permute-start.7 = (bf16[256,256]{1,0:T(8,128)(2,1)}, bf16[256,256]{1,0:T(8,128)(2,1)S(1)}, u32[]{:S(2)}, u32[]{:S(2)}) collective-permute-start(bf16[256,256]{1,0:T(8,128)(2,1)} %get-tuple-element.49), channel_id=1, source_target_pairs={{4,8},{8,4},{5,9},{9,5},{6,10},{10,6},{7,11},{11,7},{20,24},{24,20... | collective-permute-start | bytes 393224 | tf_op jit(solution)/shard_map/ppermute | solution.py:428
  21.2 1.2 collective-permute-start
  22.4 8.5 %collective-permute-start.6 = (bf16[256,256]{1,0:T(8,128)(2,1)}, bf16[256,256]{1,0:T(8,128)(2,1)S(1)}, u32[]{:S(2)}, u32[]{:S(2)}) collective-permute-start(bf16[256,256]{1,0:T(8,128)(2,1)} %get-tuple-element.49), channel_id=1, source_target_pairs={{0,4},{4,0},{8,12},{12,8},{1,5},{5,1},{9,13},{13,9},{2,6},{6,2},{1... | collective-permute-start | bytes 393224 | tf_op jit(solution)/shard_map/ppermute | solution.py:428
  28.2 30.5 %collective-permute-start.8 = (bf16[5,512,128]{2,1,0:T(8,128)(2,1)}, bf16[5,512,128]{2,1,0:T(8,128)(2,1)S(1)}, u32[]{:S(2)}, u32[]{:S(2)}) collective-permute-start(bf16[5,512,128]{2,1,0:T(8,128)(2,1)} %get-tuple-element.29), channel_id=1, source_target_pairs={{0,2},{1,3},{2,0},{3,1},{4,6},{5,7},{6,4},{7,5},{8,10},{9,11},{10,... | collective-permute-start | bytes 1966088 | tf_op jit(solution)/shard_map/ppermute | solution.py:386
  30.9 39.5 %collective-permute-start.9 = (bf16[5,512,128]{2,1,0:T(8,128)(2,1)}, bf16[5,512,128]{2,1,0:T(8,128)(2,1)S(1)}, u32[]{:S(2)}, u32[]{:S(2)}) collective-permute-start(bf16[5,512,128]{2,1,0:T(8,128)(2,1)} %get-tuple-element.30), channel_id=1, source_target_pairs={{0,3},{1,2},{2,1},{3,0},{4,7},{5,6},{6,5},{7,4},{8,11},{9,10},{10,... | collective-permute-start | bytes 1966088 | tf_op jit(solution)/shard_map/ppermute | solution.py:386
  31.0 47.4 %collective-permute-start.3 = (bf16[2,512,128]{2,1,0:T(8,128)(2,1)}, bf16[2,512,128]{2,1,0:T(8,128)(2,1)S(1)}, u32[]{:S(2)}, u32[]{:S(2)}) collective-permute-start(bf16[2,512,128]{2,1,0:T(8,128)(2,1)} %get-tuple-element.27), channel_id=1, source_target_pairs={{0,2},{1,3},{2,0},{3,1},{4,6},{5,7},{6,4},{7,5},{8,10},{9,11},{10,... | collective-permute-start | bytes 786440 | tf_op jit(solution)/shard_map/ppermute | solution.py:386
  42.3 38.8 %collective-permute-start.4 = (bf16[2,512,128]{2,1,0:T(8,128)(2,1)}, bf16[2,512,128]{2,1,0:T(8,128)(2,1)S(1)}, u32[]{:S(2)}, u32[]{:S(2)}) collective-permute-start(bf16[2,512,128]{2,1,0:T(8,128)(2,1)} %get-tuple-element.28), channel_id=1, source_target_pairs={{0,3},{1,2},{2,1},{3,0},{4,7},{5,6},{6,5},{7,4},{8,11},{9,10},{10,... | collective-permute-start | bytes 786440 | tf_op jit(solution)/shard_map/ppermute | solution.py:386
  83.6 9.7 %collective-permute-start.15 = (f32[272,256]{1,0:T(8,128)S(1)}, f32[272,256]{1,0:T(8,128)S(1)}, u32[]{:S(2)}, u32[]{:S(2)}) collective-permute-start(f32[272,256]{1,0:T(8,128)S(1)} %get-tuple-element.31.refs_3_), channel_id=1, source_target_pairs={{0,4},{4,0},{8,12},{12,8},{5,9},{9,5},{2,6},{6,2},{10,14},{14,10},... | collective-permute-start | bytes 835592 | tf_op jit(solution)/shard_map/ppermute | solution.py:473
  87.1 6.2 %collective-permute-start.14 = (f32[272,256]{1,0:T(8,128)S(1)}, f32[272,256]{1,0:T(8,128)S(1)}, u32[]{:S(2)}, u32[]{:S(2)}) collective-permute-start(f32[272,256]{1,0:T(8,128)S(1)} %get-tuple-element.31.refs_3_), channel_id=1, source_target_pairs={{1,5},{5,1},{9,13},{13,9},{4,8},{8,4},{3,7},{7,3},{11,15},{15,11},... | collective-permute-start | bytes 835592 | tf_op jit(solution)/shard_map/ppermute | solution.py:472
  87.7 5.5 %collective-permute-start.13 = (f32[272,256]{1,0:T(8,128)S(1)}, f32[272,256]{1,0:T(8,128)S(1)}, u32[]{:S(2)}, u32[]{:S(2)}) collective-permute-start(f32[272,256]{1,0:T(8,128)S(1)} %get-tuple-element.31.refs_3_), channel_id=1, source_target_pairs={{1,2},{2,1},{5,6},{6,5},{9,10},{10,9},{13,14},{14,13},{17,18},{18,... | collective-permute-start | bytes 835592 | tf_op jit(solution)/shard_map/ppermute | solution.py:466
  88.4 6.0 %collective-permute-start.12 = (f32[272,256]{1,0:T(8,128)S(1)}, f32[272,256]{1,0:T(8,128)S(1)}, u32[]{:S(2)}, u32[]{:S(2)}) collective-permute-start(f32[272,256]{1,0:T(8,128)S(1)} %get-tuple-element.31.refs_3_), channel_id=1, source_target_pairs={{0,1},{1,0},{2,3},{3,2},{4,5},{5,4},{6,7},{7,6},{8,9},{9,8},{10,11... | collective-permute-start | bytes 835592 | tf_op jit(solution)/shard_map/ppermute | solution.py:386
  94.5 6.6 %collective-permute-start.18 = (f32[4,8,128]{2,1,0:T(8,128)S(1)}, f32[4,8,128]{2,1,0:T(8,128)S(1)}, u32[]{:S(2)}, u32[]{:S(2)}) collective-permute-start(f32[4,8,128]{2,1,0:T(8,128)S(1)} %pad_maximum_fusion.1), channel_id=1, source_target_pairs={{0,3},{1,2},{2,1},{3,0},{4,7},{5,6},{6,5},{7,4},{8,11},{9,10},{10,... | collective-permute-start | bytes 49160 | tf_op jit(solution)/shard_map/ppermute | solution.py:386
  96.3 6.7 %collective-permute-start.17 = (f32[4,8,128]{2,1,0:T(8,128)S(1)}, f32[4,8,128]{2,1,0:T(8,128)S(1)}, u32[]{:S(2)}, u32[]{:S(2)}) collective-permute-start(f32[4,8,128]{2,1,0:T(8,128)S(1)} %pad_maximum_fusion.1), channel_id=1, source_target_pairs={{0,2},{1,3},{2,0},{3,1},{4,6},{5,7},{6,4},{7,5},{8,10},{9,11},{10,... | collective-permute-start | bytes 49160 | tf_op jit(solution)/shard_map/ppermute | solution.py:386
  101.1 1.9 %collective-permute-start.16 = (f32[4,8,128]{2,1,0:T(8,128)S(1)}, f32[4,8,128]{2,1,0:T(8,128)S(1)}, u32[]{:S(2)}, u32[]{:S(2)}) collective-permute-start(f32[4,8,128]{2,1,0:T(8,128)S(1)} %pad_maximum_fusion.1), channel_id=1, source_target_pairs={{0,1},{1,0},{2,3},{3,2},{4,5},{5,4},{6,7},{7,6},{8,9},{9,8},{10,11... | collective-permute-start | bytes 49160 | tf_op jit(solution)/shard_map/ppermute | solution.py:386
  103.0 4.7 %collective-permute-start.19 = (f32[4,8,128]{2,1,0:T(8,128)S(1)}, f32[4,8,128]{2,1,0:T(8,128)S(1)}, u32[]{:S(2)}, u32[]{:S(2)}) collective-permute-start(f32[4,8,128]{2,1,0:T(8,128)S(1)} %pad_maximum_fusion.2.refs_0_), channel_id=1, source_target_pairs={{0,8},{4,12},{8,0},{12,4},{1,9},{5,13},{9,1},{13,5},{2,10},{6,14},... | collective-permute-start | bytes 49160 | tf_op jit(solution)/shard_map/ppermute | solution.py:481
  114.0 5.0 %collective-permute-start.21 = (bf16[2,128,256]{2,1,0:T(8,128)(2,1)S(1)}, bf16[2,128,256]{2,1,0:T(8,128)(2,1)S(1)}, u32[]{:S(2)}, u32[]{:S(2)}) collective-permute-start(bf16[2,128,256]{2,1,0:T(8,128)(2,1)S(1)} %get-tuple-element.39), channel_id=1, source_target_pairs={{0,2},{1,3},{2,0},{3,1},{4,6},{5,7},{6,4},{7,5},{8,10},{9,11},{10,... | collective-permute-start | bytes 393224 | tf_op jit(solution)/shard_map/ppermute | solution.py:386
  115.9 3.1 %collective-permute-start.20 = (bf16[2,128,256]{2,1,0:T(8,128)(2,1)S(1)}, bf16[2,128,256]{2,1,0:T(8,128)(2,1)S(1)}, u32[]{:S(2)}, u32[]{:S(2)}) collective-permute-start(bf16[2,128,256]{2,1,0:T(8,128)(2,1)S(1)} %get-tuple-element.38.mine), channel_id=1, source_target_pairs={{0,1},{1,0},{2,3},{3,2},{4,5},{5,4},{6,7},{7,6},{8,9},{9,8},{10,11... | collective-permute-start | bytes 393224 | tf_op jit(solution)/shard_map/ppermute | solution.py:386
  119.0 1.3 %collective-permute-start.22 = (bf16[2,128,256]{2,1,0:T(8,128)(2,1)S(1)}, bf16[2,128,256]{2,1,0:T(8,128)(2,1)S(1)}, u32[]{:S(2)}, u32[]{:S(2)}) collective-permute-start(bf16[2,128,256]{2,1,0:T(8,128)(2,1)S(1)} %collective-permute-done.21.across), channel_id=1, source_target_pairs={{0,1},{1,0},{2,3},{3,2},{4,5},{5,4},{6,7},{7,6},{8,9},{9,8},{10,11... | collective-permute-start | bytes 393224 | tf_op jit(solution)/shard_map/ppermute | solution.py:386

commit v5 on v4

--- a/solution.py
+++ b/solution.py
@@ -213,31 +213,31 @@
 
 
 def first_kernel(start, stop, last, info, *refs):
-    count = 6 if start else 5
-    here, refs = refs[:count], refs[count:]
+    here, refs = refs[:4], refs[4:]
+    source, refs = refs[0], refs[1:]
+    if start:
+        before, refs = refs[0], refs[1:]
     outs, (sems, kept, *bufs) = refs[: 3 if last else 1], refs[3 if last else 1 :]
-    own, core, side, diag, source = bufs[:5]
+    own, core, side, diag = bufs
     terms = here[0].shape[0]
     span = pl.ds(start, stop - start)
     until = fetch(
         [
-            (here[4], source),
             (here[0].at[span], own),
             (here[2], side),
             (here[1].at[span], core),
             (here[3], diag),
-        ]
-        + list(zip(here[5:], bufs[5:])),
+        ],
         sems,
     )
-    until(count)
+    until(4)
     items = []
     for n in range(stop - start):
         items.append((info[4 + start + n], own, side, n, n))
         items.append((info[4 + terms + start + n], core, diag, n, n))
     total = add_terms(items, source, kept, 4)
     if start:
-        total = total + bufs[5][...]
+        total = total + before[...]
     if not last:
         outs[0][...] = total
         return
@@ -301,27 +301,25 @@
 
 
 def second_kernel(entries, spans, info, *refs):
-    count = 12 + 2 * len(spans)
-    here, refs = refs[:count], refs[count:]
+    count = 4 + 2 * len(spans)
+    here, held, refs = refs[:count], refs[count : count + 8], refs[count + 8 :]
     (mine, theirs, ritz), (sems, second, kept), bufs = refs[:3], refs[3:6], refs[6:]
-    stats_a, stats_b, source, *blocks = bufs[:8]
-    own, core = bufs[10:12]
-    pairs = list(zip(here[:8], bufs[:8]))
-    before = len(pairs)
+    stats_a, stats_b, source, *blocks = held
+    own, core = bufs[:2]
+    pairs = []
     for n, (start, stop) in enumerate(spans):
         span = pl.ds(start, stop - start)
         pairs += [
-            (here[10].at[span], own.at[span]),
-            (here[11].at[span], core.at[span]),
-            (here[12 + 2 * n], bufs[12 + 2 * n]),
-            (here[13 + 2 * n], bufs[13 + 2 * n]),
+            (here[2].at[span], own.at[span]),
+            (here[3].at[span], core.at[span]),
+            (here[4 + 2 * n], bufs[2 + 2 * n]),
+            (here[5 + 2 * n], bufs[3 + 2 * n]),
         ]
-    pairs += [(here[8], mine.at[0]), (here[9], theirs.at[0])]
+    pairs += [(here[0], mine.at[0]), (here[1], theirs.at[0])]
     until = fetch(pairs, sems)
     terms = own.shape[0]
     across, parity, lower = info[0], info[2] % 2, info[3]
     half = mine.shape[1]
-    until(before)
     parts = merged(
         [stats_a[row] for row in range(4)],
         [stats_b[row] for row in range(4)],
@@ -341,8 +339,8 @@
     items = []
     for n, (start, stop) in enumerate(spans):
         for w in range(start, stop):
-            items.append((info[4 + w], own, bufs[12 + 2 * n], w, w - start))
-            items.append((info[4 + terms + w], core, bufs[13 + 2 * n], w, w - start))
+            items.append((info[4 + w], own, bufs[2 + 2 * n], w, w - start))
+            items.append((info[4 + terms + w], core, bufs[3 + 2 * n], w, w - start))
     until(len(pairs) - 2)
     total = add_terms(items, second, kept, 4)
     total = own_first(total, across)
@@ -353,19 +351,20 @@
     until(len(pairs))
 
 
-def whole_call(body, operands, out_shape, scratch, info, flops, name):
+def whole_call(body, operands, held, out_shape, scratch, info, flops, name):
     space = pl.BlockSpec(memory_space=pltpu.VMEM)
     return pl.pallas_call(
         body,
         in_specs=[pl.BlockSpec(memory_space=pltpu.SMEM)]
-        + [pl.BlockSpec(memory_space=pl.ANY)] * len(operands),
+        + [pl.BlockSpec(memory_space=pl.ANY)] * len(operands)
+        + [space] * len(held),
         out_specs=[space] * len(out_shape),
         out_shape=out_shape,
         scratch_shapes=scratch,
         compiler_params=pltpu.CompilerParams(vmem_limit_bytes=24 * 2**20),
         cost_estimate=pl.CostEstimate(flops=flops, bytes_accessed=flops // 256, transcendentals=0),
         name=name,
-    )(info, *operands)
+    )(info, *operands, *held)
 
 
 def room(array, count=None):
@@ -444,14 +443,14 @@
     for index, (start, stop) in enumerate(spans):
         last = stop == terms
         size = stop - start
-        operands = [own_env, core_env, *messages[2 * index : 2 * index + 2], source, *total]
+        operands = [own_env, core_env, *messages[2 * index : 2 * index + 2]]
         total = whole_call(
             functools.partial(first_kernel, start, stop, last),
             operands,
+            [source, *total],
             [sent, rows, rows] if last else [plain],
             [pltpu.SemaphoreType.DMA((len(operands),)), kept]
-            + [room(m, size) for m in operands[:4]]
-            + [room(m) for m in operands[4:]],
+            + [room(m, size) for m in operands],
             info,
             8 * size * width**3,
             f"first_terms_{start}",
@@ -483,10 +482,11 @@
         if flip < sectors:
             stats = merge_tiles(stats, pair)
 
-    operands = [stats, pair, source, *blocks, mine_one, theirs_one, own_env, core_env, *messages]
+    operands = [mine_one, theirs_one, own_env, core_env, *messages]
     mine, theirs, ritz = whole_call(
         functools.partial(second_kernel, float(sectors * slots * width * width), spans),
         operands,
+        [stats, pair, source, *blocks],
         [
             jax.ShapeDtypeStruct((2, half, width), jnp.bfloat16),
             jax.ShapeDtypeStruct((2, half, width), jnp.bfloat16),
@@ -497,7 +497,7 @@
             pltpu.VMEM((5, width, width), jnp.bfloat16),
             kept,
         ]
-        + [room(m) for m in operands],
+        + [room(m) for m in operands[2:]],
         info,
         8 * terms * width**3,
         "second_terms",

time: 122 us -> 121 us (level)
  no operation moved by 1% of the time
where the time goes in v5:
time: 121 us; the launch traced here: 120 us
  waiting for transfers between devices  58 us (48%)
  starting transfers between devices  32.8 us (27%)
  Pallas kernels  23.6 us (20%)
  local copies, waits for them, and re-layouts  3.05 us (3%)
  other arithmetic  2.1 us (2%)
    ppermute x17, waiting for transfers between devices, swap(): return lax.ppermute(array, cell, [(i, i ^ flip) for i in range(slots)])  51.3 us
    ppermute x17, starting transfers between devices, swap(): return lax.ppermute(array, cell, [(i, i ^ flip) for i in range(slots)])  22.9 us
    pallas_call x4, Pallas kernels, whole_call(): pl.pallas_call(body, in_specs=[pl.BlockSpec(memory_space=pltpu.SMEM)] + [...  15.1 us
    pallas_call x2, Pallas kernels, pack(): pl.pallas_call(functools.partial(pack_kernel, parts), in_specs=[pl.BlockS...  7.63 us
    ppermute x1, waiting for transfers between devices, on_device(): lax.ppermute(stats, 'sector', [(i, i ^ flip) for i in range(sectors)])  4.62 us
    ppermute x1, starting transfers between devices, on_device(): lax.ppermute(own, 'sector', even)  4.39 us
    ppermute x1, starting transfers between devices, on_device(): in_early = lax.ppermute(image_one, planes, turns[0])  3.48 us
  transfers between devices with their start and end apart: 23, of which 13 were waited for; matrix products, arithmetic and copies ran while one was open for 3% of the time, Pallas kernels for 12%

profile of v5, /device:TPU:0, one launch (start us, length us, event | category | flops | bytes accessed | tf_op | source)
XLA Modules:
  0.0 120.5 jit_solution(8436959754362557964)
XLA Ops:
  0.7 0.9 copy-done
  1.6 3.0 %collective-permute-start.1 = (bf16[3,64,256]{2,1,0:T(8,128)(2,1)S(1)}, bf16[3,64,256]{2,1,0:T(8,128)(2,1)S(1)}, u32[]{:S(2)}, u32[]{:S(2)}) collective-permute-start(bf16[3,64,256]{2,1,0:T(8,128)(2,1)S(1)} %dynamic-slice_bitcast_fusion.1), channel_id=1, source_target_pairs={{0,2},{1,3},{2,0},{3,1},{4,6},{5,7},{6,4},{7,5},{8,10},{9,11},{10,... | collective-permute-start | bytes 294920 | tf_op jit(solution)/shard_map/ppermute | solution.py:385
  4.6 2.5 %pack_0_2.1 = (bf16[6,512,128]{2,1,0:T(8,128)(2,1)}, bf16[6,512,128]{2,1,0:T(8,128)(2,1)}) custom-call(bf16[13,1,4,128,256]{4,3,2,1,0:T(8,128)(2,1)} %left_env.3, bf16[13,1,4,256,128]{4,3,2,1,0:T(8,128)(2,1)} %right_env.3), custom_call_target="tpu_custom_call" | custom-call | bytes 3145728 | tf_op jit(solution)/shard_map/pack_0_2/pallas_call | solution.py:145
  7.2 0.9 collective-permute-start.11
  8.8 5.2 %pack_6_6.1 = (bf16[5,512,128]{2,1,0:T(8,128)(2,1)}, bf16[5,512,128]{2,1,0:T(8,128)(2,1)}, bf16[2,512,128]{2,1,0:T(8,128)(2,1)}, bf16[2,512,128]{2,1,0:T(8,128)(...) custom-call(bf16[13,1,4,128,256]{4,3,2,1,0:T(8,128)(2,1)} %left_env.3, ...), custom_call_target="tpu_custom_call" | custom-call | bytes 10485760 | tf_op jit(solution)/shard_map/pack_6_6/pallas_call | solution.py:145
  14.0 1.3 %collective-permute-start.2 = (bf16[13,512,128]{2,1,0:T(8,128)(2,1)}, bf16[13,512,128]{2,1,0:T(8,128)(2,1)}, u32[]{:S(2)}, u32[]{:S(2)}) collective-permute-start(bf16[13,512,128]{2,1,0:T(8,128)(2,1)} %get-tuple-element.26), channel_id=1, source_target_pairs={{0,1},{1,0},{2,3},{3,2},{4,5},{5,4},{6,7},{7,6},{8,9},{9,8},{10,11... | collective-permute-start | bytes 5111816 | tf_op jit(solution)/shard_map/ppermute | solution.py:385
  15.4 3.3 %collective-permute-done.5 = bf16[3,64,256]{2,1,0:T(8,128)(2,1)S(1)} collective-permute-done((bf16[3,64,256]{2,1,0:T(8,128)(2,1)}, bf16[3,64,256]{2,1,0:T(8,128)(2,1)S(1)}, u32[]{:S(2)}, u32[]{:S(2)}) %collective-permute-start.5) | collective-permute-done | bytes 98336 | tf_op jit(solution)/shard_map/ppermute | solution.py:385
  18.7 0.9 broadcast_select_fusion.1
  21.4 1.0 collective-permute-done
  22.4 4.4 %collective-permute-start.6 = (bf16[256,256]{1,0:T(8,128)(2,1)}, bf16[256,256]{1,0:T(8,128)(2,1)S(1)}, u32[]{:S(2)}, u32[]{:S(2)}) collective-permute-start(bf16[256,256]{1,0:T(8,128)(2,1)} %get-tuple-element.49), channel_id=1, source_target_pairs={{0,4},{4,0},{8,12},{12,8},{1,5},{5,1},{9,13},{13,9},{2,6},{6,2},{1... | collective-permute-start | bytes 393224 | tf_op jit(solution)/shard_map/ppermute | solution.py:427
  28.8 2.0 %collective-permute-done.6 = bf16[256,256]{1,0:T(8,128)(2,1)S(1)} collective-permute-done((bf16[256,256]{1,0:T(8,128)(2,1)}, bf16[256,256]{1,0:T(8,128)(2,1)S(1)}, u32[]{:S(2)}, u32[]{:S(2)}) %collective-permute-start.6) | collective-permute-done | bytes 131104 | tf_op jit(solution)/shard_map/ppermute | solution.py:427
  31.0 1.5 %collective-permute-start.3 = (bf16[2,512,128]{2,1,0:T(8,128)(2,1)}, bf16[2,512,128]{2,1,0:T(8,128)(2,1)S(1)}, u32[]{:S(2)}, u32[]{:S(2)}) collective-permute-start(bf16[2,512,128]{2,1,0:T(8,128)(2,1)} %get-tuple-element.27), channel_id=1, source_target_pairs={{0,2},{1,3},{2,0},{3,1},{4,6},{5,7},{6,4},{7,5},{8,10},{9,11},{10,... | collective-permute-start | bytes 786440 | tf_op jit(solution)/shard_map/ppermute | solution.py:385
  32.5 9.8 %collective-permute-done.11.refs_3_.refs_5_ = bf16[6,512,128]{2,1,0:T(8,128)(2,1)} collective-permute-done((bf16[6,512,128]{2,1,0:T(8,128)(2,1)}, bf16[6,512,128]{2,1,0:T(8,128)(2,1)}, u32[]{:S(2)}, u32[]{:S(2)}) %collective-permute-start.11) | collective-permute-done | bytes 786464 | tf_op jit(solution)/shard_map/ppermute | solution.py:385
  42.3 1.9 %collective-permute-start.4 = (bf16[2,512,128]{2,1,0:T(8,128)(2,1)}, bf16[2,512,128]{2,1,0:T(8,128)(2,1)S(1)}, u32[]{:S(2)}, u32[]{:S(2)}) collective-permute-start(bf16[2,512,128]{2,1,0:T(8,128)(2,1)} %get-tuple-element.28), channel_id=1, source_target_pairs={{0,3},{1,2},{2,1},{3,0},{4,7},{5,6},{6,5},{7,4},{8,11},{9,10},{10,... | collective-permute-start | bytes 786440 | tf_op jit(solution)/shard_map/ppermute | solution.py:385
  44.2 3.7 %first_terms_0.1.refs_5_ = f32[256,256]{1,0:T(8,128)S(1)} custom-call(s32[30]{0:T(128)S(1)} %concatenate.9.info, bf16[13,512,128]{2,1,0:T(8,128)(2,1)S(1)} %copy-done.1, bf16[13,512,128]{2,1,0:T(8,128)(2,1)} %collective-permute-done.2.refs_1_.refs_3_, bf16[6,512,128]{2,1,0:T(8,128)(2,1)} %collective-permute-done.10.refs_2_.refs_4_, ...), custom_call_target="tpu_custom_call" | custom-call | flops 805306368 | bytes 3145728 | tf_op jit(solution)/shard_map/first_terms_0/pallas_call | solution.py:356
  47.9 10.8 %collective-permute-done.8.refs_2_.refs_6_ = bf16[5,512,128]{2,1,0:T(8,128)(2,1)S(1)} collective-permute-done((bf16[5,512,128]{2,1,0:T(8,128)(2,1)}, bf16[5,512,128]{2,1,0:T(8,128)(2,1)S(1)}, u32[]{:S(2)}, u32[]{:S(2)}) %collective-permute-start.8) | collective-permute-done | bytes 655392 | tf_op jit(solution)/shard_map/ppermute | solution.py:385
  58.7 11.7 %collective-permute-done.9.refs_3_.refs_7_ = bf16[5,512,128]{2,1,0:T(8,128)(2,1)S(1)} collective-permute-done((bf16[5,512,128]{2,1,0:T(8,128)(2,1)}, bf16[5,512,128]{2,1,0:T(8,128)(2,1)S(1)}, u32[]{:S(2)}, u32[]{:S(2)}) %collective-permute-start.9) | collective-permute-done | bytes 655392 | tf_op jit(solution)/shard_map/ppermute | solution.py:385
  70.4 3.4 %first_terms_6.1.refs_5_ = f32[256,256]{1,0:T(8,128)S(1)} custom-call(s32[30]{0:T(128)S(1)} %concatenate.9.info, bf16[13,512,128]{2,1,0:T(8,128)(2,1)S(1)} %copy-done.1, bf16[13,512,128]{2,1,0:T(8,128)(2,1)} %collective-permute-done.2.refs_1_.refs_3_, bf16[5,512,128]{2,1,0:T(8,128)(2,1)S(1)} %collective-permute-done.8.refs_2_.refs_6_, ...), custom_call_target="tpu_custom_call" | custom-call | flops 671088640 | bytes 2621440 | tf_op jit(solution)/shard_map/first_terms_6/pallas_call | solution.py:356
  73.8 4.6 %collective-permute-done.3.refs_2_.refs_8_ = bf16[2,512,128]{2,1,0:T(8,128)(2,1)S(1)} collective-permute-done((bf16[2,512,128]{2,1,0:T(8,128)(2,1)}, bf16[2,512,128]{2,1,0:T(8,128)(2,1)S(1)}, u32[]{:S(2)}, u32[]{:S(2)}) %collective-permute-start.3) | collective-permute-done | bytes 262176 | tf_op jit(solution)/shard_map/ppermute | solution.py:385
  78.4 2.7 %collective-permute-done.4.refs_3_.refs_9_ = bf16[2,512,128]{2,1,0:T(8,128)(2,1)S(1)} collective-permute-done((bf16[2,512,128]{2,1,0:T(8,128)(2,1)}, bf16[2,512,128]{2,1,0:T(8,128)(2,1)S(1)}, u32[]{:S(2)}, u32[]{:S(2)}) %collective-permute-start.4) | collective-permute-done | bytes 262176 | tf_op jit(solution)/shard_map/ppermute | solution.py:385
  81.0 2.3 %first_terms_11.1 = (f32[272,256]{1,0:T(8,128)S(1)}, bf16[128,256]{1,0:T(8,128)(2,1)S(1)}, bf16[128,256]{1,0:T(8,128)(2,1)S(1)}) custom-call(s32[30]{0:T(128)S(1)} %concatenate.9.info, bf16[13,512,128]{2,1,0:T(8,128)(2,1)S(1)} %copy-done.1, bf16[13,512,128]{2,1,0:T(8,128)(2,1)} %collective-permute-done.2.refs_1_.refs_3_, ...), custom_call_target="tpu_custom_call" | custom-call | flops 268435456 | bytes 1048576 | tf_op jit(solution)/shard_map/first_terms_11/pallas_call | solution.py:356
  83.4 3.5 %collective-permute-start.15 = (f32[272,256]{1,0:T(8,128)S(1)}, f32[272,256]{1,0:T(8,128)S(1)}, u32[]{:S(2)}, u32[]{:S(2)}) collective-permute-start(f32[272,256]{1,0:T(8,128)S(1)} %get-tuple-element.33.refs_13_), channel_id=1, source_target_pairs={{0,4},{4,0},{8,12},{12,8},{5,9},{9,5},{2,6},{6,2},{10,14},{14,10},... | collective-permute-start | bytes 835592 | tf_op jit(solution)/shard_map/ppermute | solution.py:472
  88.2 4.8 %collective-permute-start.12 = (f32[272,256]{1,0:T(8,128)S(1)}, f32[272,256]{1,0:T(8,128)S(1)}, u32[]{:S(2)}, u32[]{:S(2)}) collective-permute-start(f32[272,256]{1,0:T(8,128)S(1)} %get-tuple-element.33.refs_13_), channel_id=1, source_target_pairs={{0,1},{1,0},{2,3},{3,2},{4,5},{5,4},{6,7},{7,6},{8,9},{9,8},{10,11... | collective-permute-start | bytes 835592 | tf_op jit(solution)/shard_map/ppermute | solution.py:385
  93.1 1.2 collective-permute-done.12.refs_16_
  94.3 1.8 %collective-permute-start.18 = (f32[4,8,128]{2,1,0:T(8,128)S(1)}, f32[4,8,128]{2,1,0:T(8,128)S(1)}, u32[]{:S(2)}, u32[]{:S(2)}) collective-permute-start(f32[4,8,128]{2,1,0:T(8,128)S(1)} %pad_maximum_fusion.1), channel_id=1, source_target_pairs={{0,3},{1,2},{2,1},{3,0},{4,7},{5,6},{6,5},{7,4},{8,11},{9,10},{10,... | collective-permute-start | bytes 49160 | tf_op jit(solution)/shard_map/ppermute | solution.py:385
  96.1 4.8 %collective-permute-start.17 = (f32[4,8,128]{2,1,0:T(8,128)S(1)}, f32[4,8,128]{2,1,0:T(8,128)S(1)}, u32[]{:S(2)}, u32[]{:S(2)}) collective-permute-start(f32[4,8,128]{2,1,0:T(8,128)S(1)} %pad_maximum_fusion.1), channel_id=1, source_target_pairs={{0,2},{1,3},{2,0},{3,1},{4,6},{5,7},{6,4},{7,5},{8,10},{9,11},{10,... | collective-permute-start | bytes 49160 | tf_op jit(solution)/shard_map/ppermute | solution.py:385
  100.9 1.9 %collective-permute-done.17 = f32[4,8,128]{2,1,0:T(8,128)S(1)} collective-permute-done((f32[4,8,128]{2,1,0:T(8,128)S(1)}, f32[4,8,128]{2,1,0:T(8,128)S(1)}, u32[]{:S(2)}, u32[]{:S(2)}) %collective-permute-start.17) | collective-permute-done | bytes 16416 | tf_op jit(solution)/shard_map/ppermute | solution.py:385
  102.9 4.6 %collective-permute-done.19.refs_11_ = f32[4,8,128]{2,1,0:T(8,128)S(1)} collective-permute-done((f32[4,8,128]{2,1,0:T(8,128)S(1)}, f32[4,8,128]{2,1,0:T(8,128)S(1)}, u32[]{:S(2)}, u32[]{:S(2)}) %collective-permute-start.19) | collective-permute-done | bytes 16416 | tf_op jit(solution)/shard_map/ppermute | solution.py:480
  107.5 5.7 %second_terms.1 = (bf16[2,128,256]{2,1,0:T(8,128)(2,1)S(1)}, bf16[2,128,256]{2,1,0:T(8,128)(2,1)S(1)}, f32[1,1]{1,0:T(1,128)}) custom-call(s32[30]{0:T(128)S(1)} %concatenate.9.info, bf16[128,256]{1,0:T(8,128)(2,1)S(1)} %get-tuple-element.31.refs_0_, bf16[128,256]{1,0:T(8,128)(2,1)S(1)} %get-tuple-element.32.refs_1_, bf16[13,512,128]{2,1,0:T(8,128)(2,1)S(1)} %copy-done.1, ...), custom_call_target="tpu_custom_call" | custom-call | flops 1744830464 | bytes 6815744 | tf_op jit(solution)/shard_map/second_terms/pallas_call | solution.py:356
  113.3 1.9 %collective-permute-start.21 = (bf16[2,128,256]{2,1,0:T(8,128)(2,1)S(1)}, bf16[2,128,256]{2,1,0:T(8,128)(2,1)S(1)}, u32[]{:S(2)}, u32[]{:S(2)}) collective-permute-start(bf16[2,128,256]{2,1,0:T(8,128)(2,1)S(1)} %get-tuple-element.39), channel_id=1, source_target_pairs={{0,2},{1,3},{2,0},{3,1},{4,6},{5,7},{6,4},{7,5},{8,10},{9,11},{10,... | collective-permute-start | bytes 393224 | tf_op jit(solution)/shard_map/ppermute | solution.py:385
  115.2 3.1 %collective-permute-done.21.across = bf16[2,128,256]{2,1,0:T(8,128)(2,1)S(1)} collective-permute-done((bf16[2,128,256]{2,1,0:T(8,128)(2,1)S(1)}, bf16[2,128,256]{2,1,0:T(8,128)(2,1)S(1)}, u32[]{:S(2)}, u32[]{:S(2)}) %collective-permute-start.21) | collective-permute-done | bytes 131104 | tf_op jit(solution)/shard_map/ppermute | solution.py:385
  118.3 1.3 %collective-permute-done.22.far = bf16[2,128,256]{2,1,0:T(8,128)(2,1)S(1)} collective-permute-done((bf16[2,128,256]{2,1,0:T(8,128)(2,1)S(1)}, bf16[2,128,256]{2,1,0:T(8,128)(2,1)S(1)}, u32[]{:S(2)}, u32[]{:S(2)}) %collective-permute-start.22) | collective-permute-done | bytes 131104 | tf_op jit(solution)/shard_map/ppermute | solution.py:385
  (55 shorter events, 7.2 us)
Async XLA Ops:
  0.6 1.0 copy-start
  1.6 6.5 %copy-start.4 = (s32[1,4]{1,0:T(1,128)S(1)}, s32[1,4]{1,0:T(1,128)}, u32[]{:S(2)}) copy-start(s32[1,4]{1,0:T(1,128)} %param.6) | copy-start | bytes 52
  1.6 6.5 %collective-permute-start.1 = (bf16[3,64,256]{2,1,0:T(8,128)(2,1)S(1)}, bf16[3,64,256]{2,1,0:T(8,128)(2,1)S(1)}, u32[]{:S(2)}, u32[]{:S(2)}) collective-permute-start(bf16[3,64,256]{2,1,0:T(8,128)(2,1)S(1)} %dynamic-slice_bitcast_fusion.1), channel_id=1, source_target_pairs={{0,2},{1,3},{2,0},{3,1},{4,6},{5,7},{6,4},{7,5},{8,10},{9,11},{10,... | collective-permute-start | bytes 294920 | tf_op jit(solution)/shard_map/ppermute | solution.py:385
  7.1 23.9 %collective-permute-start.10 = (bf16[6,512,128]{2,1,0:T(8,128)(2,1)}, bf16[6,512,128]{2,1,0:T(8,128)(2,1)}, u32[]{:S(2)}, u32[]{:S(2)}) collective-permute-start(bf16[6,512,128]{2,1,0:T(8,128)(2,1)} %get-tuple-element.23.refs_0_), channel_id=1, source_target_pairs={{0,2},{1,3},{2,0},{3,1},{4,6},{5,7},{6,4},{7,5},{8,10},{9,11},{10,... | collective-permute-start | bytes 2359304 | tf_op jit(solution)/shard_map/ppermute | solution.py:385
  7.2 35.1 %collective-permute-start.11 = (bf16[6,512,128]{2,1,0:T(8,128)(2,1)}, bf16[6,512,128]{2,1,0:T(8,128)(2,1)}, u32[]{:S(2)}, u32[]{:S(2)}) collective-permute-start(bf16[6,512,128]{2,1,0:T(8,128)(2,1)} %get-tuple-element.24.refs_1_), channel_id=1, source_target_pairs={{0,3},{1,2},{2,1},{3,0},{4,7},{5,6},{6,5},{7,4},{8,11},{9,10},{10,... | collective-permute-start | bytes 2359304 | tf_op jit(solution)/shard_map/ppermute | solution.py:385
  8.1 0.6 copy-start.2
  13.9 7.3 %copy-start.3 = (s32[13]{0:T(128)S(1)}, s32[13]{0:T(128)}, u32[]{:S(2)}) copy-start(s32[13]{0:T(128)} %param.9) | copy-start | bytes 160
  14.0 30.3 %collective-permute-start.2 = (bf16[13,512,128]{2,1,0:T(8,128)(2,1)}, bf16[13,512,128]{2,1,0:T(8,128)(2,1)}, u32[]{:S(2)}, u32[]{:S(2)}) collective-permute-start(bf16[13,512,128]{2,1,0:T(8,128)(2,1)} %get-tuple-element.26), channel_id=1, source_target_pairs={{0,1},{1,0},{2,3},{3,2},{4,5},{5,4},{6,7},{7,6},{8,9},{9,8},{10,11... | collective-permute-start | bytes 5111816 | tf_op jit(solution)/shard_map/ppermute | solution.py:385
  15.3 3.4 %collective-permute-start.5 = (bf16[3,64,256]{2,1,0:T(8,128)(2,1)}, bf16[3,64,256]{2,1,0:T(8,128)(2,1)S(1)}, u32[]{:S(2)}, u32[]{:S(2)}) collective-permute-start(bf16[3,64,256]{2,1,0:T(8,128)(2,1)} %copy-done.2), channel_id=1, source_target_pairs={{0,1},{1,0},{2,3},{3,2},{4,5},{5,4},{6,7},{7,6},{8,9},{9,8},{10,11... | collective-permute-start | bytes 294920 | tf_op jit(solution)/shard_map/ppermute | solution.py:385
  19.8 24.4 %copy-start.1 = (bf16[13,512,128]{2,1,0:T(8,128)(2,1)S(1)}, bf16[13,512,128]{2,1,0:T(8,128)(2,1)}, u32[]{:S(2)}) copy-start(bf16[13,512,128]{2,1,0:T(8,128)(2,1)} %get-tuple-element.25.refs_0_.refs_2_) | copy-start | bytes 5111812
  20.5 7.7 %collective-permute-start.7 = (bf16[256,256]{1,0:T(8,128)(2,1)}, bf16[256,256]{1,0:T(8,128)(2,1)S(1)}, u32[]{:S(2)}, u32[]{:S(2)}) collective-permute-start(bf16[256,256]{1,0:T(8,128)(2,1)} %get-tuple-element.49), channel_id=1, source_target_pairs={{4,8},{8,4},{5,9},{9,5},{6,10},{10,6},{7,11},{11,7},{20,24},{24,20... | collective-permute-start | bytes 393224 | tf_op jit(solution)/shard_map/ppermute | solution.py:427
  21.2 1.2 collective-permute-start
  22.4 8.5 %collective-permute-start.6 = (bf16[256,256]{1,0:T(8,128)(2,1)}, bf16[256,256]{1,0:T(8,128)(2,1)S(1)}, u32[]{:S(2)}, u32[]{:S(2)}) collective-permute-start(bf16[256,256]{1,0:T(8,128)(2,1)} %get-tuple-element.49), channel_id=1, source_target_pairs={{0,4},{4,0},{8,12},{12,8},{1,5},{5,1},{9,13},{13,9},{2,6},{6,2},{1... | collective-permute-start | bytes 393224 | tf_op jit(solution)/shard_map/ppermute | solution.py:427
  28.2 30.5 %collective-permute-start.8 = (bf16[5,512,128]{2,1,0:T(8,128)(2,1)}, bf16[5,512,128]{2,1,0:T(8,128)(2,1)S(1)}, u32[]{:S(2)}, u32[]{:S(2)}) collective-permute-start(bf16[5,512,128]{2,1,0:T(8,128)(2,1)} %get-tuple-element.29), channel_id=1, source_target_pairs={{0,2},{1,3},{2,0},{3,1},{4,6},{5,7},{6,4},{7,5},{8,10},{9,11},{10,... | collective-permute-start | bytes 1966088 | tf_op jit(solution)/shard_map/ppermute | solution.py:385
  30.9 39.5 %collective-permute-start.9 = (bf16[5,512,128]{2,1,0:T(8,128)(2,1)}, bf16[5,512,128]{2,1,0:T(8,128)(2,1)S(1)}, u32[]{:S(2)}, u32[]{:S(2)}) collective-permute-start(bf16[5,512,128]{2,1,0:T(8,128)(2,1)} %get-tuple-element.30), channel_id=1, source_target_pairs={{0,3},{1,2},{2,1},{3,0},{4,7},{5,6},{6,5},{7,4},{8,11},{9,10},{10,... | collective-permute-start | bytes 1966088 | tf_op jit(solution)/shard_map/ppermute | solution.py:385
  31.0 47.4 %collective-permute-start.3 = (bf16[2,512,128]{2,1,0:T(8,128)(2,1)}, bf16[2,512,128]{2,1,0:T(8,128)(2,1)S(1)}, u32[]{:S(2)}, u32[]{:S(2)}) collective-permute-start(bf16[2,512,128]{2,1,0:T(8,128)(2,1)} %get-tuple-element.27), channel_id=1, source_target_pairs={{0,2},{1,3},{2,0},{3,1},{4,6},{5,7},{6,4},{7,5},{8,10},{9,11},{10,... | collective-permute-start | bytes 786440 | tf_op jit(solution)/shard_map/ppermute | solution.py:385
  42.3 38.8 %collective-permute-start.4 = (bf16[2,512,128]{2,1,0:T(8,128)(2,1)}, bf16[2,512,128]{2,1,0:T(8,128)(2,1)S(1)}, u32[]{:S(2)}, u32[]{:S(2)}) collective-permute-start(bf16[2,512,128]{2,1,0:T(8,128)(2,1)} %get-tuple-element.28), channel_id=1, source_target_pairs={{0,3},{1,2},{2,1},{3,0},{4,7},{5,6},{6,5},{7,4},{8,11},{9,10},{10,... | collective-permute-start | bytes 786440 | tf_op jit(solution)/shard_map/ppermute | solution.py:385
  83.4 9.7 %collective-permute-start.15 = (f32[272,256]{1,0:T(8,128)S(1)}, f32[272,256]{1,0:T(8,128)S(1)}, u32[]{:S(2)}, u32[]{:S(2)}) collective-permute-start(f32[272,256]{1,0:T(8,128)S(1)} %get-tuple-element.33.refs_13_), channel_id=1, source_target_pairs={{0,4},{4,0},{8,12},{12,8},{5,9},{9,5},{2,6},{6,2},{10,14},{14,10},... | collective-permute-start | bytes 835592 | tf_op jit(solution)/shard_map/ppermute | solution.py:472
  86.8 6.2 %collective-permute-start.14 = (f32[272,256]{1,0:T(8,128)S(1)}, f32[272,256]{1,0:T(8,128)S(1)}, u32[]{:S(2)}, u32[]{:S(2)}) collective-permute-start(f32[272,256]{1,0:T(8,128)S(1)} %get-tuple-element.33.refs_13_), channel_id=1, source_target_pairs={{1,5},{5,1},{9,13},{13,9},{4,8},{8,4},{3,7},{7,3},{11,15},{15,11},... | collective-permute-start | bytes 835592 | tf_op jit(solution)/shard_map/ppermute | solution.py:471
  87.5 5.5 %collective-permute-start.13 = (f32[272,256]{1,0:T(8,128)S(1)}, f32[272,256]{1,0:T(8,128)S(1)}, u32[]{:S(2)}, u32[]{:S(2)}) collective-permute-start(f32[272,256]{1,0:T(8,128)S(1)} %get-tuple-element.33.refs_13_), channel_id=1, source_target_pairs={{1,2},{2,1},{5,6},{6,5},{9,10},{10,9},{13,14},{14,13},{17,18},{18,... | collective-permute-start | bytes 835592 | tf_op jit(solution)/shard_map/ppermute | solution.py:465
  88.2 6.0 %collective-permute-start.12 = (f32[272,256]{1,0:T(8,128)S(1)}, f32[272,256]{1,0:T(8,128)S(1)}, u32[]{:S(2)}, u32[]{:S(2)}) collective-permute-start(f32[272,256]{1,0:T(8,128)S(1)} %get-tuple-element.33.refs_13_), channel_id=1, source_target_pairs={{0,1},{1,0},{2,3},{3,2},{4,5},{5,4},{6,7},{7,6},{8,9},{9,8},{10,11... | collective-permute-start | bytes 835592 | tf_op jit(solution)/shard_map/ppermute | solution.py:385
  94.3 6.6 %collective-permute-start.18 = (f32[4,8,128]{2,1,0:T(8,128)S(1)}, f32[4,8,128]{2,1,0:T(8,128)S(1)}, u32[]{:S(2)}, u32[]{:S(2)}) collective-permute-start(f32[4,8,128]{2,1,0:T(8,128)S(1)} %pad_maximum_fusion.1), channel_id=1, source_target_pairs={{0,3},{1,2},{2,1},{3,0},{4,7},{5,6},{6,5},{7,4},{8,11},{9,10},{10,... | collective-permute-start | bytes 49160 | tf_op jit(solution)/shard_map/ppermute | solution.py:385
  96.1 6.7 %collective-permute-start.17 = (f32[4,8,128]{2,1,0:T(8,128)S(1)}, f32[4,8,128]{2,1,0:T(8,128)S(1)}, u32[]{:S(2)}, u32[]{:S(2)}) collective-permute-start(f32[4,8,128]{2,1,0:T(8,128)S(1)} %pad_maximum_fusion.1), channel_id=1, source_target_pairs={{0,2},{1,3},{2,0},{3,1},{4,6},{5,7},{6,4},{7,5},{8,10},{9,11},{10,... | collective-permute-start | bytes 49160 | tf_op jit(solution)/shard_map/ppermute | solution.py:385
  100.9 1.9 %collective-permute-start.16 = (f32[4,8,128]{2,1,0:T(8,128)S(1)}, f32[4,8,128]{2,1,0:T(8,128)S(1)}, u32[]{:S(2)}, u32[]{:S(2)}) collective-permute-start(f32[4,8,128]{2,1,0:T(8,128)S(1)} %pad_maximum_fusion.1), channel_id=1, source_target_pairs={{0,1},{1,0},{2,3},{3,2},{4,5},{5,4},{6,7},{7,6},{8,9},{9,8},{10,11... | collective-permute-start | bytes 49160 | tf_op jit(solution)/shard_map/ppermute | solution.py:385
  102.8 4.7 %collective-permute-start.19 = (f32[4,8,128]{2,1,0:T(8,128)S(1)}, f32[4,8,128]{2,1,0:T(8,128)S(1)}, u32[]{:S(2)}, u32[]{:S(2)}) collective-permute-start(f32[4,8,128]{2,1,0:T(8,128)S(1)} %pad_maximum_fusion.2.refs_10_), channel_id=1, source_target_pairs={{0,8},{4,12},{8,0},{12,4},{1,9},{5,13},{9,1},{13,5},{2,10},{6,14},... | collective-permute-start | bytes 49160 | tf_op jit(solution)/shard_map/ppermute | solution.py:480
  113.3 5.0 %collective-permute-start.21 = (bf16[2,128,256]{2,1,0:T(8,128)(2,1)S(1)}, bf16[2,128,256]{2,1,0:T(8,128)(2,1)S(1)}, u32[]{:S(2)}, u32[]{:S(2)}) collective-permute-start(bf16[2,128,256]{2,1,0:T(8,128)(2,1)S(1)} %get-tuple-element.39), channel_id=1, source_target_pairs={{0,2},{1,3},{2,0},{3,1},{4,6},{5,7},{6,4},{7,5},{8,10},{9,11},{10,... | collective-permute-start | bytes 393224 | tf_op jit(solution)/shard_map/ppermute | solution.py:385
  115.2 3.1 %collective-permute-start.20 = (bf16[2,128,256]{2,1,0:T(8,128)(2,1)S(1)}, bf16[2,128,256]{2,1,0:T(8,128)(2,1)S(1)}, u32[]{:S(2)}, u32[]{:S(2)}) collective-permute-start(bf16[2,128,256]{2,1,0:T(8,128)(2,1)S(1)} %get-tuple-element.38.mine), channel_id=1, source_target_pairs={{0,1},{1,0},{2,3},{3,2},{4,5},{5,4},{6,7},{7,6},{8,9},{9,8},{10,11... | collective-permute-start | bytes 393224 | tf_op jit(solution)/shard_map/ppermute | solution.py:385
  118.3 1.3 %collective-permute-start.22 = (bf16[2,128,256]{2,1,0:T(8,128)(2,1)S(1)}, bf16[2,128,256]{2,1,0:T(8,128)(2,1)S(1)}, u32[]{:S(2)}, u32[]{:S(2)}) collective-permute-start(bf16[2,128,256]{2,1,0:T(8,128)(2,1)S(1)} %collective-permute-done.21.across), channel_id=1, source_target_pairs={{0,1},{1,0},{2,3},{3,2},{4,5},{5,4},{6,7},{7,6},{8,9},{9,8},{10,11... | collective-permute-start | bytes 393224 | tf_op jit(solution)/shard_map/ppermute | solution.py:385

commit v6 on v5

--- a/solution.py
+++ b/solution.py
@@ -470,7 +470,7 @@
     ]
     in_late = lax.ppermute(image_one, planes, turns[1])
     in_early = lax.ppermute(image_one, planes, turns[0])
-    near, beyond, in_late, in_early = lax.optimization_barrier((near, beyond, in_late, in_early))
+    near, in_late, beyond, in_early = lax.optimization_barrier((near, in_late, beyond, in_early))
     even_sums = jnp.where(core == 0, in_early[width:], in_late[width:])
     stats = merge_tiles(sums_of(image_one[width:]), sums_of(even_sums))
     stats = merge_tiles(merge_tiles(stats, swap(stats, 1)), merge_tiles(swap(stats, 2), swap(stats, 3)))

time: 121 us -> 119 us (0.983)
  waiting for transfers between devices: 58 us -> 55.7 us
    ppermute x1, starting transfers between devices: 0.07 us -> 2.36 us  [on_device(): lax.ppermute(stats, 'sector', [(i, i ^ flip) for i in range(sectors)])]
    ppermute x1, waiting for transfers between devices: 4.62 us -> 2.34 us  [on_device(): lax.ppermute(stats, 'sector', [(i, i ^ flip) for i in range(sectors)])]
    ppermute x17, starting transfers between devices: 22.9 us -> 21.3 us  [swap(): return lax.ppermute(array, cell, [(i, i ^ flip) for i in range(slots)])]
where the time goes in v6:
time: 119 us
  waiting for transfers between devices  55.7 us (47%)
  starting transfers between devices  33.6 us (28%)
  Pallas kernels  23.6 us (20%)
  local copies, waits for them, and re-layouts  3.05 us (3%)
  other arithmetic  2.1 us (2%)
    ppermute x17, waiting for transfers between devices, swap(): return lax.ppermute(array, cell, [(i, i ^ flip) for i in range(slots)])  51.3 us
    ppermute x17, starting transfers between devices, swap(): return lax.ppermute(array, cell, [(i, i ^ flip) for i in range(slots)])  21.3 us
    pallas_call x4, Pallas kernels, whole_call(): pl.pallas_call(body, in_specs=[pl.BlockSpec(memory_space=pltpu.SMEM)] + [...  15.1 us
    pallas_call x2, Pallas kernels, pack(): pl.pallas_call(functools.partial(pack_kernel, parts), in_specs=[pl.BlockS...  7.63 us
    ppermute x1, starting transfers between devices, on_device(): lax.ppermute(own, 'sector', even)  4.39 us
    ppermute x1, starting transfers between devices, on_device(): in_early = lax.ppermute(image_one, planes, turns[0])  3.48 us
  transfers between devices with their start and end apart: 23, of which 13 were waited for; matrix products, arithmetic and copies ran while one was open for 3% of the time, Pallas kernels for 12%

profile of v6, /device:TPU:0, one launch (start us, length us, event | category | flops | bytes accessed | tf_op | source)
XLA Modules:
  0.0 119.0 jit_solution(14824334571008085405)
XLA Ops:
  0.7 0.9 copy-done
  1.6 3.0 %collective-permute-start.1 = (bf16[3,64,256]{2,1,0:T(8,128)(2,1)S(1)}, bf16[3,64,256]{2,1,0:T(8,128)(2,1)S(1)}, u32[]{:S(2)}, u32[]{:S(2)}) collective-permute-start(bf16[3,64,256]{2,1,0:T(8,128)(2,1)S(1)} %dynamic-slice_bitcast_fusion.1), channel_id=1, source_target_pairs={{0,2},{1,3},{2,0},{3,1},{4,6},{5,7},{6,4},{7,5},{8,10},{9,11},{10,... | collective-permute-start | bytes 294920 | tf_op jit(solution)/shard_map/ppermute | solution.py:385
  4.6 2.5 %pack_0_2.1 = (bf16[6,512,128]{2,1,0:T(8,128)(2,1)}, bf16[6,512,128]{2,1,0:T(8,128)(2,1)}) custom-call(bf16[13,1,4,128,256]{4,3,2,1,0:T(8,128)(2,1)} %left_env.3, bf16[13,1,4,256,128]{4,3,2,1,0:T(8,128)(2,1)} %right_env.3), custom_call_target="tpu_custom_call" | custom-call | bytes 3145728 | tf_op jit(solution)/shard_map/pack_0_2/pallas_call | solution.py:145
  8.8 5.2 %pack_6_6.1 = (bf16[5,512,128]{2,1,0:T(8,128)(2,1)}, bf16[5,512,128]{2,1,0:T(8,128)(2,1)}, bf16[2,512,128]{2,1,0:T(8,128)(2,1)}, bf16[2,512,128]{2,1,0:T(8,128)(...) custom-call(bf16[13,1,4,128,256]{4,3,2,1,0:T(8,128)(2,1)} %left_env.3, ...), custom_call_target="tpu_custom_call" | custom-call | bytes 10485760 | tf_op jit(solution)/shard_map/pack_6_6/pallas_call | solution.py:145
  14.0 1.3 %collective-permute-start.2 = (bf16[13,512,128]{2,1,0:T(8,128)(2,1)}, bf16[13,512,128]{2,1,0:T(8,128)(2,1)}, u32[]{:S(2)}, u32[]{:S(2)}) collective-permute-start(bf16[13,512,128]{2,1,0:T(8,128)(2,1)} %get-tuple-element.26), channel_id=1, source_target_pairs={{0,1},{1,0},{2,3},{3,2},{4,5},{5,4},{6,7},{7,6},{8,9},{9,8},{10,11... | collective-permute-start | bytes 5111816 | tf_op jit(solution)/shard_map/ppermute | solution.py:385
  15.4 3.3 %collective-permute-done.5 = bf16[3,64,256]{2,1,0:T(8,128)(2,1)S(1)} collective-permute-done((bf16[3,64,256]{2,1,0:T(8,128)(2,1)}, bf16[3,64,256]{2,1,0:T(8,128)(2,1)S(1)}, u32[]{:S(2)}, u32[]{:S(2)}) %collective-permute-start.5) | collective-permute-done | bytes 98336 | tf_op jit(solution)/shard_map/ppermute | solution.py:385
  18.7 0.9 broadcast_select_fusion.1
  21.4 1.0 collective-permute-done
  22.4 4.4 %collective-permute-start.6 = (bf16[256,256]{1,0:T(8,128)(2,1)}, bf16[256,256]{1,0:T(8,128)(2,1)S(1)}, u32[]{:S(2)}, u32[]{:S(2)}) collective-permute-start(bf16[256,256]{1,0:T(8,128)(2,1)} %get-tuple-element.49), channel_id=1, source_target_pairs={{0,4},{4,0},{8,12},{12,8},{1,5},{5,1},{9,13},{13,9},{2,6},{6,2},{1... | collective-permute-start | bytes 393224 | tf_op jit(solution)/shard_map/ppermute | solution.py:427
  28.8 2.0 %collective-permute-done.6 = bf16[256,256]{1,0:T(8,128)(2,1)S(1)} collective-permute-done((bf16[256,256]{1,0:T(8,128)(2,1)}, bf16[256,256]{1,0:T(8,128)(2,1)S(1)}, u32[]{:S(2)}, u32[]{:S(2)}) %collective-permute-start.6) | collective-permute-done | bytes 131104 | tf_op jit(solution)/shard_map/ppermute | solution.py:427
  31.0 1.5 %collective-permute-start.3 = (bf16[2,512,128]{2,1,0:T(8,128)(2,1)}, bf16[2,512,128]{2,1,0:T(8,128)(2,1)S(1)}, u32[]{:S(2)}, u32[]{:S(2)}) collective-permute-start(bf16[2,512,128]{2,1,0:T(8,128)(2,1)} %get-tuple-element.27), channel_id=1, source_target_pairs={{0,2},{1,3},{2,0},{3,1},{4,6},{5,7},{6,4},{7,5},{8,10},{9,11},{10,... | collective-permute-start | bytes 786440 | tf_op jit(solution)/shard_map/ppermute | solution.py:385
  32.5 9.8 %collective-permute-done.11.refs_3_.refs_5_ = bf16[6,512,128]{2,1,0:T(8,128)(2,1)} collective-permute-done((bf16[6,512,128]{2,1,0:T(8,128)(2,1)}, bf16[6,512,128]{2,1,0:T(8,128)(2,1)}, u32[]{:S(2)}, u32[]{:S(2)}) %collective-permute-start.11) | collective-permute-done | bytes 786464 | tf_op jit(solution)/shard_map/ppermute | solution.py:385
  42.3 1.9 %collective-permute-start.4 = (bf16[2,512,128]{2,1,0:T(8,128)(2,1)}, bf16[2,512,128]{2,1,0:T(8,128)(2,1)S(1)}, u32[]{:S(2)}, u32[]{:S(2)}) collective-permute-start(bf16[2,512,128]{2,1,0:T(8,128)(2,1)} %get-tuple-element.28), channel_id=1, source_target_pairs={{0,3},{1,2},{2,1},{3,0},{4,7},{5,6},{6,5},{7,4},{8,11},{9,10},{10,... | collective-permute-start | bytes 786440 | tf_op jit(solution)/shard_map/ppermute | solution.py:385
  44.2 3.7 %first_terms_0.1.refs_5_ = f32[256,256]{1,0:T(8,128)S(1)} custom-call(s32[30]{0:T(128)S(1)} %concatenate.9.info, bf16[13,512,128]{2,1,0:T(8,128)(2,1)S(1)} %copy-done.1, bf16[13,512,128]{2,1,0:T(8,128)(2,1)} %collective-permute-done.2.refs_1_.refs_3_, bf16[6,512,128]{2,1,0:T(8,128)(2,1)} %collective-permute-done.10.refs_2_.refs_4_, ...), custom_call_target="tpu_custom_call" | custom-call | flops 805306368 | bytes 3145728 | tf_op jit(solution)/shard_map/first_terms_0/pallas_call | solution.py:356
  47.9 10.8 %collective-permute-done.8.refs_2_.refs_6_ = bf16[5,512,128]{2,1,0:T(8,128)(2,1)S(1)} collective-permute-done((bf16[5,512,128]{2,1,0:T(8,128)(2,1)}, bf16[5,512,128]{2,1,0:T(8,128)(2,1)S(1)}, u32[]{:S(2)}, u32[]{:S(2)}) %collective-permute-start.8) | collective-permute-done | bytes 655392 | tf_op jit(solution)/shard_map/ppermute | solution.py:385
  58.7 11.7 %collective-permute-done.9.refs_3_.refs_7_ = bf16[5,512,128]{2,1,0:T(8,128)(2,1)S(1)} collective-permute-done((bf16[5,512,128]{2,1,0:T(8,128)(2,1)}, bf16[5,512,128]{2,1,0:T(8,128)(2,1)S(1)}, u32[]{:S(2)}, u32[]{:S(2)}) %collective-permute-start.9) | collective-permute-done | bytes 655392 | tf_op jit(solution)/shard_map/ppermute | solution.py:385
  70.4 3.4 %first_terms_6.1.refs_5_ = f32[256,256]{1,0:T(8,128)S(1)} custom-call(s32[30]{0:T(128)S(1)} %concatenate.9.info, bf16[13,512,128]{2,1,0:T(8,128)(2,1)S(1)} %copy-done.1, bf16[13,512,128]{2,1,0:T(8,128)(2,1)} %collective-permute-done.2.refs_1_.refs_3_, bf16[5,512,128]{2,1,0:T(8,128)(2,1)S(1)} %collective-permute-done.8.refs_2_.refs_6_, ...), custom_call_target="tpu_custom_call" | custom-call | flops 671088640 | bytes 2621440 | tf_op jit(solution)/shard_map/first_terms_6/pallas_call | solution.py:356
  73.8 4.6 %collective-permute-done.3.refs_2_.refs_8_ = bf16[2,512,128]{2,1,0:T(8,128)(2,1)S(1)} collective-permute-done((bf16[2,512,128]{2,1,0:T(8,128)(2,1)}, bf16[2,512,128]{2,1,0:T(8,128)(2,1)S(1)}, u32[]{:S(2)}, u32[]{:S(2)}) %collective-permute-start.3) | collective-permute-done | bytes 262176 | tf_op jit(solution)/shard_map/ppermute | solution.py:385
  78.4 2.7 %collective-permute-done.4.refs_3_.refs_9_ = bf16[2,512,128]{2,1,0:T(8,128)(2,1)S(1)} collective-permute-done((bf16[2,512,128]{2,1,0:T(8,128)(2,1)}, bf16[2,512,128]{2,1,0:T(8,128)(2,1)S(1)}, u32[]{:S(2)}, u32[]{:S(2)}) %collective-permute-start.4) | collective-permute-done | bytes 262176 | tf_op jit(solution)/shard_map/ppermute | solution.py:385
  81.0 2.3 %first_terms_11.1 = (f32[272,256]{1,0:T(8,128)S(1)}, bf16[128,256]{1,0:T(8,128)(2,1)S(1)}, bf16[128,256]{1,0:T(8,128)(2,1)S(1)}) custom-call(s32[30]{0:T(128)S(1)} %concatenate.9.info, bf16[13,512,128]{2,1,0:T(8,128)(2,1)S(1)} %copy-done.1, bf16[13,512,128]{2,1,0:T(8,128)(2,1)} %collective-permute-done.2.refs_1_.refs_3_, ...), custom_call_target="tpu_custom_call" | custom-call | flops 268435456 | bytes 1048576 | tf_op jit(solution)/shard_map/first_terms_11/pallas_call | solution.py:356
  83.4 3.5 %collective-permute-start.15 = (f32[272,256]{1,0:T(8,128)S(1)}, f32[272,256]{1,0:T(8,128)S(1)}, u32[]{:S(2)}, u32[]{:S(2)}) collective-permute-start(f32[272,256]{1,0:T(8,128)S(1)} %get-tuple-element.33.refs_13_), channel_id=1, source_target_pairs={{0,4},{4,0},{8,12},{12,8},{5,9},{9,5},{2,6},{6,2},{10,14},{14,10},... | collective-permute-start | bytes 835592 | tf_op jit(solution)/shard_map/ppermute | solution.py:472
  88.2 4.8 %collective-permute-start.12 = (f32[272,256]{1,0:T(8,128)S(1)}, f32[272,256]{1,0:T(8,128)S(1)}, u32[]{:S(2)}, u32[]{:S(2)}) collective-permute-start(f32[272,256]{1,0:T(8,128)S(1)} %get-tuple-element.33.refs_13_), channel_id=1, source_target_pairs={{0,1},{1,0},{2,3},{3,2},{4,5},{5,4},{6,7},{7,6},{8,9},{9,8},{10,11... | collective-permute-start | bytes 835592 | tf_op jit(solution)/shard_map/ppermute | solution.py:385
  93.1 1.2 collective-permute-done.12.refs_16_
  94.3 1.6 %collective-permute-start.18 = (f32[4,8,128]{2,1,0:T(8,128)S(1)}, f32[4,8,128]{2,1,0:T(8,128)S(1)}, u32[]{:S(2)}, u32[]{:S(2)}) collective-permute-start(f32[4,8,128]{2,1,0:T(8,128)S(1)} %pad_maximum_fusion.1), channel_id=1, source_target_pairs={{0,3},{1,2},{2,1},{3,0},{4,7},{5,6},{6,5},{7,4},{8,11},{9,10},{10,... | collective-permute-start | bytes 49160 | tf_op jit(solution)/shard_map/ppermute | solution.py:385
  95.9 3.4 %collective-permute-start.17 = (f32[4,8,128]{2,1,0:T(8,128)S(1)}, f32[4,8,128]{2,1,0:T(8,128)S(1)}, u32[]{:S(2)}, u32[]{:S(2)}) collective-permute-start(f32[4,8,128]{2,1,0:T(8,128)S(1)} %pad_maximum_fusion.1), channel_id=1, source_target_pairs={{0,2},{1,3},{2,0},{3,1},{4,6},{5,7},{6,4},{7,5},{8,10},{9,11},{10,... | collective-permute-start | bytes 49160 | tf_op jit(solution)/shard_map/ppermute | solution.py:385
  99.3 1.9 %collective-permute-done.17 = f32[4,8,128]{2,1,0:T(8,128)S(1)} collective-permute-done((f32[4,8,128]{2,1,0:T(8,128)S(1)}, f32[4,8,128]{2,1,0:T(8,128)S(1)}, u32[]{:S(2)}, u32[]{:S(2)}) %collective-permute-start.17) | collective-permute-done | bytes 16416 | tf_op jit(solution)/shard_map/ppermute | solution.py:385
  101.3 2.4 %collective-permute-start.19 = (f32[4,8,128]{2,1,0:T(8,128)S(1)}, f32[4,8,128]{2,1,0:T(8,128)S(1)}, u32[]{:S(2)}, u32[]{:S(2)}) collective-permute-start(f32[4,8,128]{2,1,0:T(8,128)S(1)} %pad_maximum_fusion.2.refs_10_), channel_id=1, source_target_pairs={{0,8},{4,12},{8,0},{12,4},{1,9},{5,13},{9,1},{13,5},{2,10},{6,14},... | collective-permute-start | bytes 49160 | tf_op jit(solution)/shard_map/ppermute | solution.py:480
  103.6 2.3 %collective-permute-done.19.refs_11_ = f32[4,8,128]{2,1,0:T(8,128)S(1)} collective-permute-done((f32[4,8,128]{2,1,0:T(8,128)S(1)}, f32[4,8,128]{2,1,0:T(8,128)S(1)}, u32[]{:S(2)}, u32[]{:S(2)}) %collective-permute-start.19) | collective-permute-done | bytes 16416 | tf_op jit(solution)/shard_map/ppermute | solution.py:480
  106.0 5.7 %second_terms.1 = (bf16[2,128,256]{2,1,0:T(8,128)(2,1)S(1)}, bf16[2,128,256]{2,1,0:T(8,128)(2,1)S(1)}, f32[1,1]{1,0:T(1,128)}) custom-call(s32[30]{0:T(128)S(1)} %concatenate.9.info, bf16[128,256]{1,0:T(8,128)(2,1)S(1)} %get-tuple-element.31.refs_0_, bf16[128,256]{1,0:T(8,128)(2,1)S(1)} %get-tuple-element.32.refs_1_, bf16[13,512,128]{2,1,0:T(8,128)(2,1)S(1)} %copy-done.1, ...), custom_call_target="tpu_custom_call" | custom-call | flops 1744830464 | bytes 6815744 | tf_op jit(solution)/shard_map/second_terms/pallas_call | solution.py:356
  111.7 1.9 %collective-permute-start.21 = (bf16[2,128,256]{2,1,0:T(8,128)(2,1)S(1)}, bf16[2,128,256]{2,1,0:T(8,128)(2,1)S(1)}, u32[]{:S(2)}, u32[]{:S(2)}) collective-permute-start(bf16[2,128,256]{2,1,0:T(8,128)(2,1)S(1)} %get-tuple-element.39), channel_id=1, source_target_pairs={{0,2},{1,3},{2,0},{3,1},{4,6},{5,7},{6,4},{7,5},{8,10},{9,11},{10,... | collective-permute-start | bytes 393224 | tf_op jit(solution)/shard_map/ppermute | solution.py:385
  113.7 3.1 %collective-permute-done.21.across = bf16[2,128,256]{2,1,0:T(8,128)(2,1)S(1)} collective-permute-done((bf16[2,128,256]{2,1,0:T(8,128)(2,1)S(1)}, bf16[2,128,256]{2,1,0:T(8,128)(2,1)S(1)}, u32[]{:S(2)}, u32[]{:S(2)}) %collective-permute-start.21) | collective-permute-done | bytes 131104 | tf_op jit(solution)/shard_map/ppermute | solution.py:385
  116.8 1.3 %collective-permute-done.22.far = bf16[2,128,256]{2,1,0:T(8,128)(2,1)S(1)} collective-permute-done((bf16[2,128,256]{2,1,0:T(8,128)(2,1)S(1)}, bf16[2,128,256]{2,1,0:T(8,128)(2,1)S(1)}, u32[]{:S(2)}, u32[]{:S(2)}) %collective-permute-start.22) | collective-permute-done | bytes 131104 | tf_op jit(solution)/shard_map/ppermute | solution.py:385
  (55 shorter events, 8.0 us)
Async XLA Ops:
  0.6 1.0 copy-start
  1.6 6.5 %copy-start.4 = (s32[1,4]{1,0:T(1,128)S(1)}, s32[1,4]{1,0:T(1,128)}, u32[]{:S(2)}) copy-start(s32[1,4]{1,0:T(1,128)} %param.6) | copy-start | bytes 52
  1.6 6.5 %collective-permute-start.1 = (bf16[3,64,256]{2,1,0:T(8,128)(2,1)S(1)}, bf16[3,64,256]{2,1,0:T(8,128)(2,1)S(1)}, u32[]{:S(2)}, u32[]{:S(2)}) collective-permute-start(bf16[3,64,256]{2,1,0:T(8,128)(2,1)S(1)} %dynamic-slice_bitcast_fusion.1), channel_id=1, source_target_pairs={{0,2},{1,3},{2,0},{3,1},{4,6},{5,7},{6,4},{7,5},{8,10},{9,11},{10,... | collective-permute-start | bytes 294920 | tf_op jit(solution)/shard_map/ppermute | solution.py:385
  7.1 23.9 %collective-permute-start.10 = (bf16[6,512,128]{2,1,0:T(8,128)(2,1)}, bf16[6,512,128]{2,1,0:T(8,128)(2,1)}, u32[]{:S(2)}, u32[]{:S(2)}) collective-permute-start(bf16[6,512,128]{2,1,0:T(8,128)(2,1)} %get-tuple-element.23.refs_0_), channel_id=1, source_target_pairs={{0,2},{1,3},{2,0},{3,1},{4,6},{5,7},{6,4},{7,5},{8,10},{9,11},{10,... | collective-permute-start | bytes 2359304 | tf_op jit(solution)/shard_map/ppermute | solution.py:385
  7.2 35.1 %collective-permute-start.11 = (bf16[6,512,128]{2,1,0:T(8,128)(2,1)}, bf16[6,512,128]{2,1,0:T(8,128)(2,1)}, u32[]{:S(2)}, u32[]{:S(2)}) collective-permute-start(bf16[6,512,128]{2,1,0:T(8,128)(2,1)} %get-tuple-element.24.refs_1_), channel_id=1, source_target_pairs={{0,3},{1,2},{2,1},{3,0},{4,7},{5,6},{6,5},{7,4},{8,11},{9,10},{10,... | collective-permute-start | bytes 2359304 | tf_op jit(solution)/shard_map/ppermute | solution.py:385
  8.1 0.6 copy-start.2
  13.9 7.3 %copy-start.3 = (s32[13]{0:T(128)S(1)}, s32[13]{0:T(128)}, u32[]{:S(2)}) copy-start(s32[13]{0:T(128)} %param.9) | copy-start | bytes 160
  14.0 30.3 %collective-permute-start.2 = (bf16[13,512,128]{2,1,0:T(8,128)(2,1)}, bf16[13,512,128]{2,1,0:T(8,128)(2,1)}, u32[]{:S(2)}, u32[]{:S(2)}) collective-permute-start(bf16[13,512,128]{2,1,0:T(8,128)(2,1)} %get-tuple-element.26), channel_id=1, source_target_pairs={{0,1},{1,0},{2,3},{3,2},{4,5},{5,4},{6,7},{7,6},{8,9},{9,8},{10,11... | collective-permute-start | bytes 5111816 | tf_op jit(solution)/shard_map/ppermute | solution.py:385
  15.3 3.4 %collective-permute-start.5 = (bf16[3,64,256]{2,1,0:T(8,128)(2,1)}, bf16[3,64,256]{2,1,0:T(8,128)(2,1)S(1)}, u32[]{:S(2)}, u32[]{:S(2)}) collective-permute-start(bf16[3,64,256]{2,1,0:T(8,128)(2,1)} %copy-done.2), channel_id=1, source_target_pairs={{0,1},{1,0},{2,3},{3,2},{4,5},{5,4},{6,7},{7,6},{8,9},{9,8},{10,11... | collective-permute-start | bytes 294920 | tf_op jit(solution)/shard_map/ppermute | solution.py:385
  19.8 24.4 %copy-start.1 = (bf16[13,512,128]{2,1,0:T(8,128)(2,1)S(1)}, bf16[13,512,128]{2,1,0:T(8,128)(2,1)}, u32[]{:S(2)}) copy-start(bf16[13,512,128]{2,1,0:T(8,128)(2,1)} %get-tuple-element.25.refs_0_.refs_2_) | copy-start | bytes 5111812
  20.5 7.7 %collective-permute-start.7 = (bf16[256,256]{1,0:T(8,128)(2,1)}, bf16[256,256]{1,0:T(8,128)(2,1)S(1)}, u32[]{:S(2)}, u32[]{:S(2)}) collective-permute-start(bf16[256,256]{1,0:T(8,128)(2,1)} %get-tuple-element.49), channel_id=1, source_target_pairs={{4,8},{8,4},{5,9},{9,5},{6,10},{10,6},{7,11},{11,7},{20,24},{24,20... | collective-permute-start | bytes 393224 | tf_op jit(solution)/shard_map/ppermute | solution.py:427
  21.2 1.2 collective-permute-start
  22.4 8.5 %collective-permute-start.6 = (bf16[256,256]{1,0:T(8,128)(2,1)}, bf16[256,256]{1,0:T(8,128)(2,1)S(1)}, u32[]{:S(2)}, u32[]{:S(2)}) collective-permute-start(bf16[256,256]{1,0:T(8,128)(2,1)} %get-tuple-element.49), channel_id=1, source_target_pairs={{0,4},{4,0},{8,12},{12,8},{1,5},{5,1},{9,13},{13,9},{2,6},{6,2},{1... | collective-permute-start | bytes 393224 | tf_op jit(solution)/shard_map/ppermute | solution.py:427
  28.2 30.5 %collective-permute-start.8 = (bf16[5,512,128]{2,1,0:T(8,128)(2,1)}, bf16[5,512,128]{2,1,0:T(8,128)(2,1)S(1)}, u32[]{:S(2)}, u32[]{:S(2)}) collective-permute-start(bf16[5,512,128]{2,1,0:T(8,128)(2,1)} %get-tuple-element.29), channel_id=1, source_target_pairs={{0,2},{1,3},{2,0},{3,1},{4,6},{5,7},{6,4},{7,5},{8,10},{9,11},{10,... | collective-permute-start | bytes 1966088 | tf_op jit(solution)/shard_map/ppermute | solution.py:385
  30.9 39.5 %collective-permute-start.9 = (bf16[5,512,128]{2,1,0:T(8,128)(2,1)}, bf16[5,512,128]{2,1,0:T(8,128)(2,1)S(1)}, u32[]{:S(2)}, u32[]{:S(2)}) collective-permute-start(bf16[5,512,128]{2,1,0:T(8,128)(2,1)} %get-tuple-element.30), channel_id=1, source_target_pairs={{0,3},{1,2},{2,1},{3,0},{4,7},{5,6},{6,5},{7,4},{8,11},{9,10},{10,... | collective-permute-start | bytes 1966088 | tf_op jit(solution)/shard_map/ppermute | solution.py:385
  31.0 47.4 %collective-permute-start.3 = (bf16[2,512,128]{2,1,0:T(8,128)(2,1)}, bf16[2,512,128]{2,1,0:T(8,128)(2,1)S(1)}, u32[]{:S(2)}, u32[]{:S(2)}) collective-permute-start(bf16[2,512,128]{2,1,0:T(8,128)(2,1)} %get-tuple-element.27), channel_id=1, source_target_pairs={{0,2},{1,3},{2,0},{3,1},{4,6},{5,7},{6,4},{7,5},{8,10},{9,11},{10,... | collective-permute-start | bytes 786440 | tf_op jit(solution)/shard_map/ppermute | solution.py:385
  42.3 38.8 %collective-permute-start.4 = (bf16[2,512,128]{2,1,0:T(8,128)(2,1)}, bf16[2,512,128]{2,1,0:T(8,128)(2,1)S(1)}, u32[]{:S(2)}, u32[]{:S(2)}) collective-permute-start(bf16[2,512,128]{2,1,0:T(8,128)(2,1)} %get-tuple-element.28), channel_id=1, source_target_pairs={{0,3},{1,2},{2,1},{3,0},{4,7},{5,6},{6,5},{7,4},{8,11},{9,10},{10,... | collective-permute-start | bytes 786440 | tf_op jit(solution)/shard_map/ppermute | solution.py:385
  83.4 9.7 %collective-permute-start.15 = (f32[272,256]{1,0:T(8,128)S(1)}, f32[272,256]{1,0:T(8,128)S(1)}, u32[]{:S(2)}, u32[]{:S(2)}) collective-permute-start(f32[272,256]{1,0:T(8,128)S(1)} %get-tuple-element.33.refs_13_), channel_id=1, source_target_pairs={{0,4},{4,0},{8,12},{12,8},{5,9},{9,5},{2,6},{6,2},{10,14},{14,10},... | collective-permute-start | bytes 835592 | tf_op jit(solution)/shard_map/ppermute | solution.py:472
  86.8 6.2 %collective-permute-start.14 = (f32[272,256]{1,0:T(8,128)S(1)}, f32[272,256]{1,0:T(8,128)S(1)}, u32[]{:S(2)}, u32[]{:S(2)}) collective-permute-start(f32[272,256]{1,0:T(8,128)S(1)} %get-tuple-element.33.refs_13_), channel_id=1, source_target_pairs={{1,2},{2,1},{5,6},{6,5},{9,10},{10,9},{13,14},{14,13},{17,18},{18,... | collective-permute-start | bytes 835592 | tf_op jit(solution)/shard_map/ppermute | solution.py:465
  87.5 5.5 %collective-permute-start.13 = (f32[272,256]{1,0:T(8,128)S(1)}, f32[272,256]{1,0:T(8,128)S(1)}, u32[]{:S(2)}, u32[]{:S(2)}) collective-permute-start(f32[272,256]{1,0:T(8,128)S(1)} %get-tuple-element.33.refs_13_), channel_id=1, source_target_pairs={{1,5},{5,1},{9,13},{13,9},{4,8},{8,4},{3,7},{7,3},{11,15},{15,11},... | collective-permute-start | bytes 835592 | tf_op jit(solution)/shard_map/ppermute | solution.py:471
  88.2 6.0 %collective-permute-start.12 = (f32[272,256]{1,0:T(8,128)S(1)}, f32[272,256]{1,0:T(8,128)S(1)}, u32[]{:S(2)}, u32[]{:S(2)}) collective-permute-start(f32[272,256]{1,0:T(8,128)S(1)} %get-tuple-element.33.refs_13_), channel_id=1, source_target_pairs={{0,1},{1,0},{2,3},{3,2},{4,5},{5,4},{6,7},{7,6},{8,9},{9,8},{10,11... | collective-permute-start | bytes 835592 | tf_op jit(solution)/shard_map/ppermute | solution.py:385
  94.3 5.1 %collective-permute-start.18 = (f32[4,8,128]{2,1,0:T(8,128)S(1)}, f32[4,8,128]{2,1,0:T(8,128)S(1)}, u32[]{:S(2)}, u32[]{:S(2)}) collective-permute-start(f32[4,8,128]{2,1,0:T(8,128)S(1)} %pad_maximum_fusion.1), channel_id=1, source_target_pairs={{0,3},{1,2},{2,1},{3,0},{4,7},{5,6},{6,5},{7,4},{8,11},{9,10},{10,... | collective-permute-start | bytes 49160 | tf_op jit(solution)/shard_map/ppermute | solution.py:385
  95.9 5.3 %collective-permute-start.17 = (f32[4,8,128]{2,1,0:T(8,128)S(1)}, f32[4,8,128]{2,1,0:T(8,128)S(1)}, u32[]{:S(2)}, u32[]{:S(2)}) collective-permute-start(f32[4,8,128]{2,1,0:T(8,128)S(1)} %pad_maximum_fusion.1), channel_id=1, source_target_pairs={{0,2},{1,3},{2,0},{3,1},{4,6},{5,7},{6,4},{7,5},{8,10},{9,11},{10,... | collective-permute-start | bytes 49160 | tf_op jit(solution)/shard_map/ppermute | solution.py:385
  99.3 1.9 %collective-permute-start.16 = (f32[4,8,128]{2,1,0:T(8,128)S(1)}, f32[4,8,128]{2,1,0:T(8,128)S(1)}, u32[]{:S(2)}, u32[]{:S(2)}) collective-permute-start(f32[4,8,128]{2,1,0:T(8,128)S(1)} %pad_maximum_fusion.1), channel_id=1, source_target_pairs={{0,1},{1,0},{2,3},{3,2},{4,5},{5,4},{6,7},{7,6},{8,9},{9,8},{10,11... | collective-permute-start | bytes 49160 | tf_op jit(solution)/shard_map/ppermute | solution.py:385
  101.3 4.7 %collective-permute-start.19 = (f32[4,8,128]{2,1,0:T(8,128)S(1)}, f32[4,8,128]{2,1,0:T(8,128)S(1)}, u32[]{:S(2)}, u32[]{:S(2)}) collective-permute-start(f32[4,8,128]{2,1,0:T(8,128)S(1)} %pad_maximum_fusion.2.refs_10_), channel_id=1, source_target_pairs={{0,8},{4,12},{8,0},{12,4},{1,9},{5,13},{9,1},{13,5},{2,10},{6,14},... | collective-permute-start | bytes 49160 | tf_op jit(solution)/shard_map/ppermute | solution.py:480
  111.7 5.0 %collective-permute-start.21 = (bf16[2,128,256]{2,1,0:T(8,128)(2,1)S(1)}, bf16[2,128,256]{2,1,0:T(8,128)(2,1)S(1)}, u32[]{:S(2)}, u32[]{:S(2)}) collective-permute-start(bf16[2,128,256]{2,1,0:T(8,128)(2,1)S(1)} %get-tuple-element.39), channel_id=1, source_target_pairs={{0,2},{1,3},{2,0},{3,1},{4,6},{5,7},{6,4},{7,5},{8,10},{9,11},{10,... | collective-permute-start | bytes 393224 | tf_op jit(solution)/shard_map/ppermute | solution.py:385
  113.7 3.1 %collective-permute-start.20 = (bf16[2,128,256]{2,1,0:T(8,128)(2,1)S(1)}, bf16[2,128,256]{2,1,0:T(8,128)(2,1)S(1)}, u32[]{:S(2)}, u32[]{:S(2)}) collective-permute-start(bf16[2,128,256]{2,1,0:T(8,128)(2,1)S(1)} %get-tuple-element.38.mine), channel_id=1, source_target_pairs={{0,1},{1,0},{2,3},{3,2},{4,5},{5,4},{6,7},{7,6},{8,9},{9,8},{10,11... | collective-permute-start | bytes 393224 | tf_op jit(solution)/shard_map/ppermute | solution.py:385
  116.8 1.3 %collective-permute-start.22 = (bf16[2,128,256]{2,1,0:T(8,128)(2,1)S(1)}, bf16[2,128,256]{2,1,0:T(8,128)(2,1)S(1)}, u32[]{:S(2)}, u32[]{:S(2)}) collective-permute-start(bf16[2,128,256]{2,1,0:T(8,128)(2,1)S(1)} %collective-permute-done.21.across), channel_id=1, source_target_pairs={{0,1},{1,0},{2,3},{3,2},{4,5},{5,4},{6,7},{7,6},{8,9},{9,8},{10,11... | collective-permute-start | bytes 393224 | tf_op jit(solution)/shard_map/ppermute | solution.py:385

commit v7 on v6

--- a/solution.py
+++ b/solution.py
@@ -282,11 +282,11 @@
     return rest + (2.0 * off * (product - own * squares) + off * off * squares)
 
 
-def spread_kernel(mine, near, across, far, first, second):
+def spread_kernel(*refs):
     me = lax.axis_index("contr") * 2 + lax.axis_index("mpo")
-    for flip, piece in enumerate((mine, near, across, far)):
-        first[0, me ^ flip] = piece[0]
-        second[0, me ^ flip] = piece[1]
+    for flip in range(4):
+        refs[8][0, me ^ flip] = refs[flip][...]
+        refs[9][0, me ^ flip] = refs[4 + flip][...]
 
 
 def merged(*stats):
@@ -301,7 +301,7 @@
 
 
 def second_kernel(entries, spans, info, *refs):
-    count = 4 + 2 * len(spans)
+    count = 2 + 2 * len(spans)
     here, held, refs = refs[:count], refs[count : count + 8], refs[count + 8 :]
     (mine, theirs, ritz), (sems, second, kept), bufs = refs[:3], refs[3:6], refs[6:]
     stats_a, stats_b, source, *blocks = held
@@ -310,16 +310,15 @@
     for n, (start, stop) in enumerate(spans):
         span = pl.ds(start, stop - start)
         pairs += [
-            (here[2].at[span], own.at[span]),
-            (here[3].at[span], core.at[span]),
-            (here[4 + 2 * n], bufs[2 + 2 * n]),
-            (here[5 + 2 * n], bufs[3 + 2 * n]),
+            (here[0].at[span], own.at[span]),
+            (here[1].at[span], core.at[span]),
+            (here[2 + 2 * n], bufs[2 + 2 * n]),
+            (here[3 + 2 * n], bufs[3 + 2 * n]),
         ]
-    pairs += [(here[0], mine.at[0]), (here[1], theirs.at[0])]
     until = fetch(pairs, sems)
     terms = own.shape[0]
     across, parity, lower = info[0], info[2] % 2, info[3]
-    half = mine.shape[1]
+    half = mine.shape[0]
     parts = merged(
         [stats_a[row] for row in range(4)],
         [stats_b[row] for row in range(4)],
@@ -341,14 +340,13 @@
         for w in range(start, stop):
             items.append((info[4 + w], own, bufs[2 + 2 * n], w, w - start))
             items.append((info[4 + terms + w], core, bufs[3 + 2 * n], w, w - start))
-    until(len(pairs) - 2)
+    until(len(pairs))
     total = add_terms(items, second, kept, 4)
     total = own_first(total, across)
     live = live_block(total.shape, across * half, info[1])
     block = jnp.where(live, total, 0.0).astype(jnp.bfloat16)
-    mine[1] = block[:half]
-    theirs[1] = block[half:]
-    until(len(pairs))
+    mine[...] = block[:half]
+    theirs[...] = block[half:]
 
 
 def whole_call(body, operands, held, out_shape, scratch, info, flops, name):
@@ -470,7 +468,7 @@
     ]
     in_late = lax.ppermute(image_one, planes, turns[1])
     in_early = lax.ppermute(image_one, planes, turns[0])
-    near, in_late, beyond, in_early = lax.optimization_barrier((near, in_late, beyond, in_early))
+    in_early, beyond, in_late, near = lax.optimization_barrier((in_early, beyond, in_late, near))
     even_sums = jnp.where(core == 0, in_early[width:], in_late[width:])
     stats = merge_tiles(sums_of(image_one[width:]), sums_of(even_sums))
     stats = merge_tiles(merge_tiles(stats, swap(stats, 1)), merge_tiles(swap(stats, 2), swap(stats, 3)))
@@ -482,14 +480,14 @@
         if flip < sectors:
             stats = merge_tiles(stats, pair)
 
-    operands = [mine_one, theirs_one, own_env, core_env, *messages]
+    operands = [own_env, core_env, *messages]
     mine, theirs, ritz = whole_call(
         functools.partial(second_kernel, float(sectors * slots * width * width), spans),
         operands,
         [stats, pair, source, *blocks],
         [
-            jax.ShapeDtypeStruct((2, half, width), jnp.bfloat16),
-            jax.ShapeDtypeStruct((2, half, width), jnp.bfloat16),
+            rows,
+            rows,
             jax.ShapeDtypeStruct((1, 1), jnp.float32),
         ],
         [
@@ -497,19 +495,21 @@
             pltpu.VMEM((5, width, width), jnp.bfloat16),
             kept,
         ]
-        + [room(m) for m in operands[2:]],
+        + [room(m) for m in operands],
         info,
         8 * terms * width**3,
         "second_terms",
     )
 
-    got = [mine, swap(mine, 1), swap(theirs, 2)]
-    got.append(swap(got[2], 1))
+    got = []
+    for near_half, far_half in ((mine_one, theirs_one), (mine, theirs)):
+        arrived = swap(far_half, 2)
+        got += [near_half, swap(near_half, 1), arrived, swap(arrived, 1)]
     image = jax.ShapeDtypeStruct((1, slots, half, width), jnp.bfloat16)
     space = pl.BlockSpec(memory_space=pltpu.VMEM)
     first_image, second_image = pl.pallas_call(
         spread_kernel,
-        in_specs=[space] * 4,
+        in_specs=[space] * 8,
         out_specs=[space] * 2,
         out_shape=[image, image],
         compiler_params=pltpu.CompilerParams(vmem_limit_bytes=16 * 2**20),

time: 119 us -> 119 us (level)
  starting transfers between devices: 33.6 us -> 30.9 us
  waiting for transfers between devices: 55.7 us -> 58.1 us
    ppermute x17 -> x20, waiting for transfers between devices: 51.3 us -> 56.2 us  [swap(): return lax.ppermute(array, cell, [(i, i ^ flip) for i in range(slots)])]
    ppermute x1, starting transfers between devices: 4.39 us -> 1.58 us  [on_device(): lax.ppermute(own, 'sector', even)]
    ppermute x1, waiting for transfers between devices: 2.34 us -> 1.02 us  [on_device(): lax.ppermute(stats, 'sector', [(i, i ^ flip) for i in range(sectors)])]
    ppermute x1, starting transfers between devices: 2.36 us -> 3.58 us  [on_device(): lax.ppermute(stats, 'sector', [(i, i ^ flip) for i in range(sectors)])]
    ppermute x17 -> x20, starting transfers between devices: 21.3 us -> 20.2 us  [swap(): return lax.ppermute(array, cell, [(i, i ^ flip) for i in range(slots)])]
  transfers between devices with their start and end apart: 23 -> 26, of which waited for: 13 -> 14; matrix products, arithmetic and copies ran while one was open for 3% -> 3% of each run, Pallas kernels for 12% -> 17%
where the time goes in v7:
time: 119 us; the launch traced here: 118 us
  waiting for transfers between devices  58.1 us (49%)
  starting transfers between devices  30.9 us (26%)
  Pallas kernels  23.1 us (19%)
  local copies, waits for them, and re-layouts  3.05 us (3%)
  other arithmetic  2.12 us (2%)
    ppermute x20, waiting for transfers between devices, swap(): return lax.ppermute(array, cell, [(i, i ^ flip) for i in range(slots)])  56.2 us
    ppermute x20, starting transfers between devices, swap(): return lax.ppermute(array, cell, [(i, i ^ flip) for i in range(slots)])  20.2 us
    pallas_call x4, Pallas kernels, whole_call(): pl.pallas_call(body, in_specs=[pl.BlockSpec(memory_space=pltpu.SMEM)] + [...  14.6 us
    pallas_call x2, Pallas kernels, pack(): pl.pallas_call(functools.partial(pack_kernel, parts), in_specs=[pl.BlockS...  7.61 us
    ppermute x1, starting transfers between devices, on_device(): lax.ppermute(stats, 'sector', [(i, i ^ flip) for i in range(sectors)])  3.58 us
    ppermute x1, starting transfers between devices, on_device(): in_early = lax.ppermute(image_one, planes, turns[0])  3.48 us
  transfers between devices with their start and end apart: 26, of which 14 were waited for; matrix products, arithmetic and copies ran while one was open for 3% of the time, Pallas kernels for 17%

profile of v7, /device:TPU:0, one launch (start us, length us, event | category | flops | bytes accessed | tf_op | source)
XLA Modules:
  0.0 118.2 jit_solution(11934334784966461517)
XLA Ops:
  0.7 0.9 copy-done
  1.6 3.0 %collective-permute-start.1 = (bf16[3,64,256]{2,1,0:T(8,128)(2,1)S(1)}, bf16[3,64,256]{2,1,0:T(8,128)(2,1)S(1)}, u32[]{:S(2)}, u32[]{:S(2)}) collective-permute-start(bf16[3,64,256]{2,1,0:T(8,128)(2,1)S(1)} %dynamic-slice_bitcast_fusion.1), channel_id=1, source_target_pairs={{0,2},{1,3},{2,0},{3,1},{4,6},{5,7},{6,4},{7,5},{8,10},{9,11},{10,... | collective-permute-start | bytes 294920 | tf_op jit(solution)/shard_map/ppermute | solution.py:383
  4.6 2.4 %pack_0_2.1 = (bf16[6,512,128]{2,1,0:T(8,128)(2,1)}, bf16[6,512,128]{2,1,0:T(8,128)(2,1)}) custom-call(bf16[13,1,4,128,256]{4,3,2,1,0:T(8,128)(2,1)} %left_env.3, bf16[13,1,4,256,128]{4,3,2,1,0:T(8,128)(2,1)} %right_env.3), custom_call_target="tpu_custom_call" | custom-call | bytes 3145728 | tf_op jit(solution)/shard_map/pack_0_2/pallas_call | solution.py:145
  7.1 0.9 collective-permute-start.11
  8.8 5.2 %pack_6_6.1 = (bf16[5,512,128]{2,1,0:T(8,128)(2,1)}, bf16[5,512,128]{2,1,0:T(8,128)(2,1)}, bf16[2,512,128]{2,1,0:T(8,128)(2,1)}, bf16[2,512,128]{2,1,0:T(8,128)(...) custom-call(bf16[13,1,4,128,256]{4,3,2,1,0:T(8,128)(2,1)} %left_env.3, ...), custom_call_target="tpu_custom_call" | custom-call | bytes 10485760 | tf_op jit(solution)/shard_map/pack_6_6/pallas_call | solution.py:145
  13.9 1.3 %collective-permute-start.2 = (bf16[13,512,128]{2,1,0:T(8,128)(2,1)}, bf16[13,512,128]{2,1,0:T(8,128)(2,1)}, u32[]{:S(2)}, u32[]{:S(2)}) collective-permute-start(bf16[13,512,128]{2,1,0:T(8,128)(2,1)} %get-tuple-element.26), channel_id=1, source_target_pairs={{0,1},{1,0},{2,3},{3,2},{4,5},{5,4},{6,7},{7,6},{8,9},{9,8},{10,11... | collective-permute-start | bytes 5111816 | tf_op jit(solution)/shard_map/ppermute | solution.py:383
  15.4 3.3 %collective-permute-done.5 = bf16[3,64,256]{2,1,0:T(8,128)(2,1)S(1)} collective-permute-done((bf16[3,64,256]{2,1,0:T(8,128)(2,1)}, bf16[3,64,256]{2,1,0:T(8,128)(2,1)S(1)}, u32[]{:S(2)}, u32[]{:S(2)}) %collective-permute-start.5) | collective-permute-done | bytes 98336 | tf_op jit(solution)/shard_map/ppermute | solution.py:383
  18.7 0.9 broadcast_select_fusion.1
  20.5 1.6 %collective-permute-start.6 = (bf16[256,256]{1,0:T(8,128)(2,1)}, bf16[256,256]{1,0:T(8,128)(2,1)S(1)}, u32[]{:S(2)}, u32[]{:S(2)}) collective-permute-start(bf16[256,256]{1,0:T(8,128)(2,1)} %get-tuple-element.49), channel_id=1, source_target_pairs={{0,4},{4,0},{8,12},{12,8},{1,5},{5,1},{9,13},{13,9},{2,6},{6,2},{1... | collective-permute-start | bytes 393224 | tf_op jit(solution)/shard_map/ppermute | solution.py:425
  22.1 1.1 collective-permute-done
  25.4 0.9 collective-permute-done.6
  28.5 13.8 %collective-permute-done.11.refs_3_ = bf16[6,512,128]{2,1,0:T(8,128)(2,1)} collective-permute-done((bf16[6,512,128]{2,1,0:T(8,128)(2,1)}, bf16[6,512,128]{2,1,0:T(8,128)(2,1)}, u32[]{:S(2)}, u32[]{:S(2)}) %collective-permute-start.11) | collective-permute-done | bytes 786464 | tf_op jit(solution)/shard_map/ppermute | solution.py:383
  42.3 1.9 %collective-permute-start.4 = (bf16[2,512,128]{2,1,0:T(8,128)(2,1)}, bf16[2,512,128]{2,1,0:T(8,128)(2,1)S(1)}, u32[]{:S(2)}, u32[]{:S(2)}) collective-permute-start(bf16[2,512,128]{2,1,0:T(8,128)(2,1)} %get-tuple-element.28), channel_id=1, source_target_pairs={{0,3},{1,2},{2,1},{3,0},{4,7},{5,6},{6,5},{7,4},{8,11},{9,10},{10,... | collective-permute-start | bytes 786440 | tf_op jit(solution)/shard_map/ppermute | solution.py:383
  44.2 3.7 %first_terms_0.1.refs_5_ = f32[256,256]{1,0:T(8,128)S(1)} custom-call(s32[30]{0:T(128)S(1)} %concatenate.9.info, bf16[13,512,128]{2,1,0:T(8,128)(2,1)S(1)} %copy-done.1, bf16[13,512,128]{2,1,0:T(8,128)(2,1)} %collective-permute-done.2.refs_1_, bf16[6,512,128]{2,1,0:T(8,128)(2,1)} %collective-permute-done.10.refs_2_, ...), custom_call_target="tpu_custom_call" | custom-call | flops 805306368 | bytes 3145728 | tf_op jit(solution)/shard_map/first_terms_0/pallas_call | solution.py:354
  47.9 10.8 %collective-permute-done.8.refs_2_.refs_4_ = bf16[5,512,128]{2,1,0:T(8,128)(2,1)S(1)} collective-permute-done((bf16[5,512,128]{2,1,0:T(8,128)(2,1)}, bf16[5,512,128]{2,1,0:T(8,128)(2,1)S(1)}, u32[]{:S(2)}, u32[]{:S(2)}) %collective-permute-start.8) | collective-permute-done | bytes 655392 | tf_op jit(solution)/shard_map/ppermute | solution.py:383
  58.7 11.7 %collective-permute-done.9.refs_3_.refs_5_ = bf16[5,512,128]{2,1,0:T(8,128)(2,1)S(1)} collective-permute-done((bf16[5,512,128]{2,1,0:T(8,128)(2,1)}, bf16[5,512,128]{2,1,0:T(8,128)(2,1)S(1)}, u32[]{:S(2)}, u32[]{:S(2)}) %collective-permute-start.9) | collective-permute-done | bytes 655392 | tf_op jit(solution)/shard_map/ppermute | solution.py:383
  70.3 3.4 %first_terms_6.1.refs_5_ = f32[256,256]{1,0:T(8,128)S(1)} custom-call(s32[30]{0:T(128)S(1)} %concatenate.9.info, bf16[13,512,128]{2,1,0:T(8,128)(2,1)S(1)} %copy-done.1, bf16[13,512,128]{2,1,0:T(8,128)(2,1)} %collective-permute-done.2.refs_1_, bf16[5,512,128]{2,1,0:T(8,128)(2,1)S(1)} %collective-permute-done.8.refs_2_.refs_4_, ...), custom_call_target="tpu_custom_call" | custom-call | flops 671088640 | bytes 2621440 | tf_op jit(solution)/shard_map/first_terms_6/pallas_call | solution.py:354
  73.7 4.6 %collective-permute-done.3.refs_2_.refs_6_ = bf16[2,512,128]{2,1,0:T(8,128)(2,1)S(1)} collective-permute-done((bf16[2,512,128]{2,1,0:T(8,128)(2,1)}, bf16[2,512,128]{2,1,0:T(8,128)(2,1)S(1)}, u32[]{:S(2)}, u32[]{:S(2)}) %collective-permute-start.3) | collective-permute-done | bytes 262176 | tf_op jit(solution)/shard_map/ppermute | solution.py:383
  78.4 2.7 %collective-permute-done.4.refs_3_.refs_7_ = bf16[2,512,128]{2,1,0:T(8,128)(2,1)S(1)} collective-permute-done((bf16[2,512,128]{2,1,0:T(8,128)(2,1)}, bf16[2,512,128]{2,1,0:T(8,128)(2,1)S(1)}, u32[]{:S(2)}, u32[]{:S(2)}) %collective-permute-start.4) | collective-permute-done | bytes 262176 | tf_op jit(solution)/shard_map/ppermute | solution.py:383
  81.0 2.3 %first_terms_11.1 = (f32[272,256]{1,0:T(8,128)S(1)}, bf16[128,256]{1,0:T(8,128)(2,1)S(1)}, bf16[128,256]{1,0:T(8,128)(2,1)S(1)}) custom-call(s32[30]{0:T(128)S(1)} %concatenate.9.info, bf16[13,512,128]{2,1,0:T(8,128)(2,1)S(1)} %copy-done.1, bf16[13,512,128]{2,1,0:T(8,128)(2,1)} %collective-permute-done.2.refs_1_, ...), custom_call_target="tpu_custom_call" | custom-call | flops 268435456 | bytes 1048576 | tf_op jit(solution)/shard_map/first_terms_11/pallas_call | solution.py:354
  83.3 3.5 %collective-permute-start.15 = (f32[272,256]{1,0:T(8,128)S(1)}, f32[272,256]{1,0:T(8,128)S(1)}, u32[]{:S(2)}, u32[]{:S(2)}) collective-permute-start(f32[272,256]{1,0:T(8,128)S(1)} %get-tuple-element.33.refs_11_), channel_id=1, source_target_pairs={{0,4},{4,0},{8,12},{12,8},{5,9},{9,5},{2,6},{6,2},{10,14},{14,10},... | collective-permute-start | bytes 835592 | tf_op jit(solution)/shard_map/ppermute | solution.py:470
  88.2 4.8 %collective-permute-start.18 = (f32[272,256]{1,0:T(8,128)S(1)}, f32[272,256]{1,0:T(8,128)S(1)}, u32[]{:S(2)}, u32[]{:S(2)}) collective-permute-start(f32[272,256]{1,0:T(8,128)S(1)} %get-tuple-element.33.refs_11_), channel_id=1, source_target_pairs={{0,1},{1,0},{2,3},{3,2},{4,5},{5,4},{6,7},{7,6},{8,9},{9,8},{10,11... | collective-permute-start | bytes 835592 | tf_op jit(solution)/shard_map/ppermute | solution.py:383
  93.1 1.2 collective-permute-done.18.refs_14_
  94.3 3.1 %collective-permute-start.19 = (f32[4,8,128]{2,1,0:T(8,128)S(1)}, f32[4,8,128]{2,1,0:T(8,128)S(1)}, u32[]{:S(2)}, u32[]{:S(2)}) collective-permute-start(f32[4,8,128]{2,1,0:T(8,128)S(1)} %pad_maximum_fusion.1), channel_id=1, source_target_pairs={{0,1},{1,0},{2,3},{3,2},{4,5},{5,4},{6,7},{7,6},{8,9},{9,8},{10,11... | collective-permute-start | bytes 49160 | tf_op jit(solution)/shard_map/ppermute | solution.py:383
  97.4 1.4 %collective-permute-start.21 = (f32[4,8,128]{2,1,0:T(8,128)S(1)}, f32[4,8,128]{2,1,0:T(8,128)S(1)}, u32[]{:S(2)}, u32[]{:S(2)}) collective-permute-start(f32[4,8,128]{2,1,0:T(8,128)S(1)} %pad_maximum_fusion.1), channel_id=1, source_target_pairs={{0,3},{1,2},{2,1},{3,0},{4,7},{5,6},{6,5},{7,4},{8,11},{9,10},{10,... | collective-permute-start | bytes 49160 | tf_op jit(solution)/shard_map/ppermute | solution.py:383
  98.8 2.3 %collective-permute-done.20 = f32[4,8,128]{2,1,0:T(8,128)S(1)} collective-permute-done((f32[4,8,128]{2,1,0:T(8,128)S(1)}, f32[4,8,128]{2,1,0:T(8,128)S(1)}, u32[]{:S(2)}, u32[]{:S(2)}) %collective-permute-start.20) | collective-permute-done | bytes 16416 | tf_op jit(solution)/shard_map/ppermute | solution.py:383
  101.2 3.6 %collective-permute-start.22 = (f32[4,8,128]{2,1,0:T(8,128)S(1)}, f32[4,8,128]{2,1,0:T(8,128)S(1)}, u32[]{:S(2)}, u32[]{:S(2)}) collective-permute-start(f32[4,8,128]{2,1,0:T(8,128)S(1)} %pad_maximum_fusion.2.refs_8_), channel_id=1, source_target_pairs={{0,8},{4,12},{8,0},{12,4},{1,9},{5,13},{9,1},{13,5},{2,10},{6,14},... | collective-permute-start | bytes 49160 | tf_op jit(solution)/shard_map/ppermute | solution.py:478
  105.5 1.0 collective-permute-done.22.refs_9_
  106.5 5.2 %second_terms.1 = (bf16[128,256]{1,0:T(8,128)(2,1)S(1)}, bf16[128,256]{1,0:T(8,128)(2,1)S(1)}, f32[1,1]{1,0:T(1,128)}) custom-call(s32[30]{0:T(128)S(1)} %concatenate.9.info, bf16[13,512,128]{2,1,0:T(8,128)(2,1)S(1)} %copy-done.1, bf16[13,512,128]{2,1,0:T(8,128)(2,1)} %collective-permute-done.2.refs_1_, ...), custom_call_target="tpu_custom_call" | custom-call | flops 1744830464 | bytes 6815744 | tf_op jit(solution)/shard_map/second_terms/pallas_call | solution.py:354
  111.7 1.1 collective-permute-start.24
  113.3 2.7 %collective-permute-done.24.refs_6_ = bf16[128,256]{1,0:T(8,128)(2,1)S(1)} collective-permute-done((bf16[128,256]{1,0:T(8,128)(2,1)S(1)}, bf16[128,256]{1,0:T(8,128)(2,1)S(1)}, u32[]{:S(2)}, u32[]{:S(2)}) %collective-permute-start.24) | collective-permute-done | bytes 65568 | tf_op jit(solution)/shard_map/ppermute | solution.py:383
  116.1 1.2 %collective-permute-done.25.refs_7_ = bf16[128,256]{1,0:T(8,128)(2,1)S(1)} collective-permute-done((bf16[128,256]{1,0:T(8,128)(2,1)S(1)}, bf16[128,256]{1,0:T(8,128)(2,1)S(1)}, u32[]{:S(2)}, u32[]{:S(2)}) %collective-permute-start.25) | collective-permute-done | bytes 65568 | tf_op jit(solution)/shard_map/ppermute | solution.py:383
  (61 shorter events, 9.6 us)
Async XLA Ops:
  0.6 1.0 copy-start
  1.6 6.4 %copy-start.4 = (s32[1,4]{1,0:T(1,128)S(1)}, s32[1,4]{1,0:T(1,128)}, u32[]{:S(2)}) copy-start(s32[1,4]{1,0:T(1,128)} %param.6) | copy-start | bytes 52
  1.6 6.5 %collective-permute-start.1 = (bf16[3,64,256]{2,1,0:T(8,128)(2,1)S(1)}, bf16[3,64,256]{2,1,0:T(8,128)(2,1)S(1)}, u32[]{:S(2)}, u32[]{:S(2)}) collective-permute-start(bf16[3,64,256]{2,1,0:T(8,128)(2,1)S(1)} %dynamic-slice_bitcast_fusion.1), channel_id=1, source_target_pairs={{0,2},{1,3},{2,0},{3,1},{4,6},{5,7},{6,4},{7,5},{8,10},{9,11},{10,... | collective-permute-start | bytes 294920 | tf_op jit(solution)/shard_map/ppermute | solution.py:383
  7.1 20.8 %collective-permute-start.10 = (bf16[6,512,128]{2,1,0:T(8,128)(2,1)}, bf16[6,512,128]{2,1,0:T(8,128)(2,1)}, u32[]{:S(2)}, u32[]{:S(2)}) collective-permute-start(bf16[6,512,128]{2,1,0:T(8,128)(2,1)} %get-tuple-element.23.refs_0_), channel_id=1, source_target_pairs={{0,2},{1,3},{2,0},{3,1},{4,6},{5,7},{6,4},{7,5},{8,10},{9,11},{10,... | collective-permute-start | bytes 2359304 | tf_op jit(solution)/shard_map/ppermute | solution.py:383
  7.1 35.1 %collective-permute-start.11 = (bf16[6,512,128]{2,1,0:T(8,128)(2,1)}, bf16[6,512,128]{2,1,0:T(8,128)(2,1)}, u32[]{:S(2)}, u32[]{:S(2)}) collective-permute-start(bf16[6,512,128]{2,1,0:T(8,128)(2,1)} %get-tuple-element.24.refs_1_), channel_id=1, source_target_pairs={{0,3},{1,2},{2,1},{3,0},{4,7},{5,6},{6,5},{7,4},{8,11},{9,10},{10,... | collective-permute-start | bytes 2359304 | tf_op jit(solution)/shard_map/ppermute | solution.py:383
  8.1 0.6 copy-start.2
  13.9 8.2 %copy-start.3 = (s32[13]{0:T(128)S(1)}, s32[13]{0:T(128)}, u32[]{:S(2)}) copy-start(s32[13]{0:T(128)} %param.9) | copy-start | bytes 160
  13.9 30.3 %collective-permute-start.2 = (bf16[13,512,128]{2,1,0:T(8,128)(2,1)}, bf16[13,512,128]{2,1,0:T(8,128)(2,1)}, u32[]{:S(2)}, u32[]{:S(2)}) collective-permute-start(bf16[13,512,128]{2,1,0:T(8,128)(2,1)} %get-tuple-element.26), channel_id=1, source_target_pairs={{0,1},{1,0},{2,3},{3,2},{4,5},{5,4},{6,7},{7,6},{8,9},{9,8},{10,11... | collective-permute-start | bytes 5111816 | tf_op jit(solution)/shard_map/ppermute | solution.py:383
  15.3 3.4 %collective-permute-start.5 = (bf16[3,64,256]{2,1,0:T(8,128)(2,1)}, bf16[3,64,256]{2,1,0:T(8,128)(2,1)S(1)}, u32[]{:S(2)}, u32[]{:S(2)}) collective-permute-start(bf16[3,64,256]{2,1,0:T(8,128)(2,1)} %copy-done.2), channel_id=1, source_target_pairs={{0,1},{1,0},{2,3},{3,2},{4,5},{5,4},{6,7},{7,6},{8,9},{9,8},{10,11... | collective-permute-start | bytes 294920 | tf_op jit(solution)/shard_map/ppermute | solution.py:383
  19.8 24.4 %copy-start.1 = (bf16[13,512,128]{2,1,0:T(8,128)(2,1)S(1)}, bf16[13,512,128]{2,1,0:T(8,128)(2,1)}, u32[]{:S(2)}) copy-start(bf16[13,512,128]{2,1,0:T(8,128)(2,1)} %get-tuple-element.25.refs_0_) | copy-start | bytes 5111812
  20.5 5.7 %collective-permute-start.6 = (bf16[256,256]{1,0:T(8,128)(2,1)}, bf16[256,256]{1,0:T(8,128)(2,1)S(1)}, u32[]{:S(2)}, u32[]{:S(2)}) collective-permute-start(bf16[256,256]{1,0:T(8,128)(2,1)} %get-tuple-element.49), channel_id=1, source_target_pairs={{0,4},{4,0},{8,12},{12,8},{1,5},{5,1},{9,13},{13,9},{2,6},{6,2},{1... | collective-permute-start | bytes 393224 | tf_op jit(solution)/shard_map/ppermute | solution.py:425
  22.1 1.1 collective-permute-start
  23.2 3.5 %collective-permute-start.7 = (bf16[256,256]{1,0:T(8,128)(2,1)}, bf16[256,256]{1,0:T(8,128)(2,1)S(1)}, u32[]{:S(2)}, u32[]{:S(2)}) collective-permute-start(bf16[256,256]{1,0:T(8,128)(2,1)} %get-tuple-element.49), channel_id=1, source_target_pairs={{4,8},{8,4},{5,9},{9,5},{6,10},{10,6},{7,11},{11,7},{20,24},{24,20... | collective-permute-start | bytes 393224 | tf_op jit(solution)/shard_map/ppermute | solution.py:425
  26.3 32.4 %collective-permute-start.8 = (bf16[5,512,128]{2,1,0:T(8,128)(2,1)}, bf16[5,512,128]{2,1,0:T(8,128)(2,1)S(1)}, u32[]{:S(2)}, u32[]{:S(2)}) collective-permute-start(bf16[5,512,128]{2,1,0:T(8,128)(2,1)} %get-tuple-element.29), channel_id=1, source_target_pairs={{0,2},{1,3},{2,0},{3,1},{4,6},{5,7},{6,4},{7,5},{8,10},{9,11},{10,... | collective-permute-start | bytes 1966088 | tf_op jit(solution)/shard_map/ppermute | solution.py:383
  26.7 43.6 %collective-permute-start.9 = (bf16[5,512,128]{2,1,0:T(8,128)(2,1)}, bf16[5,512,128]{2,1,0:T(8,128)(2,1)S(1)}, u32[]{:S(2)}, u32[]{:S(2)}) collective-permute-start(bf16[5,512,128]{2,1,0:T(8,128)(2,1)} %get-tuple-element.30), channel_id=1, source_target_pairs={{0,3},{1,2},{2,1},{3,0},{4,7},{5,6},{6,5},{7,4},{8,11},{9,10},{10,... | collective-permute-start | bytes 1966088 | tf_op jit(solution)/shard_map/ppermute | solution.py:383
  27.9 50.5 %collective-permute-start.3 = (bf16[2,512,128]{2,1,0:T(8,128)(2,1)}, bf16[2,512,128]{2,1,0:T(8,128)(2,1)S(1)}, u32[]{:S(2)}, u32[]{:S(2)}) collective-permute-start(bf16[2,512,128]{2,1,0:T(8,128)(2,1)} %get-tuple-element.27), channel_id=1, source_target_pairs={{0,2},{1,3},{2,0},{3,1},{4,6},{5,7},{6,4},{7,5},{8,10},{9,11},{10,... | collective-permute-start | bytes 786440 | tf_op jit(solution)/shard_map/ppermute | solution.py:383
  42.3 38.8 %collective-permute-start.4 = (bf16[2,512,128]{2,1,0:T(8,128)(2,1)}, bf16[2,512,128]{2,1,0:T(8,128)(2,1)S(1)}, u32[]{:S(2)}, u32[]{:S(2)}) collective-permute-start(bf16[2,512,128]{2,1,0:T(8,128)(2,1)} %get-tuple-element.28), channel_id=1, source_target_pairs={{0,3},{1,2},{2,1},{3,0},{4,7},{5,6},{6,5},{7,4},{8,11},{9,10},{10,... | collective-permute-start | bytes 786440 | tf_op jit(solution)/shard_map/ppermute | solution.py:383
  83.3 9.7 %collective-permute-start.15 = (f32[272,256]{1,0:T(8,128)S(1)}, f32[272,256]{1,0:T(8,128)S(1)}, u32[]{:S(2)}, u32[]{:S(2)}) collective-permute-start(f32[272,256]{1,0:T(8,128)S(1)} %get-tuple-element.33.refs_11_), channel_id=1, source_target_pairs={{0,4},{4,0},{8,12},{12,8},{5,9},{9,5},{2,6},{6,2},{10,14},{14,10},... | collective-permute-start | bytes 835592 | tf_op jit(solution)/shard_map/ppermute | solution.py:470
  86.8 6.2 %collective-permute-start.16 = (f32[272,256]{1,0:T(8,128)S(1)}, f32[272,256]{1,0:T(8,128)S(1)}, u32[]{:S(2)}, u32[]{:S(2)}) collective-permute-start(f32[272,256]{1,0:T(8,128)S(1)} %get-tuple-element.33.refs_11_), channel_id=1, source_target_pairs={{1,2},{2,1},{5,6},{6,5},{9,10},{10,9},{13,14},{14,13},{17,18},{18,... | collective-permute-start | bytes 835592 | tf_op jit(solution)/shard_map/ppermute | solution.py:463
  87.5 5.5 %collective-permute-start.17 = (f32[272,256]{1,0:T(8,128)S(1)}, f32[272,256]{1,0:T(8,128)S(1)}, u32[]{:S(2)}, u32[]{:S(2)}) collective-permute-start(f32[272,256]{1,0:T(8,128)S(1)} %get-tuple-element.33.refs_11_), channel_id=1, source_target_pairs={{1,5},{5,1},{9,13},{13,9},{4,8},{8,4},{3,7},{7,3},{11,15},{15,11},... | collective-permute-start | bytes 835592 | tf_op jit(solution)/shard_map/ppermute | solution.py:469
  88.2 6.0 %collective-permute-start.18 = (f32[272,256]{1,0:T(8,128)S(1)}, f32[272,256]{1,0:T(8,128)S(1)}, u32[]{:S(2)}, u32[]{:S(2)}) collective-permute-start(f32[272,256]{1,0:T(8,128)S(1)} %get-tuple-element.33.refs_11_), channel_id=1, source_target_pairs={{0,1},{1,0},{2,3},{3,2},{4,5},{5,4},{6,7},{7,6},{8,9},{9,8},{10,11... | collective-permute-start | bytes 835592 | tf_op jit(solution)/shard_map/ppermute | solution.py:383
  94.3 4.6 %collective-permute-start.19 = (f32[4,8,128]{2,1,0:T(8,128)S(1)}, f32[4,8,128]{2,1,0:T(8,128)S(1)}, u32[]{:S(2)}, u32[]{:S(2)}) collective-permute-start(f32[4,8,128]{2,1,0:T(8,128)S(1)} %pad_maximum_fusion.1), channel_id=1, source_target_pairs={{0,1},{1,0},{2,3},{3,2},{4,5},{5,4},{6,7},{7,6},{8,9},{9,8},{10,11... | collective-permute-start | bytes 49160 | tf_op jit(solution)/shard_map/ppermute | solution.py:383
  97.4 3.7 %collective-permute-start.20 = (f32[4,8,128]{2,1,0:T(8,128)S(1)}, f32[4,8,128]{2,1,0:T(8,128)S(1)}, u32[]{:S(2)}, u32[]{:S(2)}) collective-permute-start(f32[4,8,128]{2,1,0:T(8,128)S(1)} %pad_maximum_fusion.1), channel_id=1, source_target_pairs={{0,2},{1,3},{2,0},{3,1},{4,6},{5,7},{6,4},{7,5},{8,10},{9,11},{10,... | collective-permute-start | bytes 49160 | tf_op jit(solution)/shard_map/ppermute | solution.py:383
  97.4 3.7 %collective-permute-start.21 = (f32[4,8,128]{2,1,0:T(8,128)S(1)}, f32[4,8,128]{2,1,0:T(8,128)S(1)}, u32[]{:S(2)}, u32[]{:S(2)}) collective-permute-start(f32[4,8,128]{2,1,0:T(8,128)S(1)} %pad_maximum_fusion.1), channel_id=1, source_target_pairs={{0,3},{1,2},{2,1},{3,0},{4,7},{5,6},{6,5},{7,4},{8,11},{9,10},{10,... | collective-permute-start | bytes 49160 | tf_op jit(solution)/shard_map/ppermute | solution.py:383
  101.2 5.3 %collective-permute-start.22 = (f32[4,8,128]{2,1,0:T(8,128)S(1)}, f32[4,8,128]{2,1,0:T(8,128)S(1)}, u32[]{:S(2)}, u32[]{:S(2)}) collective-permute-start(f32[4,8,128]{2,1,0:T(8,128)S(1)} %pad_maximum_fusion.2.refs_8_), channel_id=1, source_target_pairs={{0,8},{4,12},{8,0},{12,4},{1,9},{5,13},{9,1},{13,5},{2,10},{6,14},... | collective-permute-start | bytes 49160 | tf_op jit(solution)/shard_map/ppermute | solution.py:478
  104.8 8.0 %collective-permute-start.13 = (bf16[128,256]{1,0:T(8,128)(2,1)S(1)}, bf16[128,256]{1,0:T(8,128)(2,1)S(1)}, u32[]{:S(2)}, u32[]{:S(2)}) collective-permute-start(bf16[128,256]{1,0:T(8,128)(2,1)S(1)} %get-tuple-element.32), channel_id=1, source_target_pairs={{0,2},{1,3},{2,0},{3,1},{4,6},{5,7},{6,4},{7,5},{8,10},{9,11},{10,... | collective-permute-start | bytes 196616 | tf_op jit(solution)/shard_map/ppermute | solution.py:383
  111.7 4.3 %collective-permute-start.24 = (bf16[128,256]{1,0:T(8,128)(2,1)S(1)}, bf16[128,256]{1,0:T(8,128)(2,1)S(1)}, u32[]{:S(2)}, u32[]{:S(2)}) collective-permute-start(bf16[128,256]{1,0:T(8,128)(2,1)S(1)} %get-tuple-element.39), channel_id=1, source_target_pairs={{0,2},{1,3},{2,0},{3,1},{4,6},{5,7},{6,4},{7,5},{8,10},{9,11},{10,... | collective-permute-start | bytes 196616 | tf_op jit(solution)/shard_map/ppermute | solution.py:383
  112.8 3.3 %collective-permute-start.12 = (bf16[128,256]{1,0:T(8,128)(2,1)S(1)}, bf16[128,256]{1,0:T(8,128)(2,1)S(1)}, u32[]{:S(2)}, u32[]{:S(2)}) collective-permute-start(bf16[128,256]{1,0:T(8,128)(2,1)S(1)} %get-tuple-element.31.refs_0_), channel_id=1, source_target_pairs={{0,1},{1,0},{2,3},{3,2},{4,5},{5,4},{6,7},{7,6},{8,9},{9,8},{10,11... | collective-permute-start | bytes 196616 | tf_op jit(solution)/shard_map/ppermute | solution.py:383
  112.8 3.3 %collective-permute-start.14 = (bf16[128,256]{1,0:T(8,128)(2,1)S(1)}, bf16[128,256]{1,0:T(8,128)(2,1)S(1)}, u32[]{:S(2)}, u32[]{:S(2)}) collective-permute-start(bf16[128,256]{1,0:T(8,128)(2,1)S(1)} %collective-permute-done.13.refs_2_), channel_id=1, source_target_pairs={{0,1},{1,0},{2,3},{3,2},{4,5},{5,4},{6,7},{7,6},{8,9},{9,8},{10,11... | collective-permute-start | bytes 196616 | tf_op jit(solution)/shard_map/ppermute | solution.py:383
  113.3 2.8 %collective-permute-start.23 = (bf16[128,256]{1,0:T(8,128)(2,1)S(1)}, bf16[128,256]{1,0:T(8,128)(2,1)S(1)}, u32[]{:S(2)}, u32[]{:S(2)}) collective-permute-start(bf16[128,256]{1,0:T(8,128)(2,1)S(1)} %get-tuple-element.38.refs_4_), channel_id=1, source_target_pairs={{0,1},{1,0},{2,3},{3,2},{4,5},{5,4},{6,7},{7,6},{8,9},{9,8},{10,11... | collective-permute-start | bytes 196616 | tf_op jit(solution)/shard_map/ppermute | solution.py:383
  116.1 1.3 %collective-permute-start.25 = (bf16[128,256]{1,0:T(8,128)(2,1)S(1)}, bf16[128,256]{1,0:T(8,128)(2,1)S(1)}, u32[]{:S(2)}, u32[]{:S(2)}) collective-permute-start(bf16[128,256]{1,0:T(8,128)(2,1)S(1)} %collective-permute-done.24.refs_6_), channel_id=1, source_target_pairs={{0,1},{1,0},{2,3},{3,2},{4,5},{5,4},{6,7},{7,6},{8,9},{9,8},{10,11... | collective-permute-start | bytes 196616 | tf_op jit(solution)/shard_map/ppermute | solution.py:383
